TPU v7x, 32 devices: a whole 2x2x4 slice. The times are simulated.
32 devices in a mesh: replica: 4 (over y, core), fsdp: 4 (over z), tensor: 2 (over x).
Axes of the slice: x: 2, y: 2, z: 4, core: 2. Of those that a mesh axis runs over, the one named last changes fastest.
Arguments:
- cotangent: bfloat16 [4096, 4096], P(('replica', 'fsdp'), 'tensor'), may hold values from -6 to 6
- gate_pre: bfloat16 [4096, 14336], P(('replica', 'fsdp'), 'tensor'), may hold values from -6 to 6
- up_pre: bfloat16 [4096, 14336], P(('replica', 'fsdp'), 'tensor'), may hold values from -6 to 6
- down_weight: bfloat16 [14336, 4096], P('tensor', 'fsdp'), may hold values from -0.09375 to 0.09375
- projector: bfloat16 [4096, 512], P('tensor', 'fsdp'), may hold values from -0.09375 to 0.09375
Outputs:
- grad_gate: bfloat16 [4096, 14336], P(('replica', 'fsdp'), 'tensor')
- grad_up: bfloat16 [4096, 14336], P(('replica', 'fsdp'), 'tensor')
- projected_grad: float32 [512, 14336], P('fsdp', 'tensor')
All inputs are finite; a program needn't handle non-finite values.
Results may differ from a plain program's by a relative error of at most 0.0049.
Values may be sent and summed in bfloat16 or wider, within the bound.
No kernel may reach another device: no remote copies, remote signals or barrier semaphores. Data moves between devices by JAX's collectives and lax.ppermute only.
A program may use at most 192 MiB of HBM per device.

v0:
```python
import math

import jax
import jax.numpy as jnp
from jax import lax
from jax.sharding import PartitionSpec as P


def local(cotangent, gate_pre, up_pre, down_weight, projector):
    whole = lax.all_gather(cotangent, "tensor", axis=1, tiled=True)
    local_rows = cotangent.shape[0]
    hidden_cols = gate_pre.shape[1]
    hidden_grad = lax.dot_general(
        whole,
        lax.all_gather(down_weight, "fsdp", axis=1, tiled=True),
        (((1,), (1,)), ((), ())),
        preferred_element_type=jnp.float32,
    )
    projector_full_cols = lax.all_gather(projector, "fsdp", axis=1, tiled=True)
    partial_rank = jnp.dot(cotangent, projector_full_cols, preferred_element_type=jnp.float32)
    low_rank = lax.psum(partial_rank, "tensor").astype(jnp.bfloat16)
    gate_float = gate_pre.astype(jnp.float32)
    up_float = up_pre.astype(jnp.float32)
    sigma = jax.nn.sigmoid(gate_float)
    activated = gate_float * sigma
    hidden = (activated * up_float).astype(jnp.bfloat16)
    grad_up = (hidden_grad * activated).astype(jnp.bfloat16)
    grad_gate = (hidden_grad * up_float * sigma * (1.0 + gate_float * (1.0 - sigma))).astype(
        jnp.bfloat16
    )
    replicas = lax.axis_size("replica")
    shards = lax.axis_size("fsdp")
    token_total = local_rows * replicas * shards
    scale_factor = 1.0 / math.sqrt(token_total)
    partial_grad = (
        lax.dot_general(
            low_rank, hidden, (((0,), (0,)), ((), ())), preferred_element_type=jnp.float32
        )
        * scale_factor
    )
    rank_size = partial_grad.shape[0]
    piece_rows = rank_size // (shards * replicas)
    reordered = partial_grad.reshape(shards, replicas, piece_rows, hidden_cols)
    reordered = jnp.swapaxes(reordered, 0, 1).reshape(rank_size, hidden_cols)
    joint_piece = lax.psum_scatter(reordered, ("replica", "fsdp"), scatter_dimension=0, tiled=True)
    projected_grad = lax.all_gather(joint_piece, "replica", axis=0, tiled=True)
    return (grad_gate, grad_up, projected_grad)


def solution(mesh):
    placed = (
        P(("replica", "fsdp"), "tensor"),
        P(("replica", "fsdp"), "tensor"),
        P(("replica", "fsdp"), "tensor"),
        P("tensor", "fsdp"),
        P("tensor", "fsdp"),
    )
    return jax.shard_map(
        local,
        mesh=mesh,
        in_specs=placed,
        out_specs=(
            P(("replica", "fsdp"), "tensor"),
            P(("replica", "fsdp"), "tensor"),
            P("fsdp", "tensor"),
        ),
        check_vma=False,
    )
```

profile of v0, /device:TPU:9, one launch (start us, length us, event | category | flops | bytes accessed | tf_op | source)
XLA Modules:
  0.0 1327.4 jit_solution(16631011317810034660)
XLA Ops:
  7.2 0.0 all-gather.9.cloned.1.call-start
  7.2 0.7 all-gather.9.cloned.1.call-update
  7.9 0.0 reduce-scatter.2.cloned.1.call-start
  7.9 47.6 %all-gather.9.cloned.1.call-done = bf16[2048,512]{1,0:T(8,128)(2,1)} async-done(((bf16[2048,128]{1,0:T(8,128)(2,1)}), bf16[2048,512]{1,0:T(8,128)(2,1)}) %all-gather.9.cloned.1.call-update) | async-done | bytes 2097168 | tf_op jit(solution)/shard_map/all_gather | solution.py:19
  55.5 2.6 fusion.11
  58.2 14.5 %all-reduce.1 = bf16[256,512]{1,0:T(8,128)(2,1)S(1)} all-reduce(f32[256,512]{1,0:T(8,128)S(1)} %fusion.11), channel_id=1, replica_groups=mesh['replica'=4,'fsdp'=4,'tensor'=2] {'tensor'}, use_global_device_ids=true, to_apply=%region_0.0 | all-reduce | flops 131072 | bytes 786432 | tf_op jit(solution)/shard_map/psum | solution.py:21
  72.7 11.6 convolution_multiply_fusion
  84.3 12.1 copy.8
  96.4 0.0 reduce-scatter.2.cloned.1.call-update
  96.4 0.0 all-gather.11.cloned.1.call-start
  96.5 150.4 %reduce-scatter.2.cloned.1.call-done = f32[32,7168]{1,0:T(8,128)} async-done(((f32[512,7168]{1,0:T(8,128)}), f32[32,7168]{1,0:T(8,128)}) %reduce-scatter.2.cloned.1.call-update) | async-done | bytes 917520 | tf_op jit(solution)/shard_map/reduce_scatter | solution.py:45
  246.9 0.0 all-gather.11.cloned.1.call-update
  246.9 0.0 all-gather.5.cloned.1.call-start
  247.0 0.5 all-gather.5.cloned.1.call-update
  247.5 0.0 all-gather.7.cloned.1.call-start
  247.5 0.5 all-gather.7.cloned.1.call-update
  248.1 32.6 %all-gather.11.cloned.1.call-done = f32[128,7168]{1,0:T(8,128)} async-done(((f32[32,7168]{1,0:T(8,128)}), f32[128,7168]{1,0:T(8,128)}) %all-gather.11.cloned.1.call-update) | async-done | bytes 3670032 | tf_op jit(solution)/shard_map/all_gather | solution.py:46
  280.7 34.1 %all-gather.5.cloned.1.call-done = bf16[256,4096]{1,0:T(8,128)(2,1)} async-done(((bf16[256,2048]{1,0:T(8,128)(2,1)}), bf16[256,4096]{1,0:T(8,128)(2,1)}) %all-gather.5.cloned.1.call-update) | async-done | bytes 2097168 | tf_op jit(solution)/shard_map/all_gather | solution.py:10
  314.8 973.0 %all-gather.7.cloned.1.call-done = bf16[7168,4096]{1,0:T(8,128)(2,1)} async-done(((bf16[7168,1024]{1,0:T(8,128)(2,1)}), bf16[7168,4096]{1,0:T(8,128)(2,1)}) %all-gather.7.cloned.1.call-update) | async-done | bytes 58720272 | tf_op jit(solution)/shard_map/all_gather | solution.py:15
  1287.8 28.8 %multiply_convert_fusion = (bf16[256,7168]{1,0:T(8,128)(2,1)}, bf16[256,7168]{1,0:T(8,128)(2,1)}) fusion(bf16[256,7168]{1,0:T(8,128)(2,1)} %param.6, bf16[256,7168]{1,0:T(8,128)(2,1)} %param.7, bf16[256,4096]{1,0:T(8,128)(2,1)} %all-gather.5.cloned.1.call-done, bf16[7168,4096]{1,0:T(8,128)(2,1)} %all-gather.7.cloned.1.call-done), kind=kOutput, calls=%fused_computation.14 | convolution fusion | flops 15059910656 | bytes 75497472 | tf_op jit(solution)/shard_map/dot_general | solution.py:13
  1316.6 4.2 copy.12
Async XLA Ops:
  7.2 48.4 %all-gather.9.cloned.1.call-start = ((), (), s32[]{:S(2)}) async-start(), calls=%async_computation.3 | async-start | bytes 2621440 | tf_op jit(solution)/shard_map/all_gather | solution.py:19
  7.9 239.0 %reduce-scatter.2.cloned.1.call-start = ((), (), s32[]{:S(2)}) async-start(), calls=%async_computation.4 | async-start | bytes 15597568 | tf_op jit(solution)/shard_map/reduce_scatter | solution.py:45
  96.4 184.2 %all-gather.11.cloned.1.call-start = ((), (), s32[]{:S(2)}) async-start(), calls=%async_computation.5 | async-start | bytes 4587520 | tf_op jit(solution)/shard_map/all_gather | solution.py:46
  246.9 67.9 %all-gather.5.cloned.1.call-start = ((), (), s32[]{:S(2)}) async-start(), calls=%async_computation.1 | async-start | bytes 3145728 | tf_op jit(solution)/shard_map/all_gather | solution.py:10
  247.5 1040.4 %all-gather.7.cloned.1.call-start = ((), (), s32[]{:S(2)}) async-start(), calls=%async_computation.2 | async-start | bytes 73400320 | tf_op jit(solution)/shard_map/all_gather | solution.py:15
Sparse Core Ops, SparseCore 0:
  9.6 45.9 all-gather.8
  96.6 150.2 reduce-scatter.1
  248.5 32.1 all-gather.10
  282.1 32.6 all-gather.4
  316.2 971.5 all-gather.6
where the time goes:
time: 1330 us
  waiting for transfers between devices  1240 us (93%)
  matrix products  43 us (3%)
  local copies, waits for them, and re-layouts  16.3 us (1%)
  blocking collectives  14.5 us (1%)
  between operations  13.8 us (1%)
    all_gather x1, waiting for transfers between devices, local(): lax.all_gather(down_weight, 'fsdp', axis=1, tiled=True)  973 us
    reduce_scatter x1, waiting for transfers between devices, local(): lax.psum_scatter(reordered, ('replica', 'fsdp'), scatter_dimension=0, til...  150 us
    all_gather x1, waiting for transfers between devices, local(): projector_full_cols = lax.all_gather(projector, 'fsdp', axis=1, tiled=True)  47.6 us
    all_gather x1, waiting for transfers between devices, local(): whole = lax.all_gather(cotangent, 'tensor', axis=1, tiled=True)  34.1 us
    all_gather x1, waiting for transfers between devices, local(): projected_grad = lax.all_gather(joint_piece, 'replica', axis=0, tiled=True)  32.6 us
    dot_general x1, matrix products, local(): lax.dot_general(whole, lax.all_gather(down_weight, 'fsdp', axis=1, tiled=...  28.8 us
  transfers between devices with their start and end apart: 5, of which 5 were waited for; matrix products, arithmetic and copies ran while one was open for 0% of the time, Pallas kernels for 0%

commit v1 on v0

--- a/solution.py
+++ b/solution.py
@@ -1,12 +1,18 @@
+import functools
 import math
 
 import jax
 import jax.numpy as jnp
 from jax import lax
+from jax.experimental import pallas as pl
+from jax.experimental.pallas import tpu as pltpu
 from jax.sharding import PartitionSpec as P
 
-
-def local(cotangent, gate_pre, up_pre, down_weight, projector):
+AXES = ("replica", "fsdp", "tensor")
+VMEM_BYTES = 40 * 1024 * 1024
+
+
+def general(cotangent, gate_pre, up_pre, down_weight, projector):
     whole = lax.all_gather(cotangent, "tensor", axis=1, tiled=True)
     local_rows = cotangent.shape[0]
     hidden_cols = gate_pre.shape[1]
@@ -47,7 +53,254 @@
     return (grad_gate, grad_up, projected_grad)
 
 
+def chunk_plan(quarter, unit, count):
+    units = quarter // unit
+    each = -(-units // count)
+    plan, at = [], 0
+    while at < units:
+        width = min(each, units - at)
+        plan.append((at * unit, width * unit))
+        at += width
+    return plan
+
+
+def mix_kernel(order, near, far, w0, w1, w2, w3, out):
+    width = w0.shape[1]
+    for side, tokens in enumerate((near, far)):
+        total = None
+        for b, w in enumerate((w0, w1, w2, w3)):
+            at = pl.multiple_of(order[b] * width, width)
+            term = lax.dot_general(
+                tokens[:, pl.ds(at, width)],
+                w[...],
+                (((1,), (1,)), ((), ())),
+                preferred_element_type=jnp.float32,
+            )
+            total = term if total is None else total + term
+        out[side, 0] = total.astype(out.dtype)
+
+
+def mix(order, near, far, blocks, leaf, rows):
+    units = blocks[0].shape[0]
+    lines = near.shape[0] // (2 * rows)
+    features = near.shape[1]
+    token_spec = pl.BlockSpec((rows, features), lambda i, order: (2 * i + leaf, 0))
+    weight_spec = pl.BlockSpec(blocks[0].shape, lambda i, order: (0, 0))
+    return pl.pallas_call(
+        mix_kernel,
+        out_shape=jax.ShapeDtypeStruct((2, lines, rows, units), jnp.bfloat16),
+        grid_spec=pltpu.PrefetchScalarGridSpec(
+            num_scalar_prefetch=1,
+            grid=(lines,),
+            in_specs=[token_spec, token_spec] + [weight_spec] * len(blocks),
+            out_specs=pl.BlockSpec((2, 1, rows, units), lambda i, order: (0, i, 0, 0)),
+        ),
+        compiler_params=pltpu.CompilerParams(vmem_limit_bytes=VMEM_BYTES),
+        cost_estimate=pl.CostEstimate(
+            flops=2 * near.shape[0] * features * units,
+            bytes_accessed=2 * (near.size + units * features + near.shape[0] * units),
+            transcendentals=0,
+        ),
+        name="hidden_grad_chunk",
+    )(order, near, far, *blocks)
+
+
+def grads_kernel(position, p0, p1, p2, p3, gate, up, *refs):
+    grad_gate, grad_up = refs[-2:]
+    for d, piece in enumerate((p0, p1, p2, p3)):
+
+        @pl.when(pl.program_id(0) == d)
+        def _():
+            gate_float = gate[...].astype(jnp.float32)
+            up_float = up[...].astype(jnp.float32)
+            hidden_grad = piece[...].astype(jnp.float32)
+            sigma = jax.nn.sigmoid(gate_float)
+            grad_up[...] = (hidden_grad * (gate_float * sigma)).astype(grad_up.dtype)
+            grad_gate[...] = (
+                hidden_grad * up_float * sigma * (1.0 + gate_float * (1.0 - sigma))
+            ).astype(grad_gate.dtype)
+
+
+def grads(position, pieces, gate, up, kept, offset, quarter, unit):
+    rows, width = pieces[0].shape
+    subs = width // unit
+
+    def piece_map(d):
+        return lambda i, j, position: (0, jnp.where(i == d, j, jnp.where(i < d, 0, subs - 1)))
+
+    def column_map(i, j, position):
+        return (0, (position[0] ^ i) * (quarter // unit) + offset // unit + j)
+
+    columns = pl.BlockSpec((rows, unit), column_map)
+    anywhere = pl.BlockSpec(memory_space=pl.ANY)
+    return pl.pallas_call(
+        grads_kernel,
+        out_shape=[jax.ShapeDtypeStruct(gate.shape, jnp.bfloat16)] * 2,
+        grid_spec=pltpu.PrefetchScalarGridSpec(
+            num_scalar_prefetch=1,
+            grid=(4, subs),
+            in_specs=[pl.BlockSpec((rows, unit), piece_map(d)) for d in range(4)]
+            + [columns, columns]
+            + [anywhere] * len(kept),
+            out_specs=[columns, columns],
+        ),
+        input_output_aliases={7: 0, 8: 1} if kept else {},
+        compiler_params=pltpu.CompilerParams(vmem_limit_bytes=VMEM_BYTES),
+        cost_estimate=pl.CostEstimate(
+            flops=4 * 12 * rows * width,
+            bytes_accessed=4 * 10 * rows * width,
+            transcendentals=4 * rows * width,
+        ),
+        name="grads_chunk",
+    )(position, *pieces, gate, up, *kept)
+
+
+def ranks_kernel(position, low, gate, up, out):
+    gate_float = gate[...].astype(jnp.float32)
+    activated = gate_float * jax.nn.sigmoid(gate_float)
+    hidden = (activated * up[...].astype(jnp.float32)).astype(jnp.bfloat16)
+    out[0] = lax.dot_general(
+        low[...], hidden, (((0,), (0,)), ((), ())), preferred_element_type=jnp.float32
+    ).astype(out.dtype)
+
+
+def ranks(position, low, gate, up, swaps, quarter, kind):
+    rows, rank = low.shape
+    parts = 2 if quarter % 256 == 0 else 1
+    width = quarter // parts
+    first, step = swaps[0], swaps[0] ^ swaps[1]
+
+    def column_map(i, j, position):
+        return (0, (position[0] ^ first ^ (i * step)) * parts + j)
+
+    columns = pl.BlockSpec((rows, width), column_map)
+    return pl.pallas_call(
+        ranks_kernel,
+        out_shape=jax.ShapeDtypeStruct((2, rank, quarter), kind),
+        grid_spec=pltpu.PrefetchScalarGridSpec(
+            num_scalar_prefetch=1,
+            grid=(2, parts),
+            in_specs=[pl.BlockSpec(low.shape, lambda i, j, position: (0, 0)), columns, columns],
+            out_specs=pl.BlockSpec((1, rank, width), lambda i, j, position: (i, 0, j)),
+        ),
+        compiler_params=pltpu.CompilerParams(vmem_limit_bytes=VMEM_BYTES),
+        cost_estimate=pl.CostEstimate(
+            flops=2 * rows * rank * 2 * quarter,
+            bytes_accessed=2 * quarter * (4 * rows + 4 * rank),
+            transcendentals=2 * rows * quarter,
+        ),
+        name="rank_terms",
+    )(position, low, gate, up)
+
+
+def line(cotangent, gate_pre, up_pre, down_weight, projector):
+    replicas, shards, tensors = (lax.axis_size(a) for a in AXES)
+    r, f, t = (lax.axis_index(a) for a in AXES)
+    rows = cotangent.shape[0]
+    quarter = down_weight.shape[0] // replicas
+    last = shards - 1
+    inner = (f != 0) & (f != last)
+    bf16, f32 = jnp.bfloat16, jnp.float32
+
+    def send(x, rule):
+        pairs = []
+        for a in range(replicas):
+            for b in range(shards):
+                for c in range(tensors):
+                    to = rule(a, b, c)
+                    if to is not None:
+                        here = (a * shards + b) * tensors + c
+                        pairs.append((here, (to[0] * shards + to[1]) * tensors + to[2]))
+        return lax.ppermute(x, AXES, pairs)
+
+    def is_inner(b):
+        return 0 < b < last
+
+    to_inner = lambda a, b, c: None if is_inner(b) else (a, b ^ 1, c)
+    to_outer = lambda a, b, c: (a, b ^ 1, c) if is_inner(b) else None
+    across = lambda a, b, c: (a, last - b, c) if is_inner(b) else None
+    inner_y = lambda a, b, c: (a ^ 2, b, c) if is_inner(b) else None
+    inner_core = lambda a, b, c: (a ^ 1, b, c) if is_inner(b) else None
+    inner_x = lambda a, b, c: (a, b, c ^ 1) if is_inner(b) else None
+    swap = lambda d: lambda a, b, c: (a ^ d, b, c)
+    swap_x = lambda a, b, c: (a, b, c ^ 1)
+
+    position = jnp.reshape(r, (1,)).astype(jnp.int32)
+
+    unit = 256 if quarter % 256 == 0 else 128
+    plan = chunk_plan(quarter, unit, 4)
+    blocks = []
+    for offset, width in plan:
+        own = lax.dynamic_slice_in_dim(down_weight, r * quarter + offset, width, 0)
+        edge = send(own, to_inner)
+        blocks.append((own, edge, send(own, across), send(edge, across)))
+
+    outer_rows = send(cotangent, to_inner)
+    mine = (cotangent, outer_rows, send(cotangent, inner_y), send(outer_rows, inner_y))
+    near = jnp.concatenate(
+        [jnp.concatenate([m, send(m, inner_x)], axis=1) for m in mine], axis=0
+    )
+    far = send(near, inner_core)
+
+    projector_rows = projector.shape[0] // replicas
+    part = lax.dynamic_slice_in_dim(projector, r * projector_rows, projector_rows, 0)
+    part = lax.all_gather(part, "fsdp", axis=1, tiled=True)
+    projector_full = lax.all_gather(part, "replica", axis=0, tiled=True)
+    partial_rank = jnp.dot(cotangent, projector_full, preferred_element_type=f32)
+    low = (partial_rank + send(partial_rank, swap_x)).astype(bf16)
+
+    rank_size = low.shape[1]
+    away = ranks(position, low, gate_pre, up_pre, (1, 3), quarter, bf16)
+    keep = ranks(position, low, gate_pre, up_pre, (0, 2), quarter, f32)
+    keep = keep + send(away, swap(1)).astype(f32)
+    mine = keep[0] + send(keep[1].astype(bf16), swap(2)).astype(f32)
+    piece = rank_size // shards
+    half = rank_size // 2
+    outgoing = jnp.where(f == 0, mine[piece:], mine[:-piece]).astype(bf16)
+    got = send(outgoing, to_inner).astype(f32)
+    pad = jnp.zeros((piece, quarter), f32)
+    joined = mine + jnp.where(
+        f < shards // 2, jnp.concatenate([pad, got]), jnp.concatenate([got, pad])
+    )
+    low_half, high_half = joined[:half], joined[half:]
+    lower = f < shards // 2
+    crossed = send(jnp.where(lower, high_half, low_half).astype(bf16), across).astype(f32)
+    pair = jnp.where(lower, low_half, high_half) + crossed
+    for_inner = jnp.where(lower, pair[piece:], pair[:piece])
+    for_outer = jnp.where(lower, pair[:piece], pair[piece:]).astype(bf16)
+    returned = send(for_outer, to_outer).astype(f32)
+    own_piece = jnp.where(lower, mine[:piece], mine[-piece:])
+    scale_factor = 1.0 / math.sqrt(rows * replicas * shards)
+    final = (jnp.where(inner, for_inner, own_piece + returned) * scale_factor).astype(bf16)
+    two = jnp.stack([final, send(final, swap(2))])
+    other = send(two, swap(1))
+    projected_grad = jnp.zeros((piece, gate_pre.shape[1]), f32)
+    for d, q in ((0, two[0]), (2, two[1]), (1, other[0]), (3, other[1])):
+        projected_grad = lax.dynamic_update_slice(
+            projected_grad, q.astype(f32), (0, (r ^ d) * quarter)
+        )
+
+    halves = shards // tensors
+    order = jnp.stack(
+        [((b // halves) ^ t) * halves + b % halves for b in (f, f ^ 1, last - f, (last - f) ^ 1)]
+    ).astype(jnp.int32)
+    kept = ()
+    for (offset, width), chunk in zip(plan, blocks):
+        outer_part = mix(order, near, far, chunk, 1, rows)
+        inner_part = mix(order, near, far, chunk, 0, rows)
+        home = jnp.where(inner, inner_part, send(outer_part, to_outer))
+        pieces = [
+            home[0, 0],
+            send(home[1, 0], swap(1)),
+            send(home[0, 1], swap(2)),
+            send(home[1, 1], swap(3)),
+        ]
+        kept = grads(position, pieces, gate_pre, up_pre, kept, offset, quarter, unit)
+    return (kept[0], kept[1], projected_grad)
+
+
 def solution(mesh):
+    sizes = tuple(mesh.shape[a] for a in AXES)
     placed = (
         P(("replica", "fsdp"), "tensor"),
         P(("replica", "fsdp"), "tensor"),
@@ -56,7 +309,7 @@
         P("tensor", "fsdp"),
     )
     return jax.shard_map(
-        local,
+        line if sizes == (4, 4, 2) else general,
         mesh=mesh,
         in_specs=placed,
         out_specs=(

time: 1330 us -> 595 us (0.45)
  waiting for transfers between devices: 1240 us -> 310 us
  starting transfers between devices: 0.19 us -> 90.1 us
  Pallas kernels: 0 us -> 83.2 us
  other arithmetic: 0 us -> 58 us
  matrix products: 43 us -> 2.75 us
    all_gather x4 -> x1, waiting for transfers between devices: 1090 us -> 24.6 us  [line(): projector_full = lax.all_gather(part, 'replica', axis=0, tiled=True)]
    ppermute x0 -> x44, waiting for transfers between devices: none -> 285 us  [send(): return lax.ppermute(x, AXES, pairs)]
    reduce_scatter x1 -> x0, waiting for transfers between devices: 150 us -> none  [local(): lax.psum_scatter(reordered, ('replica', 'fsdp'), scatter_dimension=0, til...]
    ppermute x0 -> x44, starting transfers between devices: none -> 90 us  [send(): return lax.ppermute(x, AXES, pairs)]
    pallas_call x0 -> x14, Pallas kernels: none -> 83.2 us  [the longest x8 60.8 us: mix(): pl.pallas_call(mix_kernel, out_shape=jax.ShapeDtypeStruct((2, lines, rows...]
    dot_general x3 -> x1, matrix products: 43.1 us -> 2.75 us  [line(): jnp.dot(cotangent, projector_full, preferred_element_type=f32)]
    concatenate x0 -> x1, other arithmetic: none -> 33.7 us  [line(): jnp.concatenate([jnp.concatenate([m, send(m, inner_x)], axis=1) for m in...]
    add x0 -> x4, other arithmetic: none -> 14.6 us  [the longest x1 6.87 us: line(): keep = keep + send(away, swap(1)).astype(f32)]
  transfers between devices with their start and end apart: 5 -> 45, of which waited for: 5 -> 21; matrix products, arithmetic and copies ran while one was open for 0% -> 11% of each run, Pallas kernels for 0% -> 14%
where the time goes in v1:
time: 595 us; the launch traced here: 590 us
  waiting for transfers between devices  310 us (52%)
  starting transfers between devices  90.1 us (15%)
  Pallas kernels  83.2 us (14%)
  other arithmetic  58 us (10%)
  local copies, waits for them, and re-layouts  17.9 us (3%)
  between operations  15 us (3%)
  blocking collectives  13.2 us (2%)
    ppermute x44, waiting for transfers between devices, send(): return lax.ppermute(x, AXES, pairs)  285 us
    ppermute x44, starting transfers between devices, send(): return lax.ppermute(x, AXES, pairs)  90 us
    pallas_call x8, Pallas kernels, mix(): pl.pallas_call(mix_kernel, out_shape=jax.ShapeDtypeStruct((2, lines, rows...  60.8 us
    concatenate x1, other arithmetic, line(): jnp.concatenate([jnp.concatenate([m, send(m, inner_x)], axis=1) for m in...  33.7 us
    all_gather x1, waiting for transfers between devices, line(): projector_full = lax.all_gather(part, 'replica', axis=0, tiled=True)  24.6 us
    pallas_call x4, Pallas kernels, grads(): pl.pallas_call(grads_kernel, out_shape=[jax.ShapeDtypeStruct(gate.shape,...  15 us
    all_gather x1, blocking collectives, line(): part = lax.all_gather(part, 'fsdp', axis=1, tiled=True)  13.2 us
  transfers between devices with their start and end apart: 45, of which 21 were waited for; matrix products, arithmetic and copies ran while one was open for 11% of the time, Pallas kernels for 14%

profile of v1, /device:TPU:9, one launch (start us, length us, event | category | flops | bytes accessed | tf_op | source)
XLA Modules:
  0.0 590.2 jit_solution(17857920337703549594)
XLA Ops:
  8.2 13.2 %all_gather.6 = bf16[512,512]{1,0:T(8,128)(2,1)} all-gather(bf16[512,128]{1,0:T(8,128)(2,1)S(1)} %constant_dynamic-slice_fusion), channel_id=1, replica_groups=mesh['replica'=4,'fsdp'=4,'tensor'=2] {'fsdp'}, dimensions={1}, use_global_device_ids=true | all-gather | bytes 655360 | tf_op jit(solution)/shard_map/all_gather | solution.py:247
  22.8 24.6 %all-gather.2.cloned.1.call-done = bf16[2048,512]{1,0:T(8,128)(2,1)} async-done(((bf16[512,512]{1,0:T(8,128)(2,1)}), bf16[2048,512]{1,0:T(8,128)(2,1)}) %all-gather.2.cloned.1.call-update) | async-done | bytes 2097168 | tf_op jit(solution)/shard_map/all_gather | solution.py:248
  56.7 6.8 %collective-permute-done.36 = f32[256,512]{1,0:T(8,128)S(1)} collective-permute-done((f32[256,512]{1,0:T(8,128)S(1)}, f32[256,512]{1,0:T(8,128)S(1)}, u32[]{:S(2)}, u32[]{:S(2)}) %collective-permute-start.36) | collective-permute-done | bytes 524320 | tf_op jit(solution)/shard_map/ppermute | solution.py:214
  79.6 20.3 %collective-permute-done.5 = bf16[256,2048]{1,0:T(8,128)(2,1)S(1)} collective-permute-done((bf16[256,2048]{1,0:T(8,128)(2,1)S(1)}, bf16[256,2048]{1,0:T(8,128)(2,1)S(1)}, u32[]{:S(2)}, u32[]{:S(2)}) %collective-permute-start.5) | collective-permute-done | bytes 1048608 | tf_op jit(solution)/shard_map/ppermute | solution.py:214
  102.1 39.2 %collective-permute-done.4 = bf16[256,2048]{1,0:T(8,128)(2,1)S(1)} collective-permute-done((bf16[256,2048]{1,0:T(8,128)(2,1)S(1)}, bf16[256,2048]{1,0:T(8,128)(2,1)S(1)}, u32[]{:S(2)}, u32[]{:S(2)}) %collective-permute-start.4) | collective-permute-done | bytes 1048608 | tf_op jit(solution)/shard_map/ppermute | solution.py:214
  141.3 22.5 %collective-permute-done.6 = bf16[256,2048]{1,0:T(8,128)(2,1)S(1)} collective-permute-done((bf16[256,2048]{1,0:T(8,128)(2,1)S(1)}, bf16[256,2048]{1,0:T(8,128)(2,1)S(1)}, u32[]{:S(2)}, u32[]{:S(2)}) %collective-permute-start.6) | collective-permute-done | bytes 1048608 | tf_op jit(solution)/shard_map/ppermute | solution.py:214
  163.8 33.7 %maximum_maximum_fusion.near = bf16[1024,4096]{1,0:T(8,128)(2,1)} fusion(bf16[256,2048]{1,0:T(8,128)(2,1)S(1)} %collective-permute-done.6, bf16[256,2048]{1,0:T(8,128)(2,1)S(1)} %collective-permute-done.5, bf16[256,2048]{1,0:T(8,128)(2,1)S(1)} %collective-permute-done.4, bf16[256,2048]{1,0:T(8,128)(2,1)S(1)} %collective-permute-done.3, ...), kind=kLoop, calls=%fused_computation | loop fusion | flops 67108864 | bytes 16777216 | tf_op jit(solution)/shard_map/concatenate | solution.py:240
  200.5 4.6 rank_terms.2
  205.0 6.9 %convert_add_fusion = f32[2,512,1792]{2,1,0:T(8,128)} fusion(f32[2,512,1792]{2,1,0:T(8,128)} %rank_terms.2, bf16[2,512,1792]{2,1,0:T(8,128)(2,1)S(1)} %collective-permute-done.37), kind=kLoop, calls=%fused_computation.1 | loop fusion | flops 3670016 | bytes 18350080 | tf_op jit(solution)/shard_map/add | solution.py:255
  214.4 41.5 %collective-permute-done.38 = bf16[512,1792]{1,0:T(8,128)(2,1)} collective-permute-done((bf16[512,1792]{1,0:T(8,128)(2,1)S(1)}, bf16[512,1792]{1,0:T(8,128)(2,1)}, u32[]{:S(2)}, u32[]{:S(2)}) %collective-permute-start.38) | collective-permute-done | bytes 1835040 | tf_op jit(solution)/shard_map/ppermute | solution.py:214
  273.1 33.3 %collective-permute-done.8.w1 = bf16[256,1024]{1,0:T(8,128)(2,1)} collective-permute-done((bf16[256,1024]{1,0:T(8,128)(2,1)}, bf16[256,1024]{1,0:T(8,128)(2,1)}, u32[]{:S(2)}, u32[]{:S(2)}) %collective-permute-start.8) | collective-permute-done | bytes 524320 | tf_op jit(solution)/shard_map/ppermute | solution.py:214
  323.8 5.0 collective-permute-done.15.w1
  330.3 9.3 %collective-permute-done.40 = bf16[256,1792]{1,0:T(8,128)(2,1)} collective-permute-done((bf16[256,1792]{1,0:T(8,128)(2,1)}, bf16[256,1792]{1,0:T(8,128)(2,1)}, u32[]{:S(2)}, u32[]{:S(2)}) %collective-permute-start.40) | collective-permute-done | bytes 917536 | tf_op jit(solution)/shard_map/ppermute | solution.py:214
  345.8 16.3 %collective-permute-done.16.w2 = bf16[512,1024]{1,0:T(8,128)(2,1)} collective-permute-done((bf16[512,1024]{1,0:T(8,128)(2,1)S(1)}, bf16[512,1024]{1,0:T(8,128)(2,1)}, u32[]{:S(2)}, u32[]{:S(2)}) %collective-permute-start.16) | collective-permute-done | bytes 1048608 | tf_op jit(solution)/shard_map/ppermute | solution.py:214
  367.6 6.0 %collective-permute-done.29.w1 = bf16[512,1024]{1,0:T(8,128)(2,1)} collective-permute-done((bf16[512,1024]{1,0:T(8,128)(2,1)S(1)}, bf16[512,1024]{1,0:T(8,128)(2,1)}, u32[]{:S(2)}, u32[]{:S(2)}) %collective-permute-start.29) | collective-permute-done | bytes 1048608 | tf_op jit(solution)/shard_map/ppermute | solution.py:214
  379.8 6.5 %hidden_grad_chunk.9 = bf16[2,2,256,256]{3,2,1,0:T(8,128)(2,1)} custom-call(s32[4]{0:T(128)S(1)} %pad_add_fusion.order, bf16[1024,4096]{1,0:T(8,128)(2,1)} %maximum_maximum_fusion.near, bf16[1024,4096]{1,0:T(8,128)(2,1)} %collective-permute-done.7.far, bf16[256,1024]{1,0:T(8,128)(2,1)} %constant_dynamic-slice_fusion.4.w0, ...), custom_call_target="tpu_custom_call" | custom-call | flops 2147483648 | bytes 11010048 | tf_op jit(solution)/shard_map/hidden_grad_chunk/pallas_call | solution.py:89
  387.6 8.9 %hidden_grad_chunk.11 = bf16[2,2,256,512]{3,2,1,0:T(8,128)(2,1)} custom-call(s32[4]{0:T(128)S(1)} %pad_add_fusion.order, bf16[1024,4096]{1,0:T(8,128)(2,1)} %maximum_maximum_fusion.near, bf16[1024,4096]{1,0:T(8,128)(2,1)} %collective-permute-done.7.far, bf16[512,1024]{1,0:T(8,128)(2,1)S(1)} %get-tuple-element.22.w0, ...), custom_call_target="tpu_custom_call" | custom-call | flops 4294967296 | bytes 13631488 | tf_op jit(solution)/shard_map/hidden_grad_chunk/pallas_call | solution.py:89
  396.5 10.4 %collective-permute-done.23.w2 = bf16[512,1024]{1,0:T(8,128)(2,1)S(1)} collective-permute-done((bf16[512,1024]{1,0:T(8,128)(2,1)S(1)}, bf16[512,1024]{1,0:T(8,128)(2,1)S(1)}, u32[]{:S(2)}, u32[]{:S(2)}) %collective-permute-start.23) | collective-permute-done | bytes 1048608 | tf_op jit(solution)/shard_map/ppermute | solution.py:214
  409.0 42.9 %collective-permute-done.24.w3 = bf16[512,1024]{1,0:T(8,128)(2,1)S(1)} collective-permute-done((bf16[512,1024]{1,0:T(8,128)(2,1)}, bf16[512,1024]{1,0:T(8,128)(2,1)S(1)}, u32[]{:S(2)}, u32[]{:S(2)}) %collective-permute-start.24) | collective-permute-done | bytes 1048608 | tf_op jit(solution)/shard_map/ppermute | solution.py:214
  454.2 7.8 %hidden_grad_chunk.13 = bf16[2,2,256,512]{3,2,1,0:T(8,128)(2,1)S(1)} custom-call(s32[4]{0:T(128)S(1)} %pad_add_fusion.order, bf16[1024,4096]{1,0:T(8,128)(2,1)} %maximum_maximum_fusion.near, bf16[1024,4096]{1,0:T(8,128)(2,1)} %collective-permute-done.7.far, bf16[512,1024]{1,0:T(8,128)(2,1)S(1)} %get-tuple-element.23.w0, ...), custom_call_target="tpu_custom_call" | custom-call | flops 4294967296 | bytes 13631488 | tf_op jit(solution)/shard_map/hidden_grad_chunk/pallas_call | solution.py:89
  464.4 9.9 %collective-permute-done.31.w3 = bf16[512,1024]{1,0:T(8,128)(2,1)S(1)} collective-permute-done((bf16[512,1024]{1,0:T(8,128)(2,1)}, bf16[512,1024]{1,0:T(8,128)(2,1)S(1)}, u32[]{:S(2)}, u32[]{:S(2)}) %collective-permute-start.31) | collective-permute-done | bytes 1048608 | tf_op jit(solution)/shard_map/ppermute | solution.py:214
  474.3 7.9 %hidden_grad_chunk.15 = bf16[2,2,256,512]{3,2,1,0:T(8,128)(2,1)S(1)} custom-call(s32[4]{0:T(128)S(1)} %pad_add_fusion.order, bf16[1024,4096]{1,0:T(8,128)(2,1)} %maximum_maximum_fusion.near, bf16[1024,4096]{1,0:T(8,128)(2,1)} %collective-permute-done.7.far, bf16[512,1024]{1,0:T(8,128)(2,1)S(1)} %get-tuple-element.21.w0, ...), custom_call_target="tpu_custom_call" | custom-call | flops 4294967296 | bytes 13631488 | tf_op jit(solution)/shard_map/hidden_grad_chunk/pallas_call | solution.py:89
  482.2 11.3 %collective-permute-start.32 = (bf16[2,2,256,512]{3,2,1,0:T(8,128)(2,1)S(1)}, bf16[2,2,256,512]{3,2,1,0:T(8,128)(2,1)}, u32[]{:S(2)}, u32[]{:S(2)}) collective-permute-start(bf16[2,2,256,512]{3,2,1,0:T(8,128)(2,1)S(1)} %hidden_grad_chunk.15), channel_id=1, source_target_pairs={{2,0},{3,1},{4,6},{5,7},{10,8},{11,9},{12,14},{13,15},{18,16},{19,... | collective-permute-start | bytes 3145736 | tf_op jit(solution)/shard_map/ppermute | solution.py:214
  493.6 8.2 %hidden_grad_chunk.10 = bf16[2,2,256,512]{3,2,1,0:T(8,128)(2,1)S(1)} custom-call(s32[4]{0:T(128)S(1)} %pad_add_fusion.order, bf16[1024,4096]{1,0:T(8,128)(2,1)} %maximum_maximum_fusion.near, bf16[1024,4096]{1,0:T(8,128)(2,1)} %collective-permute-done.7.far, bf16[512,1024]{1,0:T(8,128)(2,1)S(1)} %get-tuple-element.22.w0, ...), custom_call_target="tpu_custom_call" | custom-call | flops 4294967296 | bytes 13631488 | tf_op jit(solution)/shard_map/hidden_grad_chunk/pallas_call | solution.py:89
  501.7 7.9 %hidden_grad_chunk.12 = bf16[2,2,256,512]{3,2,1,0:T(8,128)(2,1)S(1)} custom-call(s32[4]{0:T(128)S(1)} %pad_add_fusion.order, bf16[1024,4096]{1,0:T(8,128)(2,1)} %maximum_maximum_fusion.near, bf16[1024,4096]{1,0:T(8,128)(2,1)} %collective-permute-done.7.far, bf16[512,1024]{1,0:T(8,128)(2,1)S(1)} %get-tuple-element.23.w0, ...), custom_call_target="tpu_custom_call" | custom-call | flops 4294967296 | bytes 13631488 | tf_op jit(solution)/shard_map/hidden_grad_chunk/pallas_call | solution.py:89
  515.6 7.8 %hidden_grad_chunk.14 = bf16[2,2,256,512]{3,2,1,0:T(8,128)(2,1)S(1)} custom-call(s32[4]{0:T(128)S(1)} %pad_add_fusion.order, bf16[1024,4096]{1,0:T(8,128)(2,1)} %maximum_maximum_fusion.near, bf16[1024,4096]{1,0:T(8,128)(2,1)} %collective-permute-done.7.far, bf16[512,1024]{1,0:T(8,128)(2,1)S(1)} %get-tuple-element.21.w0, ...), custom_call_target="tpu_custom_call" | custom-call | flops 4294967296 | bytes 13631488 | tf_op jit(solution)/shard_map/hidden_grad_chunk/pallas_call | solution.py:89
  523.4 5.8 hidden_grad_chunk.8
  536.9 3.9 collective-permute-done.20.p2
  560.0 3.8 collective-permute-done.35.p3
  564.9 4.3 grads_chunk.4
  569.2 4.2 grads_chunk.5
  574.7 4.2 grads_chunk.6
  (136 shorter events, 136.3 us)
Async XLA Ops:
  7.2 40.2 %all-gather.2.cloned.1.call-start = ((), (), s32[]{:S(2)}) async-start(), calls=%async_computation | async-start | bytes 2621440 | tf_op jit(solution)/shard_map/all_gather | solution.py:248
  21.5 32.1 %collective-permute-start.1 = (bf16[256,2048]{1,0:T(8,128)(2,1)}, bf16[256,2048]{1,0:T(8,128)(2,1)S(1)}, u32[]{:S(2)}, u32[]{:S(2)}) collective-permute-start(bf16[256,2048]{1,0:T(8,128)(2,1)} %param.5), channel_id=1, source_target_pairs={{0,2},{1,3},{6,4},{7,5},{8,10},{9,11},{14,12},{15,13},{16,18},{17,... | collective-permute-start | bytes 3145736 | tf_op jit(solution)/shard_map/ppermute | solution.py:214
  51.4 26.0 %collective-permute-start.3 = (bf16[256,2048]{1,0:T(8,128)(2,1)S(1)}, bf16[256,2048]{1,0:T(8,128)(2,1)S(1)}, u32[]{:S(2)}, u32[]{:S(2)}) collective-permute-start(bf16[256,2048]{1,0:T(8,128)(2,1)S(1)} %copy-done.15), channel_id=1, source_target_pairs={{2,18},{3,19},{4,20},{5,21},{10,26},{11,27},{12,28},{13,29},{18,2}... | collective-permute-start | bytes 3145736 | tf_op jit(solution)/shard_map/ppermute | solution.py:214
  53.6 46.3 %collective-permute-start.5 = (bf16[256,2048]{1,0:T(8,128)(2,1)S(1)}, bf16[256,2048]{1,0:T(8,128)(2,1)S(1)}, u32[]{:S(2)}, u32[]{:S(2)}) collective-permute-start(bf16[256,2048]{1,0:T(8,128)(2,1)S(1)} %collective-permute-done.1), channel_id=1, source_target_pairs={{2,18},{3,19},{4,20},{5,21},{10,26},{11,27},{12,28},{13,29},{18,2}... | collective-permute-start | bytes 3145736 | tf_op jit(solution)/shard_map/ppermute | solution.py:214
  68.6 136.5 %collective-permute-start.37 = (bf16[2,512,1792]{2,1,0:T(8,128)(2,1)S(1)}, bf16[2,512,1792]{2,1,0:T(8,128)(2,1)S(1)}, u32[]{:S(2)}, u32[]{:S(2)}) collective-permute-start(bf16[2,512,1792]{2,1,0:T(8,128)(2,1)S(1)} %rank_terms.3), channel_id=1, source_target_pairs={{0,8},{1,9},{2,10},{3,11},{4,12},{5,13},{6,14},{7,15},{8,0},{9,1},... | collective-permute-start | bytes 11010056 | tf_op jit(solution)/shard_map/ppermute | solution.py:214
  69.7 32.4 %collective-permute-start = (bf16[256,2048]{1,0:T(8,128)(2,1)S(1)}, bf16[256,2048]{1,0:T(8,128)(2,1)S(1)}, u32[]{:S(2)}, u32[]{:S(2)}) collective-permute-start(bf16[256,2048]{1,0:T(8,128)(2,1)S(1)} %copy-done.15), channel_id=1, source_target_pairs={{2,3},{3,2},{4,5},{5,4},{10,11},{11,10},{12,13},{13,12},{18,19},{1... | collective-permute-start | bytes 3145736 | tf_op jit(solution)/shard_map/ppermute | solution.py:214
  72.8 68.5 %collective-permute-start.2 = (bf16[256,2048]{1,0:T(8,128)(2,1)S(1)}, bf16[256,2048]{1,0:T(8,128)(2,1)S(1)}, u32[]{:S(2)}, u32[]{:S(2)}) collective-permute-start(bf16[256,2048]{1,0:T(8,128)(2,1)S(1)} %collective-permute-done.1), channel_id=1, source_target_pairs={{2,3},{3,2},{4,5},{5,4},{10,11},{11,10},{12,13},{13,12},{18,19},{1... | collective-permute-start | bytes 3145736 | tf_op jit(solution)/shard_map/ppermute | solution.py:214
  77.5 63.8 %collective-permute-start.4 = (bf16[256,2048]{1,0:T(8,128)(2,1)S(1)}, bf16[256,2048]{1,0:T(8,128)(2,1)S(1)}, u32[]{:S(2)}, u32[]{:S(2)}) collective-permute-start(bf16[256,2048]{1,0:T(8,128)(2,1)S(1)} %collective-permute-done.3), channel_id=1, source_target_pairs={{2,3},{3,2},{4,5},{5,4},{10,11},{11,10},{12,13},{13,12},{18,19},{1... | collective-permute-start | bytes 3145736 | tf_op jit(solution)/shard_map/ppermute | solution.py:214
  99.9 63.8 %collective-permute-start.6 = (bf16[256,2048]{1,0:T(8,128)(2,1)S(1)}, bf16[256,2048]{1,0:T(8,128)(2,1)S(1)}, u32[]{:S(2)}, u32[]{:S(2)}) collective-permute-start(bf16[256,2048]{1,0:T(8,128)(2,1)S(1)} %collective-permute-done.5), channel_id=1, source_target_pairs={{2,3},{3,2},{4,5},{5,4},{10,11},{11,10},{12,13},{13,12},{18,19},{1... | collective-permute-start | bytes 3145736 | tf_op jit(solution)/shard_map/ppermute | solution.py:214
  197.5 179.4 %collective-permute-start.7 = (bf16[1024,4096]{1,0:T(8,128)(2,1)}, bf16[1024,4096]{1,0:T(8,128)(2,1)}, u32[]{:S(2)}, u32[]{:S(2)}) collective-permute-start(bf16[1024,4096]{1,0:T(8,128)(2,1)} %maximum_maximum_fusion.near), channel_id=1, source_target_pairs={{2,10},{3,11},{4,12},{5,13},{10,2},{11,3},{12,4},{13,5},{18,26},{1... | collective-permute-start | bytes 25165832 | tf_op jit(solution)/shard_map/ppermute | solution.py:214
  214.1 41.8 %collective-permute-start.38 = (bf16[512,1792]{1,0:T(8,128)(2,1)S(1)}, bf16[512,1792]{1,0:T(8,128)(2,1)}, u32[]{:S(2)}, u32[]{:S(2)}) collective-permute-start(bf16[512,1792]{1,0:T(8,128)(2,1)S(1)} %fusion.2), channel_id=1, source_target_pairs={{0,16},{1,17},{2,18},{3,19},{4,20},{5,21},{6,22},{7,23},{8,24},{9,... | collective-permute-start | bytes 5505032 | tf_op jit(solution)/shard_map/ppermute | solution.py:214
  262.0 47.5 %collective-permute-start.39 = (bf16[384,1792]{1,0:T(8,128)(2,1)}, bf16[384,1792]{1,0:T(8,128)(2,1)}, u32[]{:S(2)}, u32[]{:S(2)}) collective-permute-start(bf16[384,1792]{1,0:T(8,128)(2,1)} %fusion.1), channel_id=1, source_target_pairs={{0,2},{1,3},{6,4},{7,5},{8,10},{9,11},{14,12},{15,13},{16,18},{17,... | collective-permute-start | bytes 4128776 | tf_op jit(solution)/shard_map/ppermute | solution.py:214
  265.2 41.2 %collective-permute-start.8 = (bf16[256,1024]{1,0:T(8,128)(2,1)}, bf16[256,1024]{1,0:T(8,128)(2,1)}, u32[]{:S(2)}, u32[]{:S(2)}) collective-permute-start(bf16[256,1024]{1,0:T(8,128)(2,1)} %constant_dynamic-slice_fusion.4.w0), channel_id=1, source_target_pairs={{0,2},{1,3},{6,4},{7,5},{8,10},{9,11},{14,12},{15,13},{16,18},{17,... | collective-permute-start | bytes 1572872 | tf_op jit(solution)/shard_map/ppermute | solution.py:214
  266.5 52.1 %collective-permute-start.9 = (bf16[256,1024]{1,0:T(8,128)(2,1)}, bf16[256,1024]{1,0:T(8,128)(2,1)}, u32[]{:S(2)}, u32[]{:S(2)}) collective-permute-start(bf16[256,1024]{1,0:T(8,128)(2,1)} %constant_dynamic-slice_fusion.4.w0), channel_id=1, source_target_pairs={{2,4},{3,5},{4,2},{5,3},{10,12},{11,13},{12,10},{13,11},{18,20},{1... | collective-permute-start | bytes 1572872 | tf_op jit(solution)/shard_map/ppermute | solution.py:214
  271.8 57.0 %collective-permute-start.15 = (bf16[512,1024]{1,0:T(8,128)(2,1)S(1)}, bf16[512,1024]{1,0:T(8,128)(2,1)}, u32[]{:S(2)}, u32[]{:S(2)}) collective-permute-start(bf16[512,1024]{1,0:T(8,128)(2,1)S(1)} %get-tuple-element.22.w0), channel_id=1, source_target_pairs={{0,2},{1,3},{6,4},{7,5},{8,10},{9,11},{14,12},{15,13},{16,18},{17,... | collective-permute-start | bytes 3145736 | tf_op jit(solution)/shard_map/ppermute | solution.py:214
  316.4 23.2 %collective-permute-start.40 = (bf16[256,1792]{1,0:T(8,128)(2,1)}, bf16[256,1792]{1,0:T(8,128)(2,1)}, u32[]{:S(2)}, u32[]{:S(2)}) collective-permute-start(bf16[256,1792]{1,0:T(8,128)(2,1)} %select_convert_fusion), channel_id=1, source_target_pairs={{2,4},{3,5},{4,2},{5,3},{10,12},{11,13},{12,10},{13,11},{18,20},{1... | collective-permute-start | bytes 2752520 | tf_op jit(solution)/shard_map/ppermute | solution.py:214
  318.6 43.5 %collective-permute-start.16 = (bf16[512,1024]{1,0:T(8,128)(2,1)S(1)}, bf16[512,1024]{1,0:T(8,128)(2,1)}, u32[]{:S(2)}, u32[]{:S(2)}) collective-permute-start(bf16[512,1024]{1,0:T(8,128)(2,1)S(1)} %get-tuple-element.22.w0), channel_id=1, source_target_pairs={{2,4},{3,5},{4,2},{5,3},{10,12},{11,13},{12,10},{13,11},{18,20},{1... | collective-permute-start | bytes 3145736 | tf_op jit(solution)/shard_map/ppermute | solution.py:214
  322.5 43.1 %collective-permute-start.22 = (bf16[512,1024]{1,0:T(8,128)(2,1)S(1)}, bf16[512,1024]{1,0:T(8,128)(2,1)}, u32[]{:S(2)}, u32[]{:S(2)}) collective-permute-start(bf16[512,1024]{1,0:T(8,128)(2,1)S(1)} %get-tuple-element.23.w0), channel_id=1, source_target_pairs={{0,2},{1,3},{6,4},{7,5},{8,10},{9,11},{14,12},{15,13},{16,18},{17,... | collective-permute-start | bytes 3145736 | tf_op jit(solution)/shard_map/ppermute | solution.py:214
  328.8 44.8 %collective-permute-start.29 = (bf16[512,1024]{1,0:T(8,128)(2,1)S(1)}, bf16[512,1024]{1,0:T(8,128)(2,1)}, u32[]{:S(2)}, u32[]{:S(2)}) collective-permute-start(bf16[512,1024]{1,0:T(8,128)(2,1)S(1)} %get-tuple-element.21.w0), channel_id=1, source_target_pairs={{0,2},{1,3},{6,4},{7,5},{8,10},{9,11},{14,12},{15,13},{16,18},{17,... | collective-permute-start | bytes 3145736 | tf_op jit(solution)/shard_map/ppermute | solution.py:214
  339.6 46.7 %collective-permute-start.17 = (bf16[512,1024]{1,0:T(8,128)(2,1)}, bf16[512,1024]{1,0:T(8,128)(2,1)S(1)}, u32[]{:S(2)}, u32[]{:S(2)}) collective-permute-start(bf16[512,1024]{1,0:T(8,128)(2,1)} %collective-permute-done.15.w1), channel_id=1, source_target_pairs={{2,4},{3,5},{4,2},{5,3},{10,12},{11,13},{12,10},{13,11},{18,20},{1... | collective-permute-start | bytes 3145736 | tf_op jit(solution)/shard_map/ppermute | solution.py:214
  362.1 44.8 %collective-permute-start.23 = (bf16[512,1024]{1,0:T(8,128)(2,1)S(1)}, bf16[512,1024]{1,0:T(8,128)(2,1)S(1)}, u32[]{:S(2)}, u32[]{:S(2)}) collective-permute-start(bf16[512,1024]{1,0:T(8,128)(2,1)S(1)} %get-tuple-element.23.w0), channel_id=1, source_target_pairs={{2,4},{3,5},{4,2},{5,3},{10,12},{11,13},{12,10},{13,11},{18,20},{1... | collective-permute-start | bytes 3145736 | tf_op jit(solution)/shard_map/ppermute | solution.py:214
  365.7 96.4 %collective-permute-start.30 = (bf16[512,1024]{1,0:T(8,128)(2,1)S(1)}, bf16[512,1024]{1,0:T(8,128)(2,1)S(1)}, u32[]{:S(2)}, u32[]{:S(2)}) collective-permute-start(bf16[512,1024]{1,0:T(8,128)(2,1)S(1)} %get-tuple-element.21.w0), channel_id=1, source_target_pairs={{2,4},{3,5},{4,2},{5,3},{10,12},{11,13},{12,10},{13,11},{18,20},{1... | collective-permute-start | bytes 3145736 | tf_op jit(solution)/shard_map/ppermute | solution.py:214
  373.7 78.2 %collective-permute-start.24 = (bf16[512,1024]{1,0:T(8,128)(2,1)}, bf16[512,1024]{1,0:T(8,128)(2,1)S(1)}, u32[]{:S(2)}, u32[]{:S(2)}) collective-permute-start(bf16[512,1024]{1,0:T(8,128)(2,1)} %collective-permute-done.22.w1), channel_id=1, source_target_pairs={{2,4},{3,5},{4,2},{5,3},{10,12},{11,13},{12,10},{13,11},{18,20},{1... | collective-permute-start | bytes 3145736 | tf_op jit(solution)/shard_map/ppermute | solution.py:214
  376.9 97.4 %collective-permute-start.31 = (bf16[512,1024]{1,0:T(8,128)(2,1)}, bf16[512,1024]{1,0:T(8,128)(2,1)S(1)}, u32[]{:S(2)}, u32[]{:S(2)}) collective-permute-start(bf16[512,1024]{1,0:T(8,128)(2,1)} %collective-permute-done.29.w1), channel_id=1, source_target_pairs={{2,4},{3,5},{4,2},{5,3},{10,12},{11,13},{12,10},{13,11},{18,20},{1... | collective-permute-start | bytes 3145736 | tf_op jit(solution)/shard_map/ppermute | solution.py:214
  386.3 123.3 %collective-permute-start.41 = (bf16[128,1792]{1,0:T(8,128)(2,1)}, bf16[128,1792]{1,0:T(8,128)(2,1)S(1)}, u32[]{:S(2)}, u32[]{:S(2)}) collective-permute-start(bf16[128,1792]{1,0:T(8,128)(2,1)} %select_convert_fusion.1), channel_id=1, source_target_pairs={{2,0},{3,1},{4,6},{5,7},{10,8},{11,9},{12,14},{13,15},{18,16},{19,... | collective-permute-start | bytes 1376264 | tf_op jit(solution)/shard_map/ppermute | solution.py:214
  406.9 128.3 %collective-permute-start.11 = (bf16[2,2,256,256]{3,2,1,0:T(8,128)(2,1)}, bf16[2,2,256,256]{3,2,1,0:T(8,128)(2,1)}, u32[]{:S(2)}, u32[]{:S(2)}) collective-permute-start(bf16[2,2,256,256]{3,2,1,0:T(8,128)(2,1)} %hidden_grad_chunk.9), channel_id=1, source_target_pairs={{2,0},{3,1},{4,6},{5,7},{10,8},{11,9},{12,14},{13,15},{18,16},{19,... | collective-permute-start | bytes 1572872 | tf_op jit(solution)/shard_map/ppermute | solution.py:214
  451.9 77.5 %collective-permute-start.18 = (bf16[2,2,256,512]{3,2,1,0:T(8,128)(2,1)}, bf16[2,2,256,512]{3,2,1,0:T(8,128)(2,1)}, u32[]{:S(2)}, u32[]{:S(2)}) collective-permute-start(bf16[2,2,256,512]{3,2,1,0:T(8,128)(2,1)} %hidden_grad_chunk.11), channel_id=1, source_target_pairs={{2,0},{3,1},{4,6},{5,7},{10,8},{11,9},{12,14},{13,15},{18,16},{19,... | collective-permute-start | bytes 3145736 | tf_op jit(solution)/shard_map/ppermute | solution.py:214
  462.1 72.0 %collective-permute-start.25 = (bf16[2,2,256,512]{3,2,1,0:T(8,128)(2,1)S(1)}, bf16[2,2,256,512]{3,2,1,0:T(8,128)(2,1)}, u32[]{:S(2)}, u32[]{:S(2)}) collective-permute-start(bf16[2,2,256,512]{3,2,1,0:T(8,128)(2,1)S(1)} %hidden_grad_chunk.13), channel_id=1, source_target_pairs={{2,0},{3,1},{4,6},{5,7},{10,8},{11,9},{12,14},{13,15},{18,16},{19,... | collective-permute-start | bytes 3145736 | tf_op jit(solution)/shard_map/ppermute | solution.py:214
  482.2 52.6 %collective-permute-start.32 = (bf16[2,2,256,512]{3,2,1,0:T(8,128)(2,1)S(1)}, bf16[2,2,256,512]{3,2,1,0:T(8,128)(2,1)}, u32[]{:S(2)}, u32[]{:S(2)}) collective-permute-start(bf16[2,2,256,512]{3,2,1,0:T(8,128)(2,1)S(1)} %hidden_grad_chunk.15), channel_id=1, source_target_pairs={{2,0},{3,1},{4,6},{5,7},{10,8},{11,9},{12,14},{13,15},{18,16},{19,... | collective-permute-start | bytes 3145736 | tf_op jit(solution)/shard_map/ppermute | solution.py:214
  535.2 45.9 %collective-permute-start.43 = (bf16[2,128,1792]{2,1,0:T(8,128)(2,1)S(1)}, bf16[2,128,1792]{2,1,0:T(8,128)(2,1)S(1)}, u32[]{:S(2)}, u32[]{:S(2)}) collective-permute-start(bf16[2,128,1792]{2,1,0:T(8,128)(2,1)S(1)} %pad_maximum_fusion), channel_id=1, source_target_pairs={{0,8},{1,9},{2,10},{3,11},{4,12},{5,13},{6,14},{7,15},{8,0},{9,1},... | collective-permute-start | bytes 2752520 | tf_op jit(solution)/shard_map/ppermute | solution.py:214
  552.6 26.3 %collective-permute-start.12 = (bf16[256,256]{1,0:T(8,128)(2,1)S(1)}, bf16[256,256]{1,0:T(8,128)(2,1)S(1)}, u32[]{:S(2)}, u32[]{:S(2)}) collective-permute-start(bf16[256,256]{1,0:T(8,128)(2,1)S(1)} %get-tuple-element.38), channel_id=1, source_target_pairs={{0,8},{1,9},{2,10},{3,11},{4,12},{5,13},{6,14},{7,15},{8,0},{9,1},... | collective-permute-start | bytes 393224 | tf_op jit(solution)/shard_map/ppermute | solution.py:214
  552.6 26.3 %collective-permute-start.13 = (bf16[256,256]{1,0:T(8,128)(2,1)S(1)}, bf16[256,256]{1,0:T(8,128)(2,1)S(1)}, u32[]{:S(2)}, u32[]{:S(2)}) collective-permute-start(bf16[256,256]{1,0:T(8,128)(2,1)S(1)} %get-tuple-element.37), channel_id=1, source_target_pairs={{0,16},{1,17},{2,18},{3,19},{4,20},{5,21},{6,22},{7,23},{8,24},{9,... | collective-permute-start | bytes 393224 | tf_op jit(solution)/shard_map/ppermute | solution.py:214
  (29 other events, 474.1 us)
Sparse Core Ops, SparseCore 0:
  21.6 25.7 all-gather.1

commit v2 on v0

--- a/solution.py
+++ b/solution.py
@@ -1,12 +1,19 @@
+import functools
 import math
 
 import jax
 import jax.numpy as jnp
 from jax import lax
+from jax.experimental import pallas as pl
+from jax.experimental.pallas import tpu as pltpu
 from jax.sharding import PartitionSpec as P
 
-
-def local(cotangent, gate_pre, up_pre, down_weight, projector):
+AXES = ("replica", "fsdp", "tensor")
+VMEM_BYTES = 40 * 1024 * 1024
+LIGHT = pl.CostEstimate(flops=0, bytes_accessed=0, transcendentals=0)
+
+
+def general(cotangent, gate_pre, up_pre, down_weight, projector):
     whole = lax.all_gather(cotangent, "tensor", axis=1, tiled=True)
     local_rows = cotangent.shape[0]
     hidden_cols = gate_pre.shape[1]
@@ -47,7 +54,327 @@
     return (grad_gate, grad_up, projected_grad)
 
 
+def chunk_plan(quarter, unit, count):
+    units = quarter // unit
+    each = -(-units // count)
+    plan, at = [], 0
+    while at < units:
+        width = min(each, units - at)
+        plan.append((at * unit, width * unit))
+        at += width
+    return plan
+
+
+def cover(start, count, step):
+    blocks = []
+    while count:
+        size = max(n for n in range(step, count + 1, step) if start % n == 0)
+        blocks.append((size, start // size))
+        start, count = start + size, count - size
+    return blocks
+
+
+def mix_kernel(held, position, tokens, *refs):
+    kept, sent = refs[-2:]
+    rows = kept.shape[1]
+    at = position[1]
+    total = None
+    for where, pieces in ((at, refs[:held]), (1 - at, refs[held:-2])):
+        w = jnp.concatenate([piece[...] for piece in pieces], axis=0)
+        term = lax.dot_general(
+            tokens[0, where], w, (((1,), (1,)), ((), ())), preferred_element_type=jnp.float32
+        )
+        total = term if total is None else total + term
+    kept[0] = total[:rows]
+    sent[0] = total[rows:].astype(sent.dtype)
+
+
+def mix(position, tokens, weight, quarter, run, unit, pieces):
+    replicas, _, both, _ = tokens.shape
+    rows, block = both // 2, weight.shape[1]
+    offset, units = run
+    held = units // unit
+    out_spec = pl.BlockSpec((1, rows, units), lambda i, position: (i, 0, 0))
+    return pl.pallas_call(
+        functools.partial(mix_kernel, held),
+        out_shape=[
+            jax.ShapeDtypeStruct((replicas, rows, units), jnp.float32),
+            jax.ShapeDtypeStruct((replicas, rows, units), jnp.bfloat16),
+        ],
+        grid_spec=pltpu.PrefetchScalarGridSpec(
+            num_scalar_prefetch=1,
+            grid=(replicas,),
+            in_specs=[
+                pl.BlockSpec((1,) + tokens.shape[1:], lambda i, position: (position[0] ^ i, 0, 0, 0))
+            ]
+            + [
+                pl.BlockSpec(
+                    (unit, block),
+                    lambda i, position, j=j: (position[0] * (quarter // unit) + offset // unit + j, 0),
+                )
+                for j in range(held)
+            ]
+            + [
+                pl.BlockSpec((size, block), lambda i, position, index=index: (index, 0))
+                for _, size, index in pieces
+            ],
+            out_specs=[out_spec, out_spec],
+        ),
+        compiler_params=pltpu.CompilerParams(vmem_limit_bytes=60 * 1024 * 1024),
+        cost_estimate=LIGHT,
+        name="hidden_grad_chunk",
+    )(position, tokens, *[weight] * held, *(w for w, _, _ in pieces))
+
+
+def grads_kernel(position, p0, p1, p2, p3, gate, up, *refs):
+    grad_gate, grad_up = refs[-2:]
+    for d, piece in enumerate((p0, p1, p2, p3)):
+
+        @pl.when(pl.program_id(0) == d)
+        def _():
+            gate_float = gate[...].astype(jnp.float32)
+            up_float = up[...].astype(jnp.float32)
+            hidden_grad = piece[...].astype(jnp.float32)
+            sigma = jax.nn.sigmoid(gate_float)
+            grad_up[...] = (hidden_grad * (gate_float * sigma)).astype(grad_up.dtype)
+            grad_gate[...] = (
+                hidden_grad * up_float * sigma * (1.0 + gate_float * (1.0 - sigma))
+            ).astype(grad_gate.dtype)
+
+
+def grads(position, pieces, gate, up, kept, offset, quarter, unit):
+    rows, width = pieces[0].shape
+    subs = width // unit
+
+    def piece_map(d):
+        return lambda i, j, position: (0, jnp.where(i == d, j, jnp.where(i < d, 0, subs - 1)))
+
+    def column_map(i, j, position):
+        return (0, (position[0] ^ i) * (quarter // unit) + offset // unit + j)
+
+    columns = pl.BlockSpec((rows, unit), column_map)
+    anywhere = pl.BlockSpec(memory_space=pl.ANY)
+    return pl.pallas_call(
+        grads_kernel,
+        out_shape=[jax.ShapeDtypeStruct(gate.shape, jnp.bfloat16)] * 2,
+        grid_spec=pltpu.PrefetchScalarGridSpec(
+            num_scalar_prefetch=1,
+            grid=(4, subs),
+            in_specs=[pl.BlockSpec((rows, unit), piece_map(d)) for d in range(4)]
+            + [columns, columns]
+            + [anywhere] * len(kept),
+            out_specs=[columns, columns],
+        ),
+        input_output_aliases={7: 0, 8: 1} if kept else {},
+        compiler_params=pltpu.CompilerParams(vmem_limit_bytes=VMEM_BYTES),
+        cost_estimate=LIGHT,
+        name="grads_chunk",
+    )(position, *pieces, gate, up, *kept)
+
+
+def hidden_kernel(position, gate, up, *outs):
+    gate_float = gate[...].astype(jnp.float32)
+    activated = gate_float * jax.nn.sigmoid(gate_float)
+    hidden = (activated * up[...].astype(jnp.float32)).astype(jnp.bfloat16)
+    for d, out in enumerate(outs):
+
+        @pl.when(pl.program_id(0) == d)
+        def _():
+            out[...] = hidden
+
+
+def hidden_quarters(position, gate, up, quarter):
+    rows = gate.shape[0]
+    columns = pl.BlockSpec((rows, quarter), lambda i, position: (0, position[0] ^ i))
+    return pl.pallas_call(
+        hidden_kernel,
+        out_shape=[jax.ShapeDtypeStruct((rows, quarter), jnp.bfloat16)] * 4,
+        grid_spec=pltpu.PrefetchScalarGridSpec(
+            num_scalar_prefetch=1,
+            grid=(4,),
+            in_specs=[columns, columns],
+            out_specs=[pl.BlockSpec((rows, quarter), lambda i, position: (0, 0))] * 4,
+        ),
+        compiler_params=pltpu.CompilerParams(vmem_limit_bytes=VMEM_BYTES),
+        cost_estimate=LIGHT,
+        name="hidden_quarters",
+    )(position, gate, up)
+
+
+def terms_kernel(*refs):
+    total = None
+    count = len(refs) // 2
+    for low, hidden in zip(refs[:count], refs[count:-1]):
+        term = lax.dot_general(
+            low[...], hidden[...], (((0,), (0,)), ((), ())), preferred_element_type=jnp.float32
+        )
+        total = term if total is None else total + term
+    refs[-1][...] = total
+
+
+def rank_terms(low, hidden):
+    rows, quarter = hidden[0].shape
+    rank = low[0].shape[1]
+    parts = 2 if quarter % 256 == 0 else 1
+    width = quarter // parts
+    return pl.pallas_call(
+        terms_kernel,
+        out_shape=jax.ShapeDtypeStruct((rank, quarter), jnp.float32),
+        grid=(parts,),
+        in_specs=[pl.BlockSpec((rows, rank), lambda i: (0, 0))] * len(low)
+        + [pl.BlockSpec((rows, width), lambda i: (0, i))] * len(hidden),
+        out_specs=pl.BlockSpec((rank, width), lambda i: (0, i)),
+        compiler_params=pltpu.CompilerParams(vmem_limit_bytes=VMEM_BYTES),
+        cost_estimate=LIGHT,
+        name="rank_terms",
+    )(*low, *hidden)
+
+
+def line(cotangent, gate_pre, up_pre, down_weight, projector):
+    replicas, shards, tensors = (lax.axis_size(a) for a in AXES)
+    r, f, t = (lax.axis_index(a) for a in AXES)
+    rows = cotangent.shape[0]
+    quarter = down_weight.shape[0] // replicas
+    block = down_weight.shape[1]
+    bf16, f32 = jnp.bfloat16, jnp.float32
+
+    def send(x, move):
+        pairs = []
+        for a in range(replicas):
+            for b in range(shards):
+                for c in range(tensors):
+                    here = (a * shards + b) * tensors + c
+                    there = ((a ^ move[0]) * shards + (b ^ move[1])) * tensors + (c ^ move[2])
+                    pairs.append((here, there))
+        return lax.ppermute(x, AXES, pairs)
+
+    def after(x, *earlier):
+        return lax.optimization_barrier((x, *earlier))[0]
+
+    along, beyond, over_tensor = (0, 1, 0), (0, 2, 0), (0, 0, 1)
+    odd, high = f % 2, f // 2
+    position = jnp.stack([r, high]).astype(jnp.int32)
+    unit = 256 if quarter % 256 == 0 else 128
+    plan = chunk_plan(quarter, unit, 4)
+
+    def spread(kept, part):
+        total = (kept + part.astype(f32)).astype(bf16)
+        return [total[0]] + [send(total[d], (d, 0, 0)) for d in range(1, 4)]
+
+    def finish(k, pieces, written):
+        return grads(position, pieces, gate_pre, up_pre, written, plan[k][0], quarter, unit)
+
+    first = 128
+    lengths = [first, plan[0][1] - first] + [count for _, count in plan[1:]]
+    starts = [sum(lengths[:i]) for i in range(5)]
+    own_rows = [
+        lax.dynamic_slice_in_dim(down_weight, r * quarter + offset, count, 0)
+        for offset, count in zip(starts, lengths)
+    ]
+    cross = [send(own_rows[0], beyond)]
+
+    def chunk(k, *earlier):
+        at, end = plan[k][0], plan[k][0] + plan[k][1]
+        pieces = []
+        for x, start, length in zip(cross, starts, lengths):
+            low, high = max(at, start), min(end, start + length)
+            if low < high:
+                pieces += [(x, *found) for found in cover(low - start, high - low, first)]
+        return mix(position, after(tokens, *earlier), down_weight, quarter, plan[k], unit, pieces)
+
+    mine = lax.dynamic_slice_in_dim(cotangent, odd * block, block, 1)
+    give = lax.dynamic_slice_in_dim(cotangent, (1 - odd) * block, block, 1)
+    given = send(give, along)
+    tokens = jnp.concatenate([mine, after(given, cross[0])], axis=0)
+    tokens = lax.all_gather(tokens, ("replica", "tensor"))
+    tokens = tokens.reshape((replicas, tensors) + tokens.shape[1:])
+    tick = (cross[0], given)
+
+    hidden = hidden_quarters(position, gate_pre, up_pre, quarter)
+    met = {2: send(hidden[2], (2, 0, 0))}
+    cross.append(send(after(own_rows[1], *tick), beyond))
+    projector_rows = projector.shape[0] // replicas
+    part = lax.dynamic_slice_in_dim(projector, r * projector_rows, projector_rows, 0)
+    part = after(part, *tick)
+    around = [part] + [send(part, (0, d, 0)) for d in (1, 2, 3)]
+    cols = part.shape[1]
+    part = jnp.zeros((projector_rows, shards * cols), bf16)
+    for d, x in enumerate(around):
+        part = lax.dynamic_update_slice(part, x, (0, (f ^ d) * cols))
+    around = [part] + [send(part, (d, 0, 0)) for d in (1, 2, 3)]
+    early = tick
+    tick = (*around[1:], cross[1], met[2])
+
+    cross.append(send(after(own_rows[2], *early), beyond))
+    projector_full = jnp.zeros((projector.shape[0], part.shape[1]), bf16)
+    for d, x in enumerate(after(around, *tick)):
+        projector_full = lax.dynamic_update_slice(
+            projector_full, x, ((r ^ d) * projector_rows, 0)
+        )
+    partial_rank = jnp.dot(cotangent, projector_full, preferred_element_type=f32)
+    over_x = send(partial_rank, over_tensor)
+    early = tick
+    tick = (over_x,)
+
+    low = (partial_rank + after(over_x, *tick)).astype(bf16)
+    lows = [low] + [send(low, (d, 0, 0)) for d in (1, 2, 3)]
+    kept, sent = [None] * 4, [None] * 4
+    kept[0], sent[0] = chunk(0, *tick)
+    parts = [send(sent[0], along)]
+    tick = (sent[0], cross[2])
+
+    cross.append(send(after(own_rows[3], *early), beyond))
+    for d in (1, 3):
+        met[d] = send(after(hidden[d], sent[0]), (d, 0, 0))
+    kept[1], sent[1] = chunk(1, *tick)
+    parts.append(send(sent[1], along))
+    early = tick
+    tick = (sent[1], cross[3])
+
+    cross.append(send(after(own_rows[4], *early), beyond))
+    total = rank_terms(after(lows, sent[1]), [hidden[0], met[1], met[2], met[3]])
+    piece = low.shape[1] // shards
+    total = total.reshape(2, 2, piece, quarter)
+    theirs = jnp.where(odd == 0, total[:, 1], total[:, 0]).astype(bf16)
+    total = jnp.where(odd == 0, total[:, 0], total[:, 1])
+    stage = send(theirs, along)
+    kept[2], sent[2] = chunk(2, *tick)
+    parts.append(send(sent[2], along))
+    pieces = [spread(after(kept[0], sent[2]), parts[0])]
+    tick = (sent[2], theirs, *pieces[0][1:], cross[4])
+
+    kept[3], sent[3] = chunk(3, *tick)
+    parts.append(send(sent[3], along))
+    total = total + after(stage, sent[3]).astype(f32)
+    theirs = jnp.where(high == 0, total[1], total[0]).astype(bf16)
+    total = jnp.where(high == 0, total[0], total[1])
+    crossed = send(theirs, beyond)
+    pieces.append(spread(after(kept[1], theirs), parts[1]))
+    written = finish(0, after(pieces[0], theirs), ())
+    tick = (written[0], *pieces[1][1:])
+
+    pieces.append(spread(after(kept[2], *tick), parts[2]))
+    written = finish(1, after(pieces[1], *tick), written)
+    scale_factor = 1.0 / math.sqrt(rows * replicas * shards)
+    final = ((total + after(crossed, *tick).astype(f32)) * scale_factor).astype(bf16)
+    over_y = send(final, (2, 0, 0))
+    tick = (parts[3], final, written[0])
+
+    pieces.append(spread(after(kept[3], *tick), parts[3]))
+    two = jnp.stack([final, over_y])
+    other = send(after(two, *pieces[2][1:]), (1, 0, 0))
+    written = finish(2, after(pieces[2], *tick), written)
+    kept = finish(3, after(pieces[3], written[0]), written)
+    projected_grad = jnp.zeros((piece, gate_pre.shape[1]), f32)
+    for d, q in ((0, two[0]), (2, two[1]), (1, other[0]), (3, other[1])):
+        projected_grad = lax.dynamic_update_slice(
+            projected_grad, q.astype(f32), (0, (r ^ d) * quarter)
+        )
+    return (kept[0], kept[1], projected_grad)
+
+
 def solution(mesh):
+    sizes = tuple(mesh.shape[a] for a in AXES)
     placed = (
         P(("replica", "fsdp"), "tensor"),
         P(("replica", "fsdp"), "tensor"),
@@ -56,7 +383,7 @@
         P("tensor", "fsdp"),
     )
     return jax.shard_map(
-        local,
+        line if sizes == (4, 4, 2) else general,
         mesh=mesh,
         in_specs=placed,
         out_specs=(

time: 1330 us -> 339 us (0.25)
  waiting for transfers between devices: 1240 us -> 169 us
  Pallas kernels: 0 us -> 63.2 us
  starting transfers between devices: 0.19 us -> 49.1 us
  matrix products: 43 us -> 0.73 us
  blocking collectives: 14.5 us -> 0 us
    all_gather x4 -> x1, waiting for transfers between devices: 1090 us -> 0.01 us  [line(): tokens = lax.all_gather(tokens, ('replica', 'tensor'))]
    ppermute x0 -> x39, waiting for transfers between devices: none -> 169 us  [send(): return lax.ppermute(x, AXES, pairs)]
    reduce_scatter x1 -> x0, waiting for transfers between devices: 150 us -> none  [local(): lax.psum_scatter(reordered, ('replica', 'fsdp'), scatter_dimension=0, til...]
    pallas_call x0 -> x10, Pallas kernels: none -> 63.2 us  [the longest x4 36.3 us: mix(): pl.pallas_call(functools.partial(mix_kernel, held), out_shape=[jax.ShapeD...]
    ppermute x0 -> x39, starting transfers between devices: none -> 49.1 us  [send(): return lax.ppermute(x, AXES, pairs)]
    dot_general x3 -> x1, matrix products: 43.1 us -> 0.73 us  [line(): jnp.dot(cotangent, projector_full, preferred_element_type=f32)]
    psum x1 -> x0, blocking collectives: 14.5 us -> none  [local(): low_rank = lax.psum(partial_rank, 'tensor').astype(jnp.bfloat16)]
  transfers between devices with their start and end apart: 5 -> 40, of which waited for: 5 -> 14; matrix products, arithmetic and copies ran while one was open for 0% -> 6% of each run, Pallas kernels for 0% -> 19%
where the time goes in v2:
time: 339 us; the launch traced here: 338 us
  waiting for transfers between devices  169 us (50%)
  Pallas kernels  63.2 us (19%)
  starting transfers between devices  49.1 us (14%)
  local copies, waits for them, and re-layouts  28.8 us (8%)
  between operations  14.6 us (4%)
  other arithmetic  12.7 us (4%)
    ppermute x39, waiting for transfers between devices, send(): return lax.ppermute(x, AXES, pairs)  169 us
    ppermute x39, starting transfers between devices, send(): return lax.ppermute(x, AXES, pairs)  49.1 us
    pallas_call x4, Pallas kernels, mix(): pl.pallas_call(functools.partial(mix_kernel, held), out_shape=[jax.ShapeD...  36.3 us
    pallas_call x4, Pallas kernels, grads(): pl.pallas_call(grads_kernel, out_shape=[jax.ShapeDtypeStruct(gate.shape,...  17.2 us
    unnamed x62, local copies, waits for them, and re-layouts  16 us
    dynamic_slice x4, local copies, waits for them, and re-layouts, line(): lax.dynamic_slice_in_dim(down_weight, r * quarter + offset, count, 0)  7.15 us
  transfers between devices with their start and end apart: 40, of which 14 were waited for; matrix products, arithmetic and copies ran while one was open for 6% of the time, Pallas kernels for 19%

profile of v2, /device:TPU:9, one launch (start us, length us, event | category | flops | bytes accessed | tf_op | source)
XLA Modules:
  0.0 337.9 jit_solution(17488614025871580871)
XLA Ops:
  9.6 2.5 collective-permute-start.1
  12.2 15.9 %collective-permute-done.1.refs_2_ = bf16[128,1024]{1,0:T(8,128)(2,1)S(1)} collective-permute-done((bf16[128,1024]{1,0:T(8,128)(2,1)S(1)}, bf16[128,1024]{1,0:T(8,128)(2,1)S(1)}, u32[]{:S(2)}, u32[]{:S(2)}) %collective-permute-start.1) | collective-permute-done | bytes 262176 | tf_op jit(solution)/shard_map/ppermute | solution.py:249
  29.9 2.0 copy-done.2
  32.0 2.0 copy-done.5
  34.0 5.6 %hidden_quarters.1 = (bf16[256,1792]{1,0:T(8,128)(2,1)S(1)}, bf16[256,1792]{1,0:T(8,128)(2,1)}, bf16[256,1792]{1,0:T(8,128)(2,1)S(1)}, bf16[256,1792]{1,0:T(8,128)(2,1)}) custom-call(s32[2]{0:T(128)S(1)} %pad_add_fusion.position, bf16[256,7168]{1,0:T(8,128)(2,1)S(1)} %copy-done.2, bf16[256,7168]{1,0:T(8,128)(2,1)S(1)} %copy-done.5), custom_call_target="tpu_custom_call" | custom-call | tf_op jit(solution)/shard_map/hidden_quarters/pallas_call | solution.py:189
  40.9 2.1 constant_dynamic-slice_fusion.3
  48.5 25.8 %collective-permute-done.4 = bf16[512,128]{1,0:T(8,128)(2,1)S(1)} collective-permute-done((bf16[512,128]{1,0:T(8,128)(2,1)S(1)}, bf16[512,128]{1,0:T(8,128)(2,1)S(1)}, u32[]{:S(2)}, u32[]{:S(2)}) %collective-permute-start.4) | collective-permute-done | bytes 131104 | tf_op jit(solution)/shard_map/ppermute | solution.py:249
  77.7 3.0 constant_dynamic-slice_fusion.1
  80.7 20.3 %collective-permute-done.6 = bf16[512,512]{1,0:T(8,128)(2,1)} collective-permute-done((bf16[512,512]{1,0:T(8,128)(2,1)S(1)}, bf16[512,512]{1,0:T(8,128)(2,1)}, u32[]{:S(2)}, u32[]{:S(2)}) %collective-permute-start.6) | collective-permute-done | bytes 524320 | tf_op jit(solution)/shard_map/ppermute | solution.py:249
  101.1 16.3 %collective-permute-done.7 = bf16[512,512]{1,0:T(8,128)(2,1)} collective-permute-done((bf16[512,512]{1,0:T(8,128)(2,1)S(1)}, bf16[512,512]{1,0:T(8,128)(2,1)}, u32[]{:S(2)}, u32[]{:S(2)}) %collective-permute-start.7) | collective-permute-done | bytes 524320 | tf_op jit(solution)/shard_map/ppermute | solution.py:249
  123.6 12.0 %collective-permute-done.10 = f32[256,512]{1,0:T(8,128)} collective-permute-done((f32[256,512]{1,0:T(8,128)S(1)}, f32[256,512]{1,0:T(8,128)}, u32[]{:S(2)}, u32[]{:S(2)}) %collective-permute-start.10) | collective-permute-done | bytes 524320 | tf_op jit(solution)/shard_map/ppermute | solution.py:249
  135.7 9.6 %hidden_grad_chunk.4 = (f32[4,256,512]{2,1,0:T(8,128)}, bf16[4,256,512]{2,1,0:T(8,128)(2,1)}) custom-call(s32[2]{0:T(128)} %copy-done.16, bf16[4,2,512,1024]{3,2,1,0:T(8,128)(2,1)} %bitcast.83, bf16[7168,1024]{1,0:T(8,128)(2,1)} %refs_0_.7, bf16[7168,1024]{1,0:T(8,128)(2,1)} %refs_0_.7, bf16[128,1024]{1,0:T(8,128)(2,1)} %copy-done.29, ...), custom_call_target="tpu_custom_call" | custom-call | tf_op jit(solution)/shard_map/hidden_grad_chunk/pallas_call | solution.py:98
  151.7 22.5 %collective-permute-done.14.refs_2_ = bf16[256,512]{1,0:T(8,128)(2,1)S(1)} collective-permute-done((bf16[256,512]{1,0:T(8,128)(2,1)S(1)}, bf16[256,512]{1,0:T(8,128)(2,1)S(1)}, u32[]{:S(2)}, u32[]{:S(2)}) %collective-permute-start.14) | collective-permute-done | bytes 262176 | tf_op jit(solution)/shard_map/ppermute | solution.py:249
  175.2 9.5 %hidden_grad_chunk.5 = (f32[4,256,512]{2,1,0:T(8,128)}, bf16[4,256,512]{2,1,0:T(8,128)(2,1)}) custom-call(s32[2]{0:T(128)} %copy-done.16, bf16[4,2,512,1024]{3,2,1,0:T(8,128)(2,1)} %bitcast.84, bf16[7168,1024]{1,0:T(8,128)(2,1)} %refs_0_.7, bf16[7168,1024]{1,0:T(8,128)(2,1)} %refs_0_.7, bf16[512,1024]{1,0:T(8,128)(2,1)} %collective-permute-done.11.refs_2_), custom_call_target="tpu_custom_call" | custom-call | tf_op jit(solution)/shard_map/hidden_grad_chunk/pallas_call | solution.py:98
  184.7 4.0 %rank_terms.1 = f32[512,1792]{1,0:T(8,128)S(1)} custom-call(bf16[256,512]{1,0:T(8,128)(2,1)S(1)} %add_convert_fusion.4.refs_0_, bf16[256,512]{1,0:T(8,128)(2,1)S(1)} %collective-permute-done.13.refs_1_, bf16[256,512]{1,0:T(8,128)(2,1)S(1)} %collective-permute-done.14.refs_2_, bf16[256,512]{1,0:T(8,128)(2,1)} %collective-permute-done.15.refs_3_, ...), custom_call_target="tpu_custom_call" | custom-call | tf_op jit(solution)/shard_map/rank_terms/pallas_call | solution.py:220
  193.0 3.5 %collective-permute-done.12.refs_2_ = bf16[512,1024]{1,0:T(8,128)(2,1)} collective-permute-done((bf16[512,1024]{1,0:T(8,128)(2,1)}, bf16[512,1024]{1,0:T(8,128)(2,1)}, u32[]{:S(2)}, u32[]{:S(2)}) %collective-permute-start.12) | collective-permute-done | bytes 1048608 | tf_op jit(solution)/shard_map/ppermute | solution.py:249
  196.5 9.5 %hidden_grad_chunk.6 = (f32[4,256,512]{2,1,0:T(8,128)}, bf16[4,256,512]{2,1,0:T(8,128)(2,1)}) custom-call(s32[2]{0:T(128)} %copy-done.16, bf16[4,2,512,1024]{3,2,1,0:T(8,128)(2,1)} %bitcast.85, bf16[7168,1024]{1,0:T(8,128)(2,1)} %refs_0_.7, bf16[7168,1024]{1,0:T(8,128)(2,1)} %refs_0_.7, bf16[512,1024]{1,0:T(8,128)(2,1)} %collective-permute-done.12.refs_2_), custom_call_target="tpu_custom_call" | custom-call | tf_op jit(solution)/shard_map/hidden_grad_chunk/pallas_call | solution.py:98
  206.0 3.1 collective-permute-start.22
  213.6 17.2 %collective-permute-done.22.refs_1_ = bf16[256,1024]{1,0:T(8,128)(2,1)S(1)} collective-permute-done((bf16[256,1024]{1,0:T(8,128)(2,1)S(1)}, bf16[256,1024]{1,0:T(8,128)(2,1)S(1)}, u32[]{:S(2)}, u32[]{:S(2)}) %collective-permute-start.22) | collective-permute-done | bytes 524320 | tf_op jit(solution)/shard_map/ppermute | solution.py:249
  234.4 7.7 %hidden_grad_chunk.7 = (f32[4,256,256]{2,1,0:T(8,128)}, bf16[4,256,256]{2,1,0:T(8,128)(2,1)}) custom-call(s32[2]{0:T(128)} %copy-done.16, bf16[4,2,512,1024]{3,2,1,0:T(8,128)(2,1)} %bitcast.86, bf16[7168,1024]{1,0:T(8,128)(2,1)} %refs_0_.7, bf16[256,1024]{1,0:T(8,128)(2,1)} %copy-done.26), custom_call_target="tpu_custom_call" | custom-call | tf_op jit(solution)/shard_map/hidden_grad_chunk/pallas_call | solution.py:98
  243.9 3.2 collective-permute-start.25
  247.0 15.6 %collective-permute-done.26 = bf16[4,256,512]{2,1,0:T(8,128)(2,1)} collective-permute-done((bf16[4,256,512]{2,1,0:T(8,128)(2,1)}, bf16[4,256,512]{2,1,0:T(8,128)(2,1)}, u32[]{:S(2)}, u32[]{:S(2)}) %collective-permute-start.26) | collective-permute-done | bytes 1048608 | tf_op jit(solution)/shard_map/ppermute | solution.py:249
  264.5 5.2 %collective-permute-start.27 = (bf16[256,512]{1,0:T(8,128)(2,1)S(1)}, bf16[256,512]{1,0:T(8,128)(2,1)S(1)}, u32[]{:S(2)}, u32[]{:S(2)}) collective-permute-start(bf16[256,512]{1,0:T(8,128)(2,1)S(1)} %get-tuple-element.142), channel_id=1, source_target_pairs={{0,8},{1,9},{2,10},{3,11},{4,12},{5,13},{6,14},{7,15},{8,0},{9,1},... | collective-permute-start | bytes 786440 | tf_op jit(solution)/shard_map/ppermute | solution.py:249
  271.5 4.8 %grads_chunk.4 = (bf16[256,7168]{1,0:T(8,128)(2,1)}, bf16[256,7168]{1,0:T(8,128)(2,1)}) custom-call(s32[2]{0:T(128)S(1)} %copy-done.17, bf16[256,512]{1,0:T(8,128)(2,1)S(1)} %get-tuple-element.100.p0, bf16[256,512]{1,0:T(8,128)(2,1)S(1)} %copy-done.11, bf16[256,512]{1,0:T(8,128)(2,1)S(1)} %copy-done.13, bf16[256,512]{1,0:T(8,128)(2,1)S(1)} %copy-done.15, ...), custom_call_target="tpu_custom_call" | custom-call | tf_op jit(solution)/shard_map/grads_chunk/pallas_call | solution.py:157
  276.3 2.3 collective-permute-start.23
  278.6 5.1 %collective-permute-done.29.p3 = bf16[256,512]{1,0:T(8,128)(2,1)S(1)} collective-permute-done((bf16[256,512]{1,0:T(8,128)(2,1)S(1)}, bf16[256,512]{1,0:T(8,128)(2,1)S(1)}, u32[]{:S(2)}, u32[]{:S(2)}) %collective-permute-start.29) | collective-permute-done | bytes 262176 | tf_op jit(solution)/shard_map/ppermute | solution.py:249
  283.7 4.5 %collective-permute-done.25 = bf16[128,1792]{1,0:T(8,128)(2,1)S(1)} collective-permute-done((bf16[128,1792]{1,0:T(8,128)(2,1)S(1)}, bf16[128,1792]{1,0:T(8,128)(2,1)S(1)}, u32[]{:S(2)}, u32[]{:S(2)}) %collective-permute-start.25) | collective-permute-done | bytes 458784 | tf_op jit(solution)/shard_map/ppermute | solution.py:249
  292.9 4.3 %collective-permute-start.34 = (bf16[256,512]{1,0:T(8,128)(2,1)S(1)}, bf16[256,512]{1,0:T(8,128)(2,1)S(1)}, u32[]{:S(2)}, u32[]{:S(2)}) collective-permute-start(bf16[256,512]{1,0:T(8,128)(2,1)S(1)} %get-tuple-element.137), channel_id=1, source_target_pairs={{0,8},{1,9},{2,10},{3,11},{4,12},{5,13},{6,14},{7,15},{8,0},{9,1},... | collective-permute-start | bytes 786440 | tf_op jit(solution)/shard_map/ppermute | solution.py:249
  299.0 4.8 %grads_chunk.5 = (bf16[256,7168]{1,0:T(8,128)(2,1)}, bf16[256,7168]{1,0:T(8,128)(2,1)}) custom-call(s32[2]{0:T(128)S(1)} %copy-done.17, bf16[256,512]{1,0:T(8,128)(2,1)S(1)} %get-tuple-element.108.p0, bf16[256,512]{1,0:T(8,128)(2,1)S(1)} %collective-permute-done.27.p1, ...), custom_call_target="tpu_custom_call", output_to_operand_aliasing={{0}: (7, {}), {1}: (8, {})} | custom-call | tf_op jit(solution)/shard_map/grads_chunk/pallas_call | solution.py:157
  305.7 7.1 %collective-permute-done.36.p3 = bf16[256,512]{1,0:T(8,128)(2,1)S(1)} collective-permute-done((bf16[256,512]{1,0:T(8,128)(2,1)S(1)}, bf16[256,512]{1,0:T(8,128)(2,1)S(1)}, u32[]{:S(2)}, u32[]{:S(2)}) %collective-permute-start.36) | collective-permute-done | bytes 262176 | tf_op jit(solution)/shard_map/ppermute | solution.py:249
  319.3 4.8 %grads_chunk.6 = (bf16[256,7168]{1,0:T(8,128)(2,1)}, bf16[256,7168]{1,0:T(8,128)(2,1)}) custom-call(s32[2]{0:T(128)S(1)} %copy-done.17, bf16[256,512]{1,0:T(8,128)(2,1)S(1)} %get-tuple-element.117.p0, bf16[256,512]{1,0:T(8,128)(2,1)S(1)} %collective-permute-done.34.p1, ...), custom_call_target="tpu_custom_call", output_to_operand_aliasing={{0}: (7, {}), {1}: (8, {})} | custom-call | tf_op jit(solution)/shard_map/grads_chunk/pallas_call | solution.py:157
  324.2 2.7 grads_chunk.7
  (158 shorter events, 64.6 us)
Async XLA Ops:
  7.2 128.5 %all-gather.3.cloned.1.call-start = ((), (), s32[]{:S(2)}) async-start(), calls=%async_computation | async-start | bytes 9437184 | tf_op jit(solution)/shard_map/all_gather | solution.py:289
  8.6 19.5 %collective-permute-start = (bf16[256,1024]{1,0:T(8,128)(2,1)S(1)}, bf16[256,1024]{1,0:T(8,128)(2,1)S(1)}, u32[]{:S(2)}, u32[]{:S(2)}) collective-permute-start(bf16[256,1024]{1,0:T(8,128)(2,1)S(1)} %get-tuple-element.148), channel_id=1, source_target_pairs={{0,2},{1,3},{2,0},{3,1},{4,6},{5,7},{6,4},{7,5},{8,10},{9,11},{10,... | collective-permute-start | bytes 1572872 | tf_op jit(solution)/shard_map/ppermute | solution.py:249
  9.6 18.4 %collective-permute-start.1 = (bf16[128,1024]{1,0:T(8,128)(2,1)S(1)}, bf16[128,1024]{1,0:T(8,128)(2,1)S(1)}, u32[]{:S(2)}, u32[]{:S(2)}) collective-permute-start(bf16[128,1024]{1,0:T(8,128)(2,1)S(1)} %constant_dynamic-slice_fusion.5), channel_id=1, source_target_pairs={{0,4},{1,5},{2,6},{3,7},{4,0},{5,1},{6,2},{7,3},{8,12},{9,13},{10,... | collective-permute-start | bytes 786440 | tf_op jit(solution)/shard_map/ppermute | solution.py:249
  39.6 41.1 %collective-permute-start.9 = (bf16[256,1792]{1,0:T(8,128)(2,1)S(1)}, bf16[256,1792]{1,0:T(8,128)(2,1)S(1)}, u32[]{:S(2)}, u32[]{:S(2)}) collective-permute-start(bf16[256,1792]{1,0:T(8,128)(2,1)S(1)} %get-tuple-element.70), channel_id=1, source_target_pairs={{0,16},{1,17},{2,18},{3,19},{4,20},{5,21},{6,22},{7,23},{8,24},{9,... | collective-permute-start | bytes 2752520 | tf_op jit(solution)/shard_map/ppermute | solution.py:249
  44.4 29.9 %collective-permute-start.4 = (bf16[512,128]{1,0:T(8,128)(2,1)S(1)}, bf16[512,128]{1,0:T(8,128)(2,1)S(1)}, u32[]{:S(2)}, u32[]{:S(2)}) collective-permute-start(bf16[512,128]{1,0:T(8,128)(2,1)S(1)} %constant_dynamic-slice_fusion.4), channel_id=1, source_target_pairs={{0,6},{1,7},{2,4},{3,5},{4,2},{5,3},{6,0},{7,1},{8,14},{9,15},{10,... | collective-permute-start | bytes 393224 | tf_op jit(solution)/shard_map/ppermute | solution.py:249
  45.6 71.7 %collective-permute-start.8 = (bf16[384,1024]{1,0:T(8,128)(2,1)}, bf16[384,1024]{1,0:T(8,128)(2,1)}, u32[]{:S(2)}, u32[]{:S(2)}) collective-permute-start(bf16[384,1024]{1,0:T(8,128)(2,1)} %constant_dynamic-slice_fusion.3), channel_id=1, source_target_pairs={{0,4},{1,5},{2,6},{3,7},{4,0},{5,1},{6,2},{7,3},{8,12},{9,13},{10,... | collective-permute-start | bytes 2359304 | tf_op jit(solution)/shard_map/ppermute | solution.py:249
  76.0 25.1 %collective-permute-start.6 = (bf16[512,512]{1,0:T(8,128)(2,1)S(1)}, bf16[512,512]{1,0:T(8,128)(2,1)}, u32[]{:S(2)}, u32[]{:S(2)}) collective-permute-start(bf16[512,512]{1,0:T(8,128)(2,1)S(1)} %constant_dynamic-update-slice_fusion.4), channel_id=1, source_target_pairs={{0,16},{1,17},{2,18},{3,19},{4,20},{5,21},{6,22},{7,23},{8,24},{9,... | collective-permute-start | bytes 1572872 | tf_op jit(solution)/shard_map/ppermute | solution.py:249
  76.2 41.2 %collective-permute-start.7 = (bf16[512,512]{1,0:T(8,128)(2,1)S(1)}, bf16[512,512]{1,0:T(8,128)(2,1)}, u32[]{:S(2)}, u32[]{:S(2)}) collective-permute-start(bf16[512,512]{1,0:T(8,128)(2,1)S(1)} %constant_dynamic-update-slice_fusion.4), channel_id=1, source_target_pairs={{0,24},{1,25},{2,26},{3,27},{4,28},{5,29},{6,30},{7,31},{8,16},{9,... | collective-permute-start | bytes 1572872 | tf_op jit(solution)/shard_map/ppermute | solution.py:249
  80.7 68.9 %collective-permute-start.11 = (bf16[512,1024]{1,0:T(8,128)(2,1)}, bf16[512,1024]{1,0:T(8,128)(2,1)}, u32[]{:S(2)}, u32[]{:S(2)}) collective-permute-start(bf16[512,1024]{1,0:T(8,128)(2,1)} %get-tuple-element.77), channel_id=1, source_target_pairs={{0,4},{1,5},{2,6},{3,7},{4,0},{5,1},{6,2},{7,3},{8,12},{9,13},{10,... | collective-permute-start | bytes 3145736 | tf_op jit(solution)/shard_map/ppermute | solution.py:249
  122.5 13.2 %collective-permute-start.10 = (f32[256,512]{1,0:T(8,128)S(1)}, f32[256,512]{1,0:T(8,128)}, u32[]{:S(2)}, u32[]{:S(2)}) collective-permute-start(f32[256,512]{1,0:T(8,128)S(1)} %convolution_bitcast_fusion), channel_id=1, source_target_pairs={{0,1},{1,0},{2,3},{3,2},{4,5},{5,4},{6,7},{7,6},{8,9},{9,8},{10,11... | collective-permute-start | bytes 1572872 | tf_op jit(solution)/shard_map/ppermute | solution.py:249
  145.3 39.4 %collective-permute-start.16 = (bf16[256,1792]{1,0:T(8,128)(2,1)}, bf16[256,1792]{1,0:T(8,128)(2,1)S(1)}, u32[]{:S(2)}, u32[]{:S(2)}) collective-permute-start(bf16[256,1792]{1,0:T(8,128)(2,1)} %get-tuple-element.90), channel_id=1, source_target_pairs={{0,8},{1,9},{2,10},{3,11},{4,12},{5,13},{6,14},{7,15},{8,0},{9,1},... | collective-permute-start | bytes 2752520 | tf_op jit(solution)/shard_map/ppermute | solution.py:249
  146.5 38.2 %collective-permute-start.17 = (bf16[256,1792]{1,0:T(8,128)(2,1)}, bf16[256,1792]{1,0:T(8,128)(2,1)}, u32[]{:S(2)}, u32[]{:S(2)}) collective-permute-start(bf16[256,1792]{1,0:T(8,128)(2,1)} %get-tuple-element.92), channel_id=1, source_target_pairs={{0,24},{1,25},{2,26},{3,27},{4,28},{5,29},{6,30},{7,31},{8,16},{9,... | collective-permute-start | bytes 2752520 | tf_op jit(solution)/shard_map/ppermute | solution.py:249
  148.4 25.8 %collective-permute-start.14 = (bf16[256,512]{1,0:T(8,128)(2,1)S(1)}, bf16[256,512]{1,0:T(8,128)(2,1)S(1)}, u32[]{:S(2)}, u32[]{:S(2)}) collective-permute-start(bf16[256,512]{1,0:T(8,128)(2,1)S(1)} %add_convert_fusion.4.refs_0_), channel_id=1, source_target_pairs={{0,16},{1,17},{2,18},{3,19},{4,20},{5,21},{6,22},{7,23},{8,24},{9,... | collective-permute-start | bytes 786440 | tf_op jit(solution)/shard_map/ppermute | solution.py:249
  149.6 46.9 %collective-permute-start.12 = (bf16[512,1024]{1,0:T(8,128)(2,1)}, bf16[512,1024]{1,0:T(8,128)(2,1)}, u32[]{:S(2)}, u32[]{:S(2)}) collective-permute-start(bf16[512,1024]{1,0:T(8,128)(2,1)} %get-tuple-element.80), channel_id=1, source_target_pairs={{0,4},{1,5},{2,6},{3,7},{4,0},{5,1},{6,2},{7,3},{8,12},{9,13},{10,... | collective-permute-start | bytes 3145736 | tf_op jit(solution)/shard_map/ppermute | solution.py:249
  151.1 58.0 %collective-permute-start.18 = (bf16[4,256,512]{2,1,0:T(8,128)(2,1)}, bf16[4,256,512]{2,1,0:T(8,128)(2,1)}, u32[]{:S(2)}, u32[]{:S(2)}) collective-permute-start(bf16[4,256,512]{2,1,0:T(8,128)(2,1)} %get-tuple-element.76), channel_id=1, source_target_pairs={{0,2},{1,3},{2,0},{3,1},{4,6},{5,7},{6,4},{7,5},{8,10},{9,11},{10,... | collective-permute-start | bytes 3145736 | tf_op jit(solution)/shard_map/ppermute | solution.py:249
  191.7 50.5 %collective-permute-start.24 = (bf16[2,128,1792]{2,1,0:T(8,128)(2,1)}, bf16[2,128,1792]{2,1,0:T(8,128)(2,1)}, u32[]{:S(2)}, u32[]{:S(2)}) collective-permute-start(bf16[2,128,1792]{2,1,0:T(8,128)(2,1)} %fusion), channel_id=1, source_target_pairs={{0,2},{1,3},{2,0},{3,1},{4,6},{5,7},{6,4},{7,5},{8,10},{9,11},{10,... | collective-permute-start | bytes 2752520 | tf_op jit(solution)/shard_map/ppermute | solution.py:249
  206.0 24.8 %collective-permute-start.22 = (bf16[256,1024]{1,0:T(8,128)(2,1)S(1)}, bf16[256,1024]{1,0:T(8,128)(2,1)S(1)}, u32[]{:S(2)}, u32[]{:S(2)}) collective-permute-start(bf16[256,1024]{1,0:T(8,128)(2,1)S(1)} %constant_dynamic-slice_fusion), channel_id=1, source_target_pairs={{0,4},{1,5},{2,6},{3,7},{4,0},{5,1},{6,2},{7,3},{8,12},{9,13},{10,... | collective-permute-start | bytes 1572872 | tf_op jit(solution)/shard_map/ppermute | solution.py:249
  210.8 21.1 %collective-permute-start.19 = (bf16[256,512]{1,0:T(8,128)(2,1)S(1)}, bf16[256,512]{1,0:T(8,128)(2,1)S(1)}, u32[]{:S(2)}, u32[]{:S(2)}) collective-permute-start(bf16[256,512]{1,0:T(8,128)(2,1)S(1)} %get-tuple-element.146), channel_id=1, source_target_pairs={{0,8},{1,9},{2,10},{3,11},{4,12},{5,13},{6,14},{7,15},{8,0},{9,1},... | collective-permute-start | bytes 786440 | tf_op jit(solution)/shard_map/ppermute | solution.py:249
  211.9 21.1 %collective-permute-start.20 = (bf16[256,512]{1,0:T(8,128)(2,1)S(1)}, bf16[256,512]{1,0:T(8,128)(2,1)S(1)}, u32[]{:S(2)}, u32[]{:S(2)}) collective-permute-start(bf16[256,512]{1,0:T(8,128)(2,1)S(1)} %get-tuple-element.145), channel_id=1, source_target_pairs={{0,16},{1,17},{2,18},{3,19},{4,20},{5,21},{6,22},{7,23},{8,24},{9,... | collective-permute-start | bytes 786440 | tf_op jit(solution)/shard_map/ppermute | solution.py:249
  212.9 20.9 %collective-permute-start.21 = (bf16[256,512]{1,0:T(8,128)(2,1)S(1)}, bf16[256,512]{1,0:T(8,128)(2,1)S(1)}, u32[]{:S(2)}, u32[]{:S(2)}) collective-permute-start(bf16[256,512]{1,0:T(8,128)(2,1)S(1)} %get-tuple-element.144), channel_id=1, source_target_pairs={{0,24},{1,25},{2,26},{3,27},{4,28},{5,29},{6,30},{7,31},{8,16},{9,... | collective-permute-start | bytes 786440 | tf_op jit(solution)/shard_map/ppermute | solution.py:249
  230.8 31.8 %collective-permute-start.26 = (bf16[4,256,512]{2,1,0:T(8,128)(2,1)}, bf16[4,256,512]{2,1,0:T(8,128)(2,1)}, u32[]{:S(2)}, u32[]{:S(2)}) collective-permute-start(bf16[4,256,512]{2,1,0:T(8,128)(2,1)} %get-tuple-element.79), channel_id=1, source_target_pairs={{0,2},{1,3},{2,0},{3,1},{4,6},{5,7},{6,4},{7,5},{8,10},{9,11},{10,... | collective-permute-start | bytes 3145736 | tf_op jit(solution)/shard_map/ppermute | solution.py:249
  232.6 58.2 %collective-permute-start.33 = (bf16[4,256,512]{2,1,0:T(8,128)(2,1)}, bf16[4,256,512]{2,1,0:T(8,128)(2,1)}, u32[]{:S(2)}, u32[]{:S(2)}) collective-permute-start(bf16[4,256,512]{2,1,0:T(8,128)(2,1)} %get-tuple-element.82), channel_id=1, source_target_pairs={{0,2},{1,3},{2,0},{3,1},{4,6},{5,7},{6,4},{7,5},{8,10},{9,11},{10,... | collective-permute-start | bytes 3145736 | tf_op jit(solution)/shard_map/ppermute | solution.py:249
  243.9 44.3 %collective-permute-start.25 = (bf16[128,1792]{1,0:T(8,128)(2,1)S(1)}, bf16[128,1792]{1,0:T(8,128)(2,1)S(1)}, u32[]{:S(2)}, u32[]{:S(2)}) collective-permute-start(bf16[128,1792]{1,0:T(8,128)(2,1)S(1)} %fusion.3), channel_id=1, source_target_pairs={{0,4},{1,5},{2,6},{3,7},{4,0},{5,1},{6,2},{7,3},{8,12},{9,13},{10,... | collective-permute-start | bytes 1376264 | tf_op jit(solution)/shard_map/ppermute | solution.py:249
  264.5 11.8 %collective-permute-start.27 = (bf16[256,512]{1,0:T(8,128)(2,1)S(1)}, bf16[256,512]{1,0:T(8,128)(2,1)S(1)}, u32[]{:S(2)}, u32[]{:S(2)}) collective-permute-start(bf16[256,512]{1,0:T(8,128)(2,1)S(1)} %get-tuple-element.142), channel_id=1, source_target_pairs={{0,8},{1,9},{2,10},{3,11},{4,12},{5,13},{6,14},{7,15},{8,0},{9,1},... | collective-permute-start | bytes 786440 | tf_op jit(solution)/shard_map/ppermute | solution.py:249
  270.3 13.4 %collective-permute-start.29 = (bf16[256,512]{1,0:T(8,128)(2,1)S(1)}, bf16[256,512]{1,0:T(8,128)(2,1)S(1)}, u32[]{:S(2)}, u32[]{:S(2)}) collective-permute-start(bf16[256,512]{1,0:T(8,128)(2,1)S(1)} %get-tuple-element.140), channel_id=1, source_target_pairs={{0,24},{1,25},{2,26},{3,27},{4,28},{5,29},{6,30},{7,31},{8,16},{9,... | collective-permute-start | bytes 786440 | tf_op jit(solution)/shard_map/ppermute | solution.py:249
  276.3 27.5 %collective-permute-start.23 = (bf16[4,256,256]{2,1,0:T(8,128)(2,1)S(1)}, bf16[4,256,256]{2,1,0:T(8,128)(2,1)S(1)}, u32[]{:S(2)}, u32[]{:S(2)}) collective-permute-start(bf16[4,256,256]{2,1,0:T(8,128)(2,1)S(1)} %copy-done.30), channel_id=1, source_target_pairs={{0,2},{1,3},{2,0},{3,1},{4,6},{5,7},{6,4},{7,5},{8,10},{9,11},{10,... | collective-permute-start | bytes 1572872 | tf_op jit(solution)/shard_map/ppermute | solution.py:249
  288.8 15.1 %collective-permute-start.37 = (bf16[128,1792]{1,0:T(8,128)(2,1)S(1)}, bf16[128,1792]{1,0:T(8,128)(2,1)S(1)}, u32[]{:S(2)}, u32[]{:S(2)}) collective-permute-start(bf16[128,1792]{1,0:T(8,128)(2,1)S(1)} %get-tuple-element.132), channel_id=1, source_target_pairs={{0,16},{1,17},{2,18},{3,19},{4,20},{5,21},{6,22},{7,23},{8,24},{9,... | collective-permute-start | bytes 1376264 | tf_op jit(solution)/shard_map/ppermute | solution.py:249
  292.9 11.0 %collective-permute-start.34 = (bf16[256,512]{1,0:T(8,128)(2,1)S(1)}, bf16[256,512]{1,0:T(8,128)(2,1)S(1)}, u32[]{:S(2)}, u32[]{:S(2)}) collective-permute-start(bf16[256,512]{1,0:T(8,128)(2,1)S(1)} %get-tuple-element.137), channel_id=1, source_target_pairs={{0,8},{1,9},{2,10},{3,11},{4,12},{5,13},{6,14},{7,15},{8,0},{9,1},... | collective-permute-start | bytes 786440 | tf_op jit(solution)/shard_map/ppermute | solution.py:249
  298.5 14.2 %collective-permute-start.36 = (bf16[256,512]{1,0:T(8,128)(2,1)S(1)}, bf16[256,512]{1,0:T(8,128)(2,1)S(1)}, u32[]{:S(2)}, u32[]{:S(2)}) collective-permute-start(bf16[256,512]{1,0:T(8,128)(2,1)S(1)} %get-tuple-element.135), channel_id=1, source_target_pairs={{0,24},{1,25},{2,26},{3,27},{4,28},{5,29},{6,30},{7,31},{8,16},{9,... | collective-permute-start | bytes 786440 | tf_op jit(solution)/shard_map/ppermute | solution.py:249
  312.7 14.2 %collective-permute-start.38 = (bf16[2,128,1792]{2,1,0:T(8,128)(2,1)S(1)}, bf16[2,128,1792]{2,1,0:T(8,128)(2,1)}, u32[]{:S(2)}, u32[]{:S(2)}) collective-permute-start(bf16[2,128,1792]{2,1,0:T(8,128)(2,1)S(1)} %pad_maximum_fusion.1), channel_id=1, source_target_pairs={{0,8},{1,9},{2,10},{3,11},{4,12},{5,13},{6,14},{7,15},{8,0},{9,1},... | collective-permute-start | bytes 2752520 | tf_op jit(solution)/shard_map/ppermute | solution.py:249
  312.9 11.2 %collective-permute-start.30 = (bf16[256,256]{1,0:T(8,128)(2,1)S(1)}, bf16[256,256]{1,0:T(8,128)(2,1)S(1)}, u32[]{:S(2)}, u32[]{:S(2)}) collective-permute-start(bf16[256,256]{1,0:T(8,128)(2,1)S(1)} %get-tuple-element.151), channel_id=1, source_target_pairs={{0,8},{1,9},{2,10},{3,11},{4,12},{5,13},{6,14},{7,15},{8,0},{9,1},... | collective-permute-start | bytes 393224 | tf_op jit(solution)/shard_map/ppermute | solution.py:249
  313.5 10.6 %collective-permute-start.31 = (bf16[256,256]{1,0:T(8,128)(2,1)S(1)}, bf16[256,256]{1,0:T(8,128)(2,1)S(1)}, u32[]{:S(2)}, u32[]{:S(2)}) collective-permute-start(bf16[256,256]{1,0:T(8,128)(2,1)S(1)} %get-tuple-element.150), channel_id=1, source_target_pairs={{0,16},{1,17},{2,18},{3,19},{4,20},{5,21},{6,22},{7,23},{8,24},{9,... | collective-permute-start | bytes 393224 | tf_op jit(solution)/shard_map/ppermute | solution.py:249
  (39 other events, 311.4 us)
Sparse Core Ops, SparseCore 0:
  30.0 83.2 all-gather.2

commit v3 on v0

--- a/solution.py
+++ b/solution.py
@@ -1,12 +1,19 @@
+import functools
 import math
 
 import jax
 import jax.numpy as jnp
 from jax import lax
+from jax.experimental import pallas as pl
+from jax.experimental.pallas import tpu as pltpu
 from jax.sharding import PartitionSpec as P
 
-
-def local(cotangent, gate_pre, up_pre, down_weight, projector):
+AXES = ("replica", "fsdp", "tensor")
+VMEM_BYTES = 40 * 1024 * 1024
+LIGHT = pl.CostEstimate(flops=0, bytes_accessed=0, transcendentals=0)
+
+
+def general(cotangent, gate_pre, up_pre, down_weight, projector):
     whole = lax.all_gather(cotangent, "tensor", axis=1, tiled=True)
     local_rows = cotangent.shape[0]
     hidden_cols = gate_pre.shape[1]
@@ -47,7 +54,401 @@
     return (grad_gate, grad_up, projected_grad)
 
 
+def chunk_plan(quarter, unit, count):
+    units = quarter // unit
+    each = -(-units // count)
+    plan, at = [], 0
+    while at < units:
+        width = min(each, units - at)
+        plan.append((at * unit, width * unit))
+        at += width
+    return plan
+
+
+def mix_kernel(position, tokens, own, cross, *refs):
+    columns, out = refs[:-1], refs[-1]
+    replicas, _, rows, block = tokens.shape
+    at = position[1]
+    unit = own.shape[0]
+    step = pl.program_id(0)
+    where = pl.ds(pl.multiple_of(step * unit, unit), unit)
+    total = None
+    for side, w in ((at, own[...]), (1 - at, cross[...])):
+        x = tokens[:, side].reshape(replicas * rows, block)
+        term = lax.dot_general(
+            x, w, (((1,), (1,)), ((), ())), preferred_element_type=jnp.float32
+        )
+        total = term if total is None else total + term
+    for a in range(replicas):
+        out[position[0] ^ a, :, where] = total[a * rows : (a + 1) * rows].astype(out.dtype)
+    if columns:
+        width = columns[0].shape[1]
+
+        @pl.when(step == 0)
+        def _():
+            total = None
+            for side, p in enumerate(columns):
+                x = tokens[:, side].reshape(replicas * rows, block)
+                term = jnp.dot(x, p[...], preferred_element_type=jnp.float32)
+                total = term if total is None else total + term
+            for a in range(replicas):
+                out[position[0] ^ a, :, out.shape[2] - width :] = total[
+                    a * rows : (a + 1) * rows
+                ].astype(out.dtype)
+
+
+def mix(position, tokens, weight, quarter, run, unit, cross, columns, kind, cost):
+    replicas, _, rows, _ = tokens.shape
+    block = weight.shape[1]
+    offset, units = run
+    shape = (replicas, rows, units + sum(p.shape[1] for p in columns[:1]))
+    return pl.pallas_call(
+        mix_kernel,
+        out_shape=jax.ShapeDtypeStruct(shape, kind),
+        grid_spec=pltpu.PrefetchScalarGridSpec(
+            num_scalar_prefetch=1,
+            grid=(units // unit,),
+            in_specs=[
+                pl.BlockSpec(tokens.shape, lambda i, position: (0, 0, 0, 0)),
+                pl.BlockSpec(
+                    (unit, block),
+                    lambda i, position: (position[0] * (quarter // unit) + offset // unit + i, 0),
+                ),
+                pl.BlockSpec((unit, block), lambda i, position: (i, 0)),
+            ]
+            + [pl.BlockSpec(p.shape, lambda i, position: (0, 0)) for p in columns],
+            out_specs=pl.BlockSpec(shape, lambda i, position: (0, 0, 0)),
+        ),
+        compiler_params=pltpu.CompilerParams(vmem_limit_bytes=60 * 1024 * 1024),
+        cost_estimate=pl.CostEstimate(flops=cost, bytes_accessed=0, transcendentals=0),
+        name="hidden_grad_chunk",
+    )(position, tokens, weight, cross, *columns)
+
+
+def join_kernel(widths, *refs):
+    count = len(widths)
+    for d, out, at_row in ((0, refs[-3], 0), (1, refs[-2], 0), (2, refs[-1], 0), (3, refs[-1], 1)):
+
+        @pl.when(pl.program_id(0) == d)
+        def _():
+            at = 0
+            for width, kept, part in zip(widths, refs[:count], refs[count:-3]):
+                total = kept[0, :, :width] + part[0, :, :width].astype(jnp.float32)
+                out[at_row, :, at : at + width] = total.astype(out.dtype)
+                at += width
+
+
+def join(widths, kept, parts):
+    replicas, rows, _ = kept[0].shape
+    shapes = [(count, rows, sum(widths)) for count in (1, 1, 2)]
+    return pl.pallas_call(
+        functools.partial(join_kernel, widths),
+        out_shape=[jax.ShapeDtypeStruct(shape, jnp.bfloat16) for shape in shapes],
+        grid=(replicas,),
+        in_specs=[
+            pl.BlockSpec((1, rows, x.shape[2]), lambda i: (i, 0, 0)) for x in (*kept, *parts)
+        ],
+        out_specs=[pl.BlockSpec(shape, lambda i: (0, 0, 0)) for shape in shapes],
+        compiler_params=pltpu.CompilerParams(vmem_limit_bytes=VMEM_BYTES),
+        cost_estimate=LIGHT,
+        name="hidden_grad_sum",
+    )(*kept, *parts)
+
+
+def grads_kernel(position, p0, p1, p2, p3, gate, up, *refs):
+    grad_gate, grad_up = refs[-2:]
+    for d, piece in enumerate((p0, p1, p2, p3)):
+
+        @pl.when(pl.program_id(0) == d)
+        def _():
+            gate_float = gate[...].astype(jnp.float32)
+            up_float = up[...].astype(jnp.float32)
+            hidden_grad = piece[0].astype(jnp.float32)
+            sigma = jax.nn.sigmoid(gate_float)
+            grad_up[...] = (hidden_grad * (gate_float * sigma)).astype(grad_up.dtype)
+            grad_gate[...] = (
+                hidden_grad * up_float * sigma * (1.0 + gate_float * (1.0 - sigma))
+            ).astype(grad_gate.dtype)
+
+
+def grads(position, pieces, gate, up, kept, offset, quarter, unit):
+    _, rows, width = pieces[0][0].shape
+    subs = width // unit
+
+    def piece_map(d):
+        which = pieces[d][1]
+        return lambda i, j, position: (
+            which,
+            0,
+            jnp.where(i == d, j, jnp.where(i < d, 0, subs - 1)),
+        )
+
+    def column_map(i, j, position):
+        return (0, (position[0] ^ i) * (quarter // unit) + offset // unit + j)
+
+    columns = pl.BlockSpec((rows, unit), column_map)
+    anywhere = pl.BlockSpec(memory_space=pl.ANY)
+    return pl.pallas_call(
+        grads_kernel,
+        out_shape=[jax.ShapeDtypeStruct(gate.shape, jnp.bfloat16)] * 2,
+        grid_spec=pltpu.PrefetchScalarGridSpec(
+            num_scalar_prefetch=1,
+            grid=(4, subs),
+            in_specs=[pl.BlockSpec((1, rows, unit), piece_map(d)) for d in range(4)]
+            + [columns, columns]
+            + [anywhere] * len(kept),
+            out_specs=[columns, columns],
+        ),
+        input_output_aliases={7: 0, 8: 1} if kept else {},
+        compiler_params=pltpu.CompilerParams(vmem_limit_bytes=VMEM_BYTES),
+        cost_estimate=pl.CostEstimate(
+            flops=0, bytes_accessed=4 * 10 * rows * width, transcendentals=0
+        ),
+        name="grads_chunk",
+    )(position, *(x for x, _ in pieces), gate, up, *kept)
+
+
+def hidden_kernel(position, gate, up, *outs):
+    gate_float = gate[...].astype(jnp.float32)
+    activated = gate_float * jax.nn.sigmoid(gate_float)
+    hidden = (activated * up[...].astype(jnp.float32)).astype(jnp.bfloat16)
+    for d, out in enumerate(outs):
+
+        @pl.when(pl.program_id(0) == d)
+        def _():
+            out[...] = hidden
+
+
+def hidden_quarters(position, gate, up, quarter):
+    rows = gate.shape[0]
+    columns = pl.BlockSpec((rows, quarter), lambda i, position: (0, position[0] ^ i))
+    return pl.pallas_call(
+        hidden_kernel,
+        out_shape=[jax.ShapeDtypeStruct((rows, quarter), jnp.bfloat16)] * 4,
+        grid_spec=pltpu.PrefetchScalarGridSpec(
+            num_scalar_prefetch=1,
+            grid=(4,),
+            in_specs=[columns, columns],
+            out_specs=[pl.BlockSpec((rows, quarter), lambda i, position: (0, 0))] * 4,
+        ),
+        compiler_params=pltpu.CompilerParams(vmem_limit_bytes=VMEM_BYTES),
+        cost_estimate=LIGHT,
+        name="hidden_quarters",
+    )(position, gate, up)
+
+
+def terms_kernel(position, *refs):
+    lows, hidden, (out, low) = refs[:4], refs[4:8], refs[8:]
+    rows, width = lows[0].shape[1:]
+
+    @pl.when(pl.program_id(0) == 0)
+    def _():
+        for e, piece in enumerate(lows):
+            at = pl.multiple_of((position[0] ^ e) * width, width)
+            for d in range(4):
+                low[d * rows : (d + 1) * rows, pl.ds(at, width)] = piece[d ^ e]
+
+    total = None
+    for d, block in enumerate(hidden):
+        term = lax.dot_general(
+            low[d * rows : (d + 1) * rows, :],
+            block[...],
+            (((0,), (0,)), ((), ())),
+            preferred_element_type=jnp.float32,
+        )
+        total = term if total is None else total + term
+    out[...] = total
+
+
+def rank_terms(position, lows, hidden):
+    rows, quarter = hidden[0].shape
+    rank = 4 * lows[0].shape[2]
+    parts = 2 if quarter % 256 == 0 else 1
+    width = quarter // parts
+    return pl.pallas_call(
+        terms_kernel,
+        out_shape=jax.ShapeDtypeStruct((rank, quarter), jnp.float32),
+        grid_spec=pltpu.PrefetchScalarGridSpec(
+            num_scalar_prefetch=1,
+            grid=(parts,),
+            in_specs=[pl.BlockSpec(lows[0].shape, lambda i, position: (0, 0, 0))] * 4
+            + [pl.BlockSpec((rows, width), lambda i, position: (0, i))] * 4,
+            out_specs=pl.BlockSpec((rank, width), lambda i, position: (0, i)),
+            scratch_shapes=[pltpu.VMEM((4 * rows, rank), jnp.bfloat16)],
+        ),
+        compiler_params=pltpu.CompilerParams(vmem_limit_bytes=VMEM_BYTES),
+        cost_estimate=LIGHT,
+        name="rank_terms",
+    )(position, *lows, *hidden)
+
+
+def widen_kernel(position, *refs):
+    for d, piece in enumerate(refs[:-1]):
+
+        @pl.when(pl.program_id(0) == d)
+        def _():
+            refs[-1][...] = piece[0].astype(refs[-1].dtype)
+
+
+def widen(position, pieces):
+    _, rows, quarter = pieces[0][0].shape
+    return pl.pallas_call(
+        widen_kernel,
+        out_shape=jax.ShapeDtypeStruct((rows, len(pieces) * quarter), jnp.float32),
+        grid_spec=pltpu.PrefetchScalarGridSpec(
+            num_scalar_prefetch=1,
+            grid=(len(pieces),),
+            in_specs=[
+                pl.BlockSpec((1, rows, quarter), lambda i, position, which=which: (which, 0, 0))
+                for _, which in pieces
+            ],
+            out_specs=pl.BlockSpec((rows, quarter), lambda i, position: (0, position[0] ^ i)),
+        ),
+        compiler_params=pltpu.CompilerParams(vmem_limit_bytes=VMEM_BYTES),
+        cost_estimate=LIGHT,
+        name="projected_grad",
+    )(position, *(x for x, _ in pieces))
+
+
+def line(cotangent, gate_pre, up_pre, down_weight, projector):
+    replicas, shards, tensors = (lax.axis_size(a) for a in AXES)
+    r, f, t = (lax.axis_index(a) for a in AXES)
+    rows = cotangent.shape[0]
+    quarter = down_weight.shape[0] // replicas
+    block = down_weight.shape[1]
+    bf16, f32 = jnp.bfloat16, jnp.float32
+
+    def send(x, move, sends=lambda a, b, c: True):
+        pairs = []
+        for a in range(replicas):
+            for b in range(shards):
+                for c in range(tensors):
+                    here = (a * shards + b) * tensors + c
+                    there = ((a ^ move[0]) * shards + (b ^ move[1])) * tensors + (c ^ move[2])
+                    if sends(a, b, c):
+                        pairs.append((here, there))
+        return lax.ppermute(x, AXES, pairs)
+
+    def after(x, *earlier):
+        return lax.optimization_barrier((x, *earlier))[0]
+
+    along, beyond, over_tensor = (0, 1, 0), (0, 2, 0), (0, 0, 1)
+    odd, high = f % 2, f // 2
+    position = jnp.stack([r, high]).astype(jnp.int32)
+    unit = 256 if quarter % 256 == 0 else 128
+    plan = chunk_plan(quarter, unit, 4)
+
+    def total_of(first, kept, parts):
+        return join([plan[first + i][1] for i in range(len(kept))], kept, parts)
+
+    def over_replicas(total, *earlier):
+        return send(after(total[2], *earlier), (2, 0, 0))
+
+    def over_cores(total, arrived, *earlier):
+        x = jnp.concatenate([total[1], arrived[1:]], axis=0)
+        return send(after(x, *earlier), (1, 0, 0))
+
+    def finish(k, total, arrived, last, written):
+        pieces = [(total[0], 0), (last, 0), (arrived, 0), (last, 1)]
+        return grads(position, pieces, gate_pre, up_pre, written, plan[k][0], quarter, unit)
+
+    own_rows = [
+        lax.dynamic_slice_in_dim(down_weight, r * quarter + offset, count, 0)
+        for offset, count in plan
+    ]
+
+    def chunk(k, tokens, kind, columns=(), cost=0):
+        return mix(
+            position, tokens, down_weight, quarter, plan[k], unit, cross[k], columns, kind, cost
+        )
+
+    mine = lax.dynamic_slice_in_dim(cotangent, odd * block, block, 1)
+    give = lax.dynamic_slice_in_dim(cotangent, (1 - odd) * block, block, 1)
+    given = send(give, along)
+    halves = [projector[:block], projector[block:]]
+    found = jnp.where(odd == 0, halves[0], halves[1])
+    for d in (1, 2, 3):
+        x = jnp.where((odd == 0) == (d == 2), halves[0], halves[1])
+        column = send(x, (0, d, 0), lambda a, b, c: a == b)
+        found = jnp.where(r ^ f == d, column, found)
+    def everyone(x):
+        return lax.all_gather(x, ("replica", "tensor")).reshape((replicas, tensors) + x.shape)
+
+    theirs_all = everyone(after(given, found))
+    mine_all = everyone(after(mine, given, found))
+    hidden = hidden_quarters(position, gate_pre, up_pre, quarter)
+    tick = (given, found)
+    light, heavy = 0, 16 * rows * block * plan[0][1]
+
+    cross = [send(after(own_rows[0], *tick), beyond)]
+    theirs = send(after(found, *tick), over_tensor)
+    columns = [jnp.where(t == 0, found, theirs), jnp.where(t == 0, theirs, found)]
+    met = {1: send(after(hidden[1], *tick), (1, 0, 0))}
+    sent = [chunk(0, after(theirs_all, *tick), bf16, columns, heavy)]
+    tick = (sent[0], met[1])
+
+    cross.append(send(after(own_rows[1], *tick), beyond))
+    parts = [send(after(sent[0], *tick), along)]
+    met[2] = send(after(hidden[2], *tick), (2, 0, 0))
+    met[3] = send(after(hidden[3], *tick), (3, 0, 0))
+    kept = [chunk(0, after(mine_all, *tick), f32, columns, light)]
+    sent.append(chunk(1, after(theirs_all, *tick), bf16, (), heavy))
+    tick = (sent[1], parts[0], met[2], met[3], kept[0])
+
+    cross.append(send(after(own_rows[2], *tick), beyond))
+    parts.append(send(after(sent[1], *tick), along))
+    width = plan[0][1]
+    low = (kept[0][:, :, width:] + after(parts[0], *tick)[:, :, width:].astype(f32)).astype(bf16)
+    lows = [low] + [send(low, (d, 0, 0)) for d in (1, 2, 3)]
+    kept.append(chunk(1, after(mine_all, *tick), f32, (), light))
+    total = rank_terms(position, after(lows, kept[1]), [hidden[0], met[1], met[2], met[3]])
+    piece = 4 * low.shape[2] // shards
+    total = total.reshape(2, 2, piece, quarter)
+    theirs = jnp.where(odd == 0, total[:, 1], total[:, 0]).astype(bf16)
+    total = jnp.where(odd == 0, total[:, 0], total[:, 1])
+    sent.append(chunk(2, after(theirs_all, *tick), bf16, (), heavy))
+    tick = (sent[2], theirs, parts[1])
+
+    cross.append(send(after(own_rows[3], *tick), beyond))
+    stage = send(after(theirs, *tick), along)
+    parts.append(send(after(sent[2], *tick), along))
+    first = total_of(0, after(kept, *tick), parts[:2])
+    first_y = over_replicas(first)
+    kept.append(chunk(2, after(mine_all, *tick), f32, (), light))
+    sent.append(chunk(3, after(theirs_all, *tick), bf16, (), 8 * heavy))
+    total = total + after(stage, sent[3]).astype(f32)
+    theirs = jnp.where(high == 0, total[1], total[0]).astype(bf16)
+    total = jnp.where(high == 0, total[0], total[1])
+    tick = (theirs, kept[2], parts[2], first_y)
+
+    crossed = send(after(theirs, *tick), beyond)
+    parts.append(send(after(sent[3], *tick), along))
+    first_home = over_cores(first, first_y, *tick)
+    second = total_of(2, after(kept[2:], *tick), parts[2:3])
+    second_y = over_replicas(second)
+    kept.append(chunk(3, after(mine_all, *tick), f32, (), light))
+    scale_factor = 1.0 / math.sqrt(rows * replicas * shards)
+    final = ((total + crossed.astype(f32)) * scale_factor).astype(bf16)
+    tick = (final, parts[3], kept[3], first_home, second_y)
+
+    over_y = send(after(final, *tick), (2, 0, 0))
+    second_home = over_cores(second, second_y, *tick)
+    third = total_of(3, after(kept[3:], *tick), parts[3:])
+    third_y = over_replicas(third)
+    written = finish(0, first, first_y, first_home, ())
+    tick = (over_y, second_home, third_y, written[0])
+
+    two = jnp.stack([final, over_y])
+    other = send(after(two, *tick), (1, 0, 0))
+    third_home = over_cores(third, third_y, *tick)
+    written = finish(2, second, second_y, second_home, after(written, *tick))
+    kept = finish(3, third, third_y, third_home, written)
+    projected_grad = widen(position, ((two, 0), (other, 0), (two, 1), (other, 1)))
+    return (kept[0], kept[1], projected_grad)
+
+
 def solution(mesh):
+    sizes = tuple(mesh.shape[a] for a in AXES)
     placed = (
         P(("replica", "fsdp"), "tensor"),
         P(("replica", "fsdp"), "tensor"),
@@ -56,7 +457,7 @@
         P("tensor", "fsdp"),
     )
     return jax.shard_map(
-        local,
+        line if sizes == (4, 4, 2) else general,
         mesh=mesh,
         in_specs=placed,
         out_specs=(

time: 1330 us -> 328 us (0.25)
  waiting for transfers between devices: 1240 us -> 131 us
  Pallas kernels: 0 us -> 97.2 us
  starting transfers between devices: 0.19 us -> 43.2 us
  matrix products: 43 us -> 0 us
  blocking collectives: 14.5 us -> 0 us
    all_gather x4 -> x2, waiting for transfers between devices: 1090 us -> 36.6 us  [everyone(): lax.all_gather(x, ('replica', 'tensor'))]
    reduce_scatter x1 -> x0, waiting for transfers between devices: 150 us -> none  [local(): lax.psum_scatter(reordered, ('replica', 'fsdp'), scatter_dimension=0, til...]
    pallas_call x0 -> x17, Pallas kernels: none -> 97.2 us  [the longest x8 55.9 us: mix(): pl.pallas_call(mix_kernel, out_shape=jax.ShapeDtypeStruct(shape, kind), g...]
    ppermute x0 -> x29, waiting for transfers between devices: none -> 93.5 us  [send(): return lax.ppermute(x, AXES, pairs)]
    ppermute x0 -> x29, starting transfers between devices: none -> 43.1 us  [send(): return lax.ppermute(x, AXES, pairs)]
    dot_general x3 -> x0, matrix products: 43.1 us -> none  [the longest x1 28.8 us: local(): lax.dot_general(whole, lax.all_gather(down_weight, 'fsdp', axis=1, tiled=...]
    unnamed x1 -> x54, local copies, waits for them, and re-layouts: 4.23 us -> 19.4 us
    psum x1 -> x0, blocking collectives: 14.5 us -> none  [local(): low_rank = lax.psum(partial_rank, 'tensor').astype(jnp.bfloat16)]
  transfers between devices with their start and end apart: 5 -> 31, of which waited for: 5 -> 16; matrix products, arithmetic and copies ran while one was open for 0% -> 6% of each run, Pallas kernels for 0% -> 29%
where the time goes in v3:
time: 328 us; the launch traced here: 325 us
  waiting for transfers between devices  131 us (40%)
  Pallas kernels  97.2 us (30%)
  starting transfers between devices  43.2 us (13%)
  local copies, waits for them, and re-layouts  29 us (9%)
  between operations  14.3 us (4%)
  other arithmetic  10.4 us (3%)
    ppermute x29, waiting for transfers between devices, send(): return lax.ppermute(x, AXES, pairs)  93.5 us
    pallas_call x8, Pallas kernels, mix(): pl.pallas_call(mix_kernel, out_shape=jax.ShapeDtypeStruct(shape, kind), g...  55.9 us
    ppermute x29, starting transfers between devices, send(): return lax.ppermute(x, AXES, pairs)  43.1 us
    all_gather x2, waiting for transfers between devices, everyone(): lax.all_gather(x, ('replica', 'tensor'))  36.6 us
    pallas_call x3, Pallas kernels, grads(): pl.pallas_call(grads_kernel, out_shape=[jax.ShapeDtypeStruct(gate.shape,...  19.8 us
    unnamed x54, local copies, waits for them, and re-layouts  19.4 us
    pallas_call x3, Pallas kernels, join(): pl.pallas_call(functools.partial(join_kernel, widths), out_shape=[jax.Sha...  8.4 us
  transfers between devices with their start and end apart: 31, of which 16 were waited for; matrix products, arithmetic and copies ran while one was open for 6% of the time, Pallas kernels for 29%

profile of v3, /device:TPU:9, one launch (start us, length us, event | category | flops | bytes accessed | tf_op | source)
XLA Modules:
  0.0 325.0 jit_solution(8943233470067829643)
XLA Ops:
  10.4 4.5 %collective-permute-start.1 = (bf16[1024,128]{1,0:T(8,128)(2,1)S(1)}, bf16[1024,128]{1,0:T(8,128)(2,1)S(1)}, u32[]{:S(2)}, u32[]{:S(2)}) collective-permute-start(bf16[1024,128]{1,0:T(8,128)(2,1)S(1)} %get-tuple-element.131), channel_id=1, source_target_pairs={{0,6},{1,7},{10,12},{11,13},{20,18},{21,19},{30,24},{31,25}} | collective-permute-start | bytes 786440 | tf_op jit(solution)/shard_map/ppermute | solution.py:330
  25.5 3.6 %constant_dynamic-slice_fusion.1 = (bf16[512,1024]{1,0:T(8,128)(2,1)}, bf16[512,1024]{1,0:T(8,128)(2,1)}, bf16[512,1024]{1,0:T(8,128)(2,1)}) fusion(bf16[7168,1024]{1,0:T(8,128)(2,1)} %own.15, s32[]{:T(128)S(6)} %select_n.131, s32[]{:T(128)S(6)} %select_n.127, s32[]{:T(128)S(6)} %select_n.123), kind=kLoop, calls=%fused_computation.22 | loop fusion | bytes 6291468 | tf_op jit(solution)/shard_map/dynamic_slice | solution.py:356
  29.1 6.1 %collective-permute-start.4 = (bf16[512,1024]{1,0:T(8,128)(2,1)}, bf16[512,1024]{1,0:T(8,128)(2,1)S(1)}, u32[]{:S(2)}, u32[]{:S(2)}) collective-permute-start(bf16[512,1024]{1,0:T(8,128)(2,1)} %get-tuple-element.66), channel_id=1, source_target_pairs={{0,4},{1,5},{2,6},{3,7},{4,0},{5,1},{6,2},{7,3},{8,12},{9,13},{10,... | collective-permute-start | bytes 3145736 | tf_op jit(solution)/shard_map/ppermute | solution.py:330
  39.4 5.5 %hidden_quarters.1 = (bf16[256,1792]{1,0:T(8,128)(2,1)S(1)}, bf16[256,1792]{1,0:T(8,128)(2,1)S(1)}, bf16[256,1792]{1,0:T(8,128)(2,1)}, bf16[256,1792]{1,0:T(8,128)(2,1)}) custom-call(s32[2]{0:T(128)S(1)} %pad_add_fusion.position, bf16[256,7168]{1,0:T(8,128)(2,1)S(1)} %copy-done, bf16[256,7168]{1,0:T(8,128)(2,1)S(1)} %copy-done.2), custom_call_target="tpu_custom_call" | custom-call | tf_op jit(solution)/shard_map/hidden_quarters/pallas_call | solution.py:225
  49.4 6.7 %collective-permute-done.5 = bf16[1024,128]{1,0:T(8,128)(2,1)S(1)} collective-permute-done((bf16[1024,128]{1,0:T(8,128)(2,1)S(1)}, bf16[1024,128]{1,0:T(8,128)(2,1)S(1)}, u32[]{:S(2)}, u32[]{:S(2)}) %collective-permute-start.5) | collective-permute-done | bytes 262176 | tf_op jit(solution)/shard_map/ppermute | solution.py:330
  56.9 12.5 %all-gather.7.cloned.1.call-done = bf16[2048,1024]{1,0:T(8,128)(2,1)} async-done(((bf16[256,1024]{1,0:T(8,128)(2,1)}), bf16[2048,1024]{1,0:T(8,128)(2,1)}) %all-gather.7.cloned.1.call-update) | async-done | bytes 4194320 | tf_op jit(solution)/shard_map/all_gather | solution.py:375
  69.4 10.5 %collective-permute-done.4.cross = bf16[512,1024]{1,0:T(8,128)(2,1)S(1)} collective-permute-done((bf16[512,1024]{1,0:T(8,128)(2,1)}, bf16[512,1024]{1,0:T(8,128)(2,1)S(1)}, u32[]{:S(2)}, u32[]{:S(2)}) %collective-permute-start.4) | collective-permute-done | bytes 1048608 | tf_op jit(solution)/shard_map/ppermute | solution.py:330
  80.9 8.2 %hidden_grad_chunk.8 = bf16[4,256,640]{2,1,0:T(8,128)(2,1)} custom-call(s32[2]{0:T(128)} %copy-done.21, bf16[4,2,256,1024]{3,2,1,0:T(8,128)(2,1)} %bitcast.41, bf16[7168,1024]{1,0:T(8,128)(2,1)} %own.15, bf16[512,1024]{1,0:T(8,128)(2,1)} %copy-done.25, bf16[1024,128]{1,0:T(8,128)(2,1)} %get-tuple-element.129.refs_0_, ...), custom_call_target="tpu_custom_call" | custom-call | flops 2147483648 | tf_op jit(solution)/shard_map/hidden_grad_chunk/pallas_call | solution.py:105
  90.0 3.0 collective-permute-start.8
  95.4 24.2 %all-gather.5.cloned.1.call-done = bf16[2048,1024]{1,0:T(8,128)(2,1)} async-done(((bf16[256,1024]{1,0:T(8,128)(2,1)}), bf16[2048,1024]{1,0:T(8,128)(2,1)}) %all-gather.5.cloned.1.call-update) | async-done | bytes 4194320 | tf_op jit(solution)/shard_map/all_gather | solution.py:375
  119.6 8.6 %hidden_grad_chunk.9.refs_0_ = f32[4,256,640]{2,1,0:T(8,128)} custom-call(s32[2]{0:T(128)} %copy-done.21, bf16[4,2,256,1024]{3,2,1,0:T(8,128)(2,1)} %bitcast.37, bf16[7168,1024]{1,0:T(8,128)(2,1)} %own.15, bf16[512,1024]{1,0:T(8,128)(2,1)} %copy-done.25, bf16[1024,128]{1,0:T(8,128)(2,1)} %get-tuple-element.129.refs_0_, ...), custom_call_target="tpu_custom_call" | custom-call | tf_op jit(solution)/shard_map/hidden_grad_chunk/pallas_call | solution.py:105
  128.2 16.3 %collective-permute-done.8.cross = bf16[512,1024]{1,0:T(8,128)(2,1)} collective-permute-done((bf16[512,1024]{1,0:T(8,128)(2,1)}, bf16[512,1024]{1,0:T(8,128)(2,1)}, u32[]{:S(2)}, u32[]{:S(2)}) %collective-permute-start.8) | collective-permute-done | bytes 1048608 | tf_op jit(solution)/shard_map/ppermute | solution.py:330
  144.5 6.8 %hidden_grad_chunk.10 = bf16[4,256,512]{2,1,0:T(8,128)(2,1)} custom-call(s32[2]{0:T(128)} %copy-done.21, bf16[4,2,256,1024]{3,2,1,0:T(8,128)(2,1)} %bitcast.42, bf16[7168,1024]{1,0:T(8,128)(2,1)} %own.15, bf16[512,1024]{1,0:T(8,128)(2,1)} %collective-permute-done.8.cross), custom_call_target="tpu_custom_call" | custom-call | flops 2147483648 | tf_op jit(solution)/shard_map/hidden_grad_chunk/pallas_call | solution.py:105
  160.3 7.3 %hidden_grad_chunk.11.refs_1_ = f32[4,256,512]{2,1,0:T(8,128)} custom-call(s32[2]{0:T(128)} %copy-done.21, bf16[4,2,256,1024]{3,2,1,0:T(8,128)(2,1)} %bitcast.38, bf16[7168,1024]{1,0:T(8,128)(2,1)} %own.15, bf16[512,1024]{1,0:T(8,128)(2,1)} %collective-permute-done.8.cross), custom_call_target="tpu_custom_call" | custom-call | tf_op jit(solution)/shard_map/hidden_grad_chunk/pallas_call | solution.py:105
  167.6 3.4 %collective-permute-done.13.refs_3_ = bf16[4,256,128]{2,1,0:T(8,128)(2,1)} collective-permute-done((bf16[4,256,128]{2,1,0:T(8,128)(2,1)S(1)}, bf16[4,256,128]{2,1,0:T(8,128)(2,1)}, u32[]{:S(2)}, u32[]{:S(2)}) %collective-permute-start.13) | collective-permute-done | bytes 262176 | tf_op jit(solution)/shard_map/ppermute | solution.py:330
  174.5 4.7 %rank_terms.1 = f32[512,1792]{1,0:T(8,128)S(1)} custom-call(s32[2]{0:T(128)S(1)} %copy-done.22, bf16[4,256,128]{2,1,0:T(8,128)(2,1)S(1)} %fusion.3.refs_0_, bf16[4,256,128]{2,1,0:T(8,128)(2,1)S(1)} %collective-permute-done.11.refs_1_, bf16[4,256,128]{2,1,0:T(8,128)(2,1)S(1)} %collective-permute-done.12.refs_2_, ...), custom_call_target="tpu_custom_call" | custom-call | tf_op jit(solution)/shard_map/rank_terms/pallas_call | solution.py:268
  182.2 15.6 %collective-permute-done.14.cross = bf16[512,1024]{1,0:T(8,128)(2,1)} collective-permute-done((bf16[512,1024]{1,0:T(8,128)(2,1)}, bf16[512,1024]{1,0:T(8,128)(2,1)}, u32[]{:S(2)}, u32[]{:S(2)}) %collective-permute-start.14) | collective-permute-done | bytes 1048608 | tf_op jit(solution)/shard_map/ppermute | solution.py:330
  197.8 6.8 %hidden_grad_chunk.12 = bf16[4,256,512]{2,1,0:T(8,128)(2,1)} custom-call(s32[2]{0:T(128)} %copy-done.21, bf16[4,2,256,1024]{3,2,1,0:T(8,128)(2,1)} %bitcast.43, bf16[7168,1024]{1,0:T(8,128)(2,1)} %own.15, bf16[512,1024]{1,0:T(8,128)(2,1)} %collective-permute-done.14.cross), custom_call_target="tpu_custom_call" | custom-call | flops 2147483648 | tf_op jit(solution)/shard_map/hidden_grad_chunk/pallas_call | solution.py:105
  204.5 3.1 collective-permute-start.17
  210.7 3.5 %hidden_grad_sum.3 = (bf16[1,256,1024]{2,1,0:T(8,128)(2,1)S(1)}, bf16[1,256,1024]{2,1,0:T(8,128)(2,1)S(1)}, bf16[2,256,1024]{2,1,0:T(8,128)(2,1)}) custom-call(f32[4,256,640]{2,1,0:T(8,128)S(1)} %copy-done.6, f32[4,256,512]{2,1,0:T(8,128)S(1)} %copy-done.7, bf16[4,256,640]{2,1,0:T(8,128)(2,1)} %collective-permute-done.7.refs_2_, ...), custom_call_target="tpu_custom_call" | custom-call | tf_op jit(solution)/shard_map/hidden_grad_sum/pallas_call | solution.py:144
  216.6 7.3 %hidden_grad_chunk.14.refs_0_ = f32[4,256,512]{2,1,0:T(8,128)} custom-call(s32[2]{0:T(128)} %copy-done.21, bf16[4,2,256,1024]{3,2,1,0:T(8,128)(2,1)} %bitcast.39, bf16[7168,1024]{1,0:T(8,128)(2,1)} %own.15, bf16[512,1024]{1,0:T(8,128)(2,1)} %collective-permute-done.14.cross), custom_call_target="tpu_custom_call" | custom-call | tf_op jit(solution)/shard_map/hidden_grad_chunk/pallas_call | solution.py:105
  223.9 3.5 %collective-permute-done.17.cross = bf16[256,1024]{1,0:T(8,128)(2,1)} collective-permute-done((bf16[256,1024]{1,0:T(8,128)(2,1)}, bf16[256,1024]{1,0:T(8,128)(2,1)}, u32[]{:S(2)}, u32[]{:S(2)}) %collective-permute-start.17) | collective-permute-done | bytes 524320 | tf_op jit(solution)/shard_map/ppermute | solution.py:330
  227.5 5.2 %hidden_grad_chunk.13 = bf16[4,256,256]{2,1,0:T(8,128)(2,1)} custom-call(s32[2]{0:T(128)} %copy-done.21, bf16[4,2,256,1024]{3,2,1,0:T(8,128)(2,1)} %bitcast.44, bf16[7168,1024]{1,0:T(8,128)(2,1)} %own.15, bf16[256,1024]{1,0:T(8,128)(2,1)} %collective-permute-done.17.cross), custom_call_target="tpu_custom_call" | custom-call | flops 17179869184 | tf_op jit(solution)/shard_map/hidden_grad_chunk/pallas_call | solution.py:105
  232.6 3.4 %collective-permute-done.16 = bf16[2,128,1792]{2,1,0:T(8,128)(2,1)} collective-permute-done((bf16[2,128,1792]{2,1,0:T(8,128)(2,1)}, bf16[2,128,1792]{2,1,0:T(8,128)(2,1)}, u32[]{:S(2)}, u32[]{:S(2)}) %collective-permute-start.16) | collective-permute-done | bytes 917536 | tf_op jit(solution)/shard_map/ppermute | solution.py:330
  241.4 17.1 %collective-permute-done.18.refs_1_ = bf16[4,256,512]{2,1,0:T(8,128)(2,1)} collective-permute-done((bf16[4,256,512]{2,1,0:T(8,128)(2,1)}, bf16[4,256,512]{2,1,0:T(8,128)(2,1)}, u32[]{:S(2)}, u32[]{:S(2)}) %collective-permute-start.18) | collective-permute-done | bytes 1048608 | tf_op jit(solution)/shard_map/ppermute | solution.py:330
  260.2 4.3 %collective-permute-start.20 = (bf16[128,1792]{1,0:T(8,128)(2,1)}, bf16[128,1792]{1,0:T(8,128)(2,1)}, u32[]{:S(2)}, u32[]{:S(2)}) collective-permute-start(bf16[128,1792]{1,0:T(8,128)(2,1)} %fusion.4), channel_id=1, source_target_pairs={{0,4},{1,5},{2,6},{3,7},{4,0},{5,1},{6,2},{7,3},{8,12},{9,13},{10,... | collective-permute-start | bytes 1376264 | tf_op jit(solution)/shard_map/ppermute | solution.py:330
  264.5 2.9 hidden_grad_sum.4
  269.3 5.8 %hidden_grad_chunk.15.refs_0_ = f32[4,256,256]{2,1,0:T(8,128)} custom-call(s32[2]{0:T(128)} %copy-done.21, bf16[4,2,256,1024]{3,2,1,0:T(8,128)(2,1)} %bitcast.40, bf16[7168,1024]{1,0:T(8,128)(2,1)} %own.15, bf16[256,1024]{1,0:T(8,128)(2,1)} %collective-permute-done.17.cross), custom_call_target="tpu_custom_call" | custom-call | tf_op jit(solution)/shard_map/hidden_grad_chunk/pallas_call | solution.py:105
  275.1 9.5 %collective-permute-done.20 = bf16[128,1792]{1,0:T(8,128)(2,1)} collective-permute-done((bf16[128,1792]{1,0:T(8,128)(2,1)}, bf16[128,1792]{1,0:T(8,128)(2,1)}, u32[]{:S(2)}, u32[]{:S(2)}) %collective-permute-start.20) | collective-permute-done | bytes 458784 | tf_op jit(solution)/shard_map/ppermute | solution.py:330
  294.6 11.2 %grads_chunk.3 = (bf16[256,7168]{1,0:T(8,128)(2,1)}, bf16[256,7168]{1,0:T(8,128)(2,1)}) custom-call(s32[2]{0:T(128)S(1)} %copy-done.23, bf16[1,256,1024]{2,1,0:T(8,128)(2,1)S(1)} %copy-done.17, bf16[2,256,1024]{2,1,0:T(8,128)(2,1)} %collective-permute-done.22.p1.p3, bf16[2,256,1024]{2,1,0:T(8,128)(2,1)} %collective-permute-done.19.p2, ...), custom_call_target="tpu_custom_call" | custom-call | bytes 10485760 | tf_op jit(solution)/shard_map/grads_chunk/pallas_call | solution.py:191
  306.6 6.0 %grads_chunk.4 = (bf16[256,7168]{1,0:T(8,128)(2,1)}, bf16[256,7168]{1,0:T(8,128)(2,1)}) custom-call(s32[2]{0:T(128)S(1)} %copy-done.23, bf16[1,256,512]{2,1,0:T(8,128)(2,1)S(1)} %get-tuple-element.114.p0, bf16[2,256,512]{2,1,0:T(8,128)(2,1)S(1)} %collective-permute-done.26.p1.p3, ...), custom_call_target="tpu_custom_call", output_to_operand_aliasing={{0}: (7, {}), {1}: (8, {})} | custom-call | bytes 5242880 | tf_op jit(solution)/shard_map/grads_chunk/pallas_call | solution.py:191
  315.3 2.9 projected_grad.1
  (122 shorter events, 70.9 us)
Async XLA Ops:
  7.2 62.2 %all-gather.7.cloned.1.call-start = ((), (), s32[]{:S(2)}) async-start(), calls=%async_computation.1 | async-start | bytes 4718592 | tf_op jit(solution)/shard_map/all_gather | solution.py:375
  9.3 14.6 %collective-permute-start = (bf16[256,1024]{1,0:T(8,128)(2,1)S(1)}, bf16[256,1024]{1,0:T(8,128)(2,1)S(1)}, u32[]{:S(2)}, u32[]{:S(2)}) collective-permute-start(bf16[256,1024]{1,0:T(8,128)(2,1)S(1)} %get-tuple-element.126), channel_id=1, source_target_pairs={{0,2},{1,3},{2,0},{3,1},{4,6},{5,7},{6,4},{7,5},{8,10},{9,11},{10,... | collective-permute-start | bytes 1572872 | tf_op jit(solution)/shard_map/ppermute | solution.py:330
  10.4 7.8 %collective-permute-start.1 = (bf16[1024,128]{1,0:T(8,128)(2,1)S(1)}, bf16[1024,128]{1,0:T(8,128)(2,1)S(1)}, u32[]{:S(2)}, u32[]{:S(2)}) collective-permute-start(bf16[1024,128]{1,0:T(8,128)(2,1)S(1)} %get-tuple-element.131), channel_id=1, source_target_pairs={{0,6},{1,7},{10,12},{11,13},{20,18},{21,19},{30,24},{31,25}} | collective-permute-start | bytes 786440 | tf_op jit(solution)/shard_map/ppermute | solution.py:330
  14.9 6.1 %collective-permute-start.2 = (bf16[1024,128]{1,0:T(8,128)(2,1)S(1)}, bf16[1024,128]{1,0:T(8,128)(2,1)S(1)}, u32[]{:S(2)}, u32[]{:S(2)}) collective-permute-start(bf16[1024,128]{1,0:T(8,128)(2,1)S(1)} %get-tuple-element.130), channel_id=1, source_target_pairs={{0,4},{1,5},{10,14},{11,15},{20,16},{21,17},{30,26},{31,27}} | collective-permute-start | bytes 786440 | tf_op jit(solution)/shard_map/ppermute | solution.py:330
  16.2 7.7 %collective-permute-start.3 = (bf16[1024,128]{1,0:T(8,128)(2,1)S(1)}, bf16[1024,128]{1,0:T(8,128)(2,1)S(1)}, u32[]{:S(2)}, u32[]{:S(2)}) collective-permute-start(bf16[1024,128]{1,0:T(8,128)(2,1)S(1)} %get-tuple-element.131), channel_id=1, source_target_pairs={{0,2},{1,3},{10,8},{11,9},{20,22},{21,23},{30,28},{31,29}} | collective-permute-start | bytes 786440 | tf_op jit(solution)/shard_map/ppermute | solution.py:330
  24.8 94.8 %all-gather.5.cloned.1.call-start = ((), (), s32[]{:S(2)}) async-start(), calls=%async_computation | async-start | bytes 4718592 | tf_op jit(solution)/shard_map/all_gather | solution.py:375
  29.1 50.7 %collective-permute-start.4 = (bf16[512,1024]{1,0:T(8,128)(2,1)}, bf16[512,1024]{1,0:T(8,128)(2,1)S(1)}, u32[]{:S(2)}, u32[]{:S(2)}) collective-permute-start(bf16[512,1024]{1,0:T(8,128)(2,1)} %get-tuple-element.66), channel_id=1, source_target_pairs={{0,4},{1,5},{2,6},{3,7},{4,0},{5,1},{6,2},{7,3},{8,12},{9,13},{10,... | collective-permute-start | bytes 3145736 | tf_op jit(solution)/shard_map/ppermute | solution.py:330
  45.9 43.2 %collective-permute-start.6 = (bf16[256,1792]{1,0:T(8,128)(2,1)S(1)}, bf16[256,1792]{1,0:T(8,128)(2,1)S(1)}, u32[]{:S(2)}, u32[]{:S(2)}) collective-permute-start(bf16[256,1792]{1,0:T(8,128)(2,1)S(1)} %get-tuple-element.69), channel_id=1, source_target_pairs={{0,8},{1,9},{2,10},{3,11},{4,12},{5,13},{6,14},{7,15},{8,0},{9,1},... | collective-permute-start | bytes 2752520 | tf_op jit(solution)/shard_map/ppermute | solution.py:330
  48.1 7.9 %collective-permute-start.5 = (bf16[1024,128]{1,0:T(8,128)(2,1)S(1)}, bf16[1024,128]{1,0:T(8,128)(2,1)S(1)}, u32[]{:S(2)}, u32[]{:S(2)}) collective-permute-start(bf16[1024,128]{1,0:T(8,128)(2,1)S(1)} %select_select_fusion), channel_id=1, source_target_pairs={{0,1},{1,0},{2,3},{3,2},{4,5},{5,4},{6,7},{7,6},{8,9},{9,8},{10,11... | collective-permute-start | bytes 786440 | tf_op jit(solution)/shard_map/ppermute | solution.py:330
  90.0 62.3 %collective-permute-start.7 = (bf16[4,256,640]{2,1,0:T(8,128)(2,1)}, bf16[4,256,640]{2,1,0:T(8,128)(2,1)}, u32[]{:S(2)}, u32[]{:S(2)}) collective-permute-start(bf16[4,256,640]{2,1,0:T(8,128)(2,1)} %hidden_grad_chunk.8), channel_id=1, source_target_pairs={{0,2},{1,3},{2,0},{3,1},{4,6},{5,7},{6,4},{7,5},{8,10},{9,11},{10,... | collective-permute-start | bytes 3932168 | tf_op jit(solution)/shard_map/ppermute | solution.py:330
  90.0 54.5 %collective-permute-start.8 = (bf16[512,1024]{1,0:T(8,128)(2,1)}, bf16[512,1024]{1,0:T(8,128)(2,1)}, u32[]{:S(2)}, u32[]{:S(2)}) collective-permute-start(bf16[512,1024]{1,0:T(8,128)(2,1)} %get-tuple-element.73), channel_id=1, source_target_pairs={{0,4},{1,5},{2,6},{3,7},{4,0},{5,1},{6,2},{7,3},{8,12},{9,13},{10,... | collective-permute-start | bytes 3145736 | tf_op jit(solution)/shard_map/ppermute | solution.py:330
  93.0 58.3 %collective-permute-start.9 = (bf16[256,1792]{1,0:T(8,128)(2,1)}, bf16[256,1792]{1,0:T(8,128)(2,1)S(1)}, u32[]{:S(2)}, u32[]{:S(2)}) collective-permute-start(bf16[256,1792]{1,0:T(8,128)(2,1)} %get-tuple-element.75), channel_id=1, source_target_pairs={{0,16},{1,17},{2,18},{3,19},{4,20},{5,21},{6,22},{7,23},{8,24},{9,... | collective-permute-start | bytes 2752520 | tf_op jit(solution)/shard_map/ppermute | solution.py:330
  94.5 57.8 %collective-permute-start.10 = (bf16[256,1792]{1,0:T(8,128)(2,1)}, bf16[256,1792]{1,0:T(8,128)(2,1)}, u32[]{:S(2)}, u32[]{:S(2)}) collective-permute-start(bf16[256,1792]{1,0:T(8,128)(2,1)} %get-tuple-element.77), channel_id=1, source_target_pairs={{0,24},{1,25},{2,26},{3,27},{4,28},{5,29},{6,30},{7,31},{8,16},{9,... | collective-permute-start | bytes 2752520 | tf_op jit(solution)/shard_map/ppermute | solution.py:330
  152.3 45.5 %collective-permute-start.14 = (bf16[512,1024]{1,0:T(8,128)(2,1)}, bf16[512,1024]{1,0:T(8,128)(2,1)}, u32[]{:S(2)}, u32[]{:S(2)}) collective-permute-start(bf16[512,1024]{1,0:T(8,128)(2,1)} %get-tuple-element.86), channel_id=1, source_target_pairs={{0,4},{1,5},{2,6},{3,7},{4,0},{5,1},{6,2},{7,3},{8,12},{9,13},{10,... | collective-permute-start | bytes 3145736 | tf_op jit(solution)/shard_map/ppermute | solution.py:330
  152.3 52.3 %collective-permute-start.15 = (bf16[4,256,512]{2,1,0:T(8,128)(2,1)}, bf16[4,256,512]{2,1,0:T(8,128)(2,1)}, u32[]{:S(2)}, u32[]{:S(2)}) collective-permute-start(bf16[4,256,512]{2,1,0:T(8,128)(2,1)} %hidden_grad_chunk.10), channel_id=1, source_target_pairs={{0,2},{1,3},{2,0},{3,1},{4,6},{5,7},{6,4},{7,5},{8,10},{9,11},{10,... | collective-permute-start | bytes 3145736 | tf_op jit(solution)/shard_map/ppermute | solution.py:330
  153.8 13.8 %collective-permute-start.11 = (bf16[4,256,128]{2,1,0:T(8,128)(2,1)S(1)}, bf16[4,256,128]{2,1,0:T(8,128)(2,1)S(1)}, u32[]{:S(2)}, u32[]{:S(2)}) collective-permute-start(bf16[4,256,128]{2,1,0:T(8,128)(2,1)S(1)} %fusion.3.refs_0_), channel_id=1, source_target_pairs={{0,8},{1,9},{2,10},{3,11},{4,12},{5,13},{6,14},{7,15},{8,0},{9,1},... | collective-permute-start | bytes 786440 | tf_op jit(solution)/shard_map/ppermute | solution.py:330
  155.8 11.8 %collective-permute-start.12 = (bf16[4,256,128]{2,1,0:T(8,128)(2,1)S(1)}, bf16[4,256,128]{2,1,0:T(8,128)(2,1)S(1)}, u32[]{:S(2)}, u32[]{:S(2)}) collective-permute-start(bf16[4,256,128]{2,1,0:T(8,128)(2,1)S(1)} %fusion.3.refs_0_), channel_id=1, source_target_pairs={{0,16},{1,17},{2,18},{3,19},{4,20},{5,21},{6,22},{7,23},{8,24},{9,... | collective-permute-start | bytes 786440 | tf_op jit(solution)/shard_map/ppermute | solution.py:330
  158.4 12.6 %collective-permute-start.13 = (bf16[4,256,128]{2,1,0:T(8,128)(2,1)S(1)}, bf16[4,256,128]{2,1,0:T(8,128)(2,1)}, u32[]{:S(2)}, u32[]{:S(2)}) collective-permute-start(bf16[4,256,128]{2,1,0:T(8,128)(2,1)S(1)} %fusion.3.refs_0_), channel_id=1, source_target_pairs={{0,24},{1,25},{2,26},{3,27},{4,28},{5,29},{6,30},{7,31},{8,16},{9,... | collective-permute-start | bytes 786440 | tf_op jit(solution)/shard_map/ppermute | solution.py:330
  204.5 22.9 %collective-permute-start.17 = (bf16[256,1024]{1,0:T(8,128)(2,1)}, bf16[256,1024]{1,0:T(8,128)(2,1)}, u32[]{:S(2)}, u32[]{:S(2)}) collective-permute-start(bf16[256,1024]{1,0:T(8,128)(2,1)} %constant_dynamic-slice_fusion), channel_id=1, source_target_pairs={{0,4},{1,5},{2,6},{3,7},{4,0},{5,1},{6,2},{7,3},{8,12},{9,13},{10,... | collective-permute-start | bytes 1572872 | tf_op jit(solution)/shard_map/ppermute | solution.py:330
  207.6 28.4 %collective-permute-start.16 = (bf16[2,128,1792]{2,1,0:T(8,128)(2,1)}, bf16[2,128,1792]{2,1,0:T(8,128)(2,1)}, u32[]{:S(2)}, u32[]{:S(2)}) collective-permute-start(bf16[2,128,1792]{2,1,0:T(8,128)(2,1)} %fusion), channel_id=1, source_target_pairs={{0,2},{1,3},{2,0},{3,1},{4,6},{5,7},{6,4},{7,5},{8,10},{9,11},{10,... | collective-permute-start | bytes 2752520 | tf_op jit(solution)/shard_map/ppermute | solution.py:330
  207.6 50.8 %collective-permute-start.18 = (bf16[4,256,512]{2,1,0:T(8,128)(2,1)}, bf16[4,256,512]{2,1,0:T(8,128)(2,1)}, u32[]{:S(2)}, u32[]{:S(2)}) collective-permute-start(bf16[4,256,512]{2,1,0:T(8,128)(2,1)} %hidden_grad_chunk.12), channel_id=1, source_target_pairs={{0,2},{1,3},{2,0},{3,1},{4,6},{5,7},{6,4},{7,5},{8,10},{9,11},{10,... | collective-permute-start | bytes 3145736 | tf_op jit(solution)/shard_map/ppermute | solution.py:330
  215.9 23.3 %collective-permute-start.19 = (bf16[2,256,1024]{2,1,0:T(8,128)(2,1)}, bf16[2,256,1024]{2,1,0:T(8,128)(2,1)}, u32[]{:S(2)}, u32[]{:S(2)}) collective-permute-start(bf16[2,256,1024]{2,1,0:T(8,128)(2,1)} %get-tuple-element.96), channel_id=1, source_target_pairs={{0,16},{1,17},{2,18},{3,19},{4,20},{5,21},{6,22},{7,23},{8,24},{9,... | collective-permute-start | bytes 3145736 | tf_op jit(solution)/shard_map/ppermute | solution.py:330
  237.4 27.1 %copy-start.24 = (f32[2,128,1792]{2,1,0:T(8,128)}, f32[2,128,1792]{2,1,0:T(8,128)S(1)}, u32[]{:S(2)}) copy-start(f32[2,128,1792]{2,1,0:T(8,128)S(1)} %bitcast_add_fusion) | copy-start | bytes 5505028
  258.5 28.3 %collective-permute-start.22 = (bf16[2,256,1024]{2,1,0:T(8,128)(2,1)}, bf16[2,256,1024]{2,1,0:T(8,128)(2,1)}, u32[]{:S(2)}, u32[]{:S(2)}) collective-permute-start(bf16[2,256,1024]{2,1,0:T(8,128)(2,1)} %pad_maximum_fusion), channel_id=1, source_target_pairs={{0,8},{1,9},{2,10},{3,11},{4,12},{5,13},{6,14},{7,15},{8,0},{9,1},... | collective-permute-start | bytes 3145736 | tf_op jit(solution)/shard_map/ppermute | solution.py:330
  260.2 24.5 %collective-permute-start.20 = (bf16[128,1792]{1,0:T(8,128)(2,1)}, bf16[128,1792]{1,0:T(8,128)(2,1)}, u32[]{:S(2)}, u32[]{:S(2)}) collective-permute-start(bf16[128,1792]{1,0:T(8,128)(2,1)} %fusion.4), channel_id=1, source_target_pairs={{0,4},{1,5},{2,6},{3,7},{4,0},{5,1},{6,2},{7,3},{8,12},{9,13},{10,... | collective-permute-start | bytes 1376264 | tf_op jit(solution)/shard_map/ppermute | solution.py:330
  264.5 22.2 %collective-permute-start.21 = (bf16[4,256,256]{2,1,0:T(8,128)(2,1)}, bf16[4,256,256]{2,1,0:T(8,128)(2,1)}, u32[]{:S(2)}, u32[]{:S(2)}) collective-permute-start(bf16[4,256,256]{2,1,0:T(8,128)(2,1)} %hidden_grad_chunk.13), channel_id=1, source_target_pairs={{0,2},{1,3},{2,0},{3,1},{4,6},{5,7},{6,4},{7,5},{8,10},{9,11},{10,... | collective-permute-start | bytes 1572872 | tf_op jit(solution)/shard_map/ppermute | solution.py:330
  268.1 18.6 %collective-permute-start.23 = (bf16[2,256,512]{2,1,0:T(8,128)(2,1)}, bf16[2,256,512]{2,1,0:T(8,128)(2,1)}, u32[]{:S(2)}, u32[]{:S(2)}) collective-permute-start(bf16[2,256,512]{2,1,0:T(8,128)(2,1)} %get-tuple-element.103), channel_id=1, source_target_pairs={{0,16},{1,17},{2,18},{3,19},{4,20},{5,21},{6,22},{7,23},{8,24},{9,... | collective-permute-start | bytes 1572872 | tf_op jit(solution)/shard_map/ppermute | solution.py:330
  286.8 19.1 %collective-permute-start.25 = (bf16[128,1792]{1,0:T(8,128)(2,1)S(1)}, bf16[128,1792]{1,0:T(8,128)(2,1)S(1)}, u32[]{:S(2)}, u32[]{:S(2)}) collective-permute-start(bf16[128,1792]{1,0:T(8,128)(2,1)S(1)} %fusion.2), channel_id=1, source_target_pairs={{0,16},{1,17},{2,18},{3,19},{4,20},{5,21},{6,22},{7,23},{8,24},{9,... | collective-permute-start | bytes 1376264 | tf_op jit(solution)/shard_map/ppermute | solution.py:330
  289.5 16.4 %collective-permute-start.26 = (bf16[2,256,512]{2,1,0:T(8,128)(2,1)S(1)}, bf16[2,256,512]{2,1,0:T(8,128)(2,1)S(1)}, u32[]{:S(2)}, u32[]{:S(2)}) collective-permute-start(bf16[2,256,512]{2,1,0:T(8,128)(2,1)S(1)} %pad_maximum_fusion.2), channel_id=1, source_target_pairs={{0,8},{1,9},{2,10},{3,11},{4,12},{5,13},{6,14},{7,15},{8,0},{9,1},... | collective-permute-start | bytes 1572872 | tf_op jit(solution)/shard_map/ppermute | solution.py:330
  293.8 12.1 %collective-permute-start.24 = (bf16[2,256,256]{2,1,0:T(8,128)(2,1)S(1)}, bf16[2,256,256]{2,1,0:T(8,128)(2,1)S(1)}, u32[]{:S(2)}, u32[]{:S(2)}) collective-permute-start(bf16[2,256,256]{2,1,0:T(8,128)(2,1)S(1)} %get-tuple-element.107), channel_id=1, source_target_pairs={{0,16},{1,17},{2,18},{3,19},{4,20},{5,21},{6,22},{7,23},{8,24},{9,... | collective-permute-start | bytes 786440 | tf_op jit(solution)/shard_map/ppermute | solution.py:330
  305.9 9.4 %collective-permute-start.28 = (bf16[2,128,1792]{2,1,0:T(8,128)(2,1)S(1)}, bf16[2,128,1792]{2,1,0:T(8,128)(2,1)S(1)}, u32[]{:S(2)}, u32[]{:S(2)}) collective-permute-start(bf16[2,128,1792]{2,1,0:T(8,128)(2,1)S(1)} %pad_maximum_fusion.1.refs_0_.refs_2_), channel_id=1, source_target_pairs={{0,8},{1,9},{2,10},{3,11},{4,12},{5,13},{6,14},{7,15},{8,0},{9,1},... | collective-permute-start | bytes 2752520 | tf_op jit(solution)/shard_map/ppermute | solution.py:330
  306.3 6.2 %collective-permute-start.27 = (bf16[2,256,256]{2,1,0:T(8,128)(2,1)S(1)}, bf16[2,256,256]{2,1,0:T(8,128)(2,1)S(1)}, u32[]{:S(2)}, u32[]{:S(2)}) collective-permute-start(bf16[2,256,256]{2,1,0:T(8,128)(2,1)S(1)} %pad_maximum_fusion.3), channel_id=1, source_target_pairs={{0,8},{1,9},{2,10},{3,11},{4,12},{5,13},{6,14},{7,15},{8,0},{9,1},... | collective-permute-start | bytes 786440 | tf_op jit(solution)/shard_map/ppermute | solution.py:330
  (26 other events, 190.6 us)
Sparse Core Ops, SparseCore 0:
  24.9 44.4 all-gather.6
  71.3 48.2 all-gather.4

commit v4 on v3

--- a/solution.py
+++ b/solution.py
@@ -9,7 +9,7 @@
 from jax.sharding import PartitionSpec as P
 
 AXES = ("replica", "fsdp", "tensor")
-VMEM_BYTES = 40 * 1024 * 1024
+VMEM_BYTES = 24 * 1024 * 1024
 LIGHT = pl.CostEstimate(flops=0, bytes_accessed=0, transcendentals=0)
 
 
@@ -119,7 +119,7 @@
             + [pl.BlockSpec(p.shape, lambda i, position: (0, 0)) for p in columns],
             out_specs=pl.BlockSpec(shape, lambda i, position: (0, 0, 0)),
         ),
-        compiler_params=pltpu.CompilerParams(vmem_limit_bytes=60 * 1024 * 1024),
+        compiler_params=pltpu.CompilerParams(vmem_limit_bytes=VMEM_BYTES),
         cost_estimate=pl.CostEstimate(flops=cost, bytes_accessed=0, transcendentals=0),
         name="hidden_grad_chunk",
     )(position, tokens, weight, cross, *columns)
@@ -384,18 +384,18 @@
     theirs = send(after(found, *tick), over_tensor)
     columns = [jnp.where(t == 0, found, theirs), jnp.where(t == 0, theirs, found)]
     met = {1: send(after(hidden[1], *tick), (1, 0, 0))}
-    sent = [chunk(0, after(theirs_all, *tick), bf16, columns, heavy)]
+    sent = [chunk(0, after(theirs_all, met[1]), bf16, columns, heavy)]
     tick = (sent[0], met[1])
 
-    cross.append(send(after(own_rows[1], *tick), beyond))
+    cross.append(send(after(own_rows[1], cross[0], theirs_all, *columns, met[1]), beyond))
     parts = [send(after(sent[0], *tick), along)]
     met[2] = send(after(hidden[2], *tick), (2, 0, 0))
     met[3] = send(after(hidden[3], *tick), (3, 0, 0))
     kept = [chunk(0, after(mine_all, *tick), f32, columns, light)]
-    sent.append(chunk(1, after(theirs_all, *tick), bf16, (), heavy))
+    sent.append(chunk(1, after(theirs_all, *tick), bf16, (), 2 * heavy))
     tick = (sent[1], parts[0], met[2], met[3], kept[0])
 
-    cross.append(send(after(own_rows[2], *tick), beyond))
+    cross.append(send(after(own_rows[2], cross[1], *tick[1:]), beyond))
     parts.append(send(after(sent[1], *tick), along))
     width = plan[0][1]
     low = (kept[0][:, :, width:] + after(parts[0], *tick)[:, :, width:].astype(f32)).astype(bf16)
@@ -406,10 +406,10 @@
     total = total.reshape(2, 2, piece, quarter)
     theirs = jnp.where(odd == 0, total[:, 1], total[:, 0]).astype(bf16)
     total = jnp.where(odd == 0, total[:, 0], total[:, 1])
-    sent.append(chunk(2, after(theirs_all, *tick), bf16, (), heavy))
+    sent.append(chunk(2, after(theirs_all, *tick), bf16, (), 3 * heavy))
     tick = (sent[2], theirs, parts[1])
 
-    cross.append(send(after(own_rows[3], *tick), beyond))
+    cross.append(send(after(own_rows[3], cross[2], *tick[1:]), beyond))
     stage = send(after(theirs, *tick), along)
     parts.append(send(after(sent[2], *tick), along))
     first = total_of(0, after(kept, *tick), parts[:2])

time: 328 us -> 322 us (0.982)
  Pallas kernels: 97.2 us -> 60.3 us
  waiting for transfers between devices: 131 us -> 148 us
  local copies, waits for them, and re-layouts: 29 us -> 45 us
  other arithmetic: 10.4 us -> 5.15 us
    ppermute x29, waiting for transfers between devices: 93.5 us -> 124 us  [send(): return lax.ppermute(x, AXES, pairs)]
    pallas_call x8, Pallas kernels: 55.9 us -> 27.3 us  [mix(): pl.pallas_call(mix_kernel, out_shape=jax.ShapeDtypeStruct(shape, kind), g...]
    unnamed x54 -> x76, local copies, waits for them, and re-layouts: 19.4 us -> 37.4 us
    all_gather x2, waiting for transfers between devices: 36.6 us -> 23.2 us  [everyone(): lax.all_gather(x, ('replica', 'tensor'))]
    pallas_call x3, Pallas kernels: 8.4 us -> 3.38 us  [join(): pl.pallas_call(functools.partial(join_kernel, widths), out_shape=[jax.Sha...]
    pallas_call x3, Pallas kernels: 19.8 us -> 16.4 us  [grads(): pl.pallas_call(grads_kernel, out_shape=[jax.ShapeDtypeStruct(gate.shape,...]
  transfers between devices with their start and end apart: 31 -> 31, of which waited for: 16 -> 14; matrix products, arithmetic and copies ran while one was open for 6% -> 3% of each run, Pallas kernels for 29% -> 18%
where the time goes in v4:
time: 322 us; the launch traced here: 318 us
  waiting for transfers between devices  148 us (46%)
  Pallas kernels  60.3 us (19%)
  local copies, waits for them, and re-layouts  45 us (14%)
  starting transfers between devices  44.6 us (14%)
  between operations  14.5 us (5%)
  other arithmetic  5.15 us (2%)
    ppermute x29, waiting for transfers between devices, send(): return lax.ppermute(x, AXES, pairs)  124 us
    ppermute x29, starting transfers between devices, send(): return lax.ppermute(x, AXES, pairs)  44.5 us
    unnamed x76, local copies, waits for them, and re-layouts  37.4 us
    pallas_call x8, Pallas kernels, mix(): pl.pallas_call(mix_kernel, out_shape=jax.ShapeDtypeStruct(shape, kind), g...  27.3 us
    all_gather x2, waiting for transfers between devices, everyone(): lax.all_gather(x, ('replica', 'tensor'))  23.2 us
    pallas_call x3, Pallas kernels, grads(): pl.pallas_call(grads_kernel, out_shape=[jax.ShapeDtypeStruct(gate.shape,...  16.4 us
  transfers between devices with their start and end apart: 31, of which 14 were waited for; matrix products, arithmetic and copies ran while one was open for 3% of the time, Pallas kernels for 18%

profile of v4, /device:TPU:9, one launch (start us, length us, event | category | flops | bytes accessed | tf_op | source)
XLA Modules:
  0.0 317.8 jit_solution(18437693226135604887)
XLA Ops:
  10.4 4.4 %collective-permute-start.2 = (bf16[1024,128]{1,0:T(8,128)(2,1)S(1)}, bf16[1024,128]{1,0:T(8,128)(2,1)S(1)}, u32[]{:S(2)}, u32[]{:S(2)}) collective-permute-start(bf16[1024,128]{1,0:T(8,128)(2,1)S(1)} %get-tuple-element.130), channel_id=1, source_target_pairs={{0,4},{1,5},{10,14},{11,15},{20,16},{21,17},{30,26},{31,27}} | collective-permute-start | bytes 786440 | tf_op jit(solution)/shard_map/ppermute | solution.py:330
  18.1 5.7 %collective-permute-done.3 = bf16[1024,128]{1,0:T(8,128)(2,1)S(1)} collective-permute-done((bf16[1024,128]{1,0:T(8,128)(2,1)S(1)}, bf16[1024,128]{1,0:T(8,128)(2,1)S(1)}, u32[]{:S(2)}, u32[]{:S(2)}) %collective-permute-start.3) | collective-permute-done | bytes 262176 | tf_op jit(solution)/shard_map/ppermute | solution.py:330
  25.6 3.6 %constant_dynamic-slice_fusion.1 = (bf16[512,1024]{1,0:T(8,128)(2,1)}, bf16[512,1024]{1,0:T(8,128)(2,1)}, bf16[512,1024]{1,0:T(8,128)(2,1)}) fusion(bf16[7168,1024]{1,0:T(8,128)(2,1)} %own.15, s32[]{:T(128)S(6)} %select_n.131, s32[]{:T(128)S(6)} %select_n.127, s32[]{:T(128)S(6)} %select_n.123), kind=kLoop, calls=%fused_computation.22 | loop fusion | bytes 6291468 | tf_op jit(solution)/shard_map/dynamic_slice | solution.py:356
  29.2 3.2 %collective-permute-start.5 = (bf16[512,1024]{1,0:T(8,128)(2,1)}, bf16[512,1024]{1,0:T(8,128)(2,1)S(1)}, u32[]{:S(2)}, u32[]{:S(2)}) collective-permute-start(bf16[512,1024]{1,0:T(8,128)(2,1)} %get-tuple-element.68), channel_id=1, source_target_pairs={{0,4},{1,5},{2,6},{3,7},{4,0},{5,1},{6,2},{7,3},{8,12},{9,13},{10,... | collective-permute-start | bytes 3145736 | tf_op jit(solution)/shard_map/ppermute | solution.py:330
  36.5 5.5 %hidden_quarters.1 = (bf16[256,1792]{1,0:T(8,128)(2,1)S(1)}, bf16[256,1792]{1,0:T(8,128)(2,1)S(1)}, bf16[256,1792]{1,0:T(8,128)(2,1)}, bf16[256,1792]{1,0:T(8,128)(2,1)}) custom-call(s32[2]{0:T(128)S(1)} %pad_add_fusion.position, bf16[256,7168]{1,0:T(8,128)(2,1)S(1)} %copy-done.6, bf16[256,7168]{1,0:T(8,128)(2,1)S(1)} %copy-done.8), custom_call_target="tpu_custom_call" | custom-call | tf_op jit(solution)/shard_map/hidden_quarters/pallas_call | solution.py:225
  43.0 7.5 %collective-permute-start.4 = (bf16[256,1792]{1,0:T(8,128)(2,1)S(1)}, bf16[256,1792]{1,0:T(8,128)(2,1)S(1)}, u32[]{:S(2)}, u32[]{:S(2)}) collective-permute-start(bf16[256,1792]{1,0:T(8,128)(2,1)S(1)} %get-tuple-element.66), channel_id=1, source_target_pairs={{0,8},{1,9},{2,10},{3,11},{4,12},{5,13},{6,14},{7,15},{8,0},{9,1},... | collective-permute-start | bytes 2752520 | tf_op jit(solution)/shard_map/ppermute | solution.py:330
  51.7 8.7 %collective-permute-done.6 = bf16[1024,128]{1,0:T(8,128)(2,1)} collective-permute-done((bf16[1024,128]{1,0:T(8,128)(2,1)S(1)}, bf16[1024,128]{1,0:T(8,128)(2,1)}, u32[]{:S(2)}, u32[]{:S(2)}) %collective-permute-start.6) | collective-permute-done | bytes 262176 | tf_op jit(solution)/shard_map/ppermute | solution.py:330
  62.4 14.6 %collective-permute-done.5.cross = bf16[512,1024]{1,0:T(8,128)(2,1)S(1)} collective-permute-done((bf16[512,1024]{1,0:T(8,128)(2,1)}, bf16[512,1024]{1,0:T(8,128)(2,1)S(1)}, u32[]{:S(2)}, u32[]{:S(2)}) %collective-permute-start.5) | collective-permute-done | bytes 1048608 | tf_op jit(solution)/shard_map/ppermute | solution.py:330
  77.0 3.0 collective-permute-start.8
  80.0 5.5 %copy-done = bf16[7168,1024]{1,0:T(8,128)(2,1)S(1)} copy-done((bf16[7168,1024]{1,0:T(8,128)(2,1)S(1)}, bf16[7168,1024]{1,0:T(8,128)(2,1)}, u32[]{:S(2)}) %copy-start) | copy-done | bytes 14680088
  87.7 5.4 %hidden_grad_chunk.8 = bf16[4,256,640]{2,1,0:T(8,128)(2,1)} custom-call(s32[2]{0:T(128)S(1)} %pad_add_fusion.position, bf16[4,2,256,1024]{3,2,1,0:T(8,128)(2,1)S(1)} %bitcast.43, bf16[7168,1024]{1,0:T(8,128)(2,1)S(1)} %copy-done, bf16[512,1024]{1,0:T(8,128)(2,1)S(1)} %collective-permute-done.5.cross, bf16[1024,128]{1,0:T(8,128)(2,1)S(1)} %get-tuple-element.129.refs_0_, ...), custom_call_target="tpu_custom_call" | custom-call | flops 2147483648 | tf_op jit(solution)/shard_map/hidden_grad_chunk/pallas_call | solution.py:105
  93.1 3.1 collective-permute-start.9
  96.8 23.2 %all-gather.5.cloned.1.call-done = bf16[2048,1024]{1,0:T(8,128)(2,1)} async-done(((bf16[256,1024]{1,0:T(8,128)(2,1)}), bf16[2048,1024]{1,0:T(8,128)(2,1)}) %all-gather.5.cloned.1.call-update) | async-done | bytes 4194320 | tf_op jit(solution)/shard_map/all_gather | solution.py:375
  120.0 5.2 %copy-done.1 = bf16[7168,1024]{1,0:T(8,128)(2,1)S(1)} copy-done((bf16[7168,1024]{1,0:T(8,128)(2,1)S(1)}, bf16[7168,1024]{1,0:T(8,128)(2,1)}, u32[]{:S(2)}) %copy-start.1) | copy-done | bytes 14680088
  127.4 4.4 %hidden_grad_chunk.9.refs_0_ = f32[4,256,640]{2,1,0:T(8,128)S(1)} custom-call(s32[2]{0:T(128)S(1)} %pad_add_fusion.position, bf16[4,2,256,1024]{3,2,1,0:T(8,128)(2,1)S(1)} %bitcast.37, bf16[7168,1024]{1,0:T(8,128)(2,1)S(1)} %copy-done.1, bf16[512,1024]{1,0:T(8,128)(2,1)S(1)} %collective-permute-done.5.cross, ...), custom_call_target="tpu_custom_call" | custom-call | tf_op jit(solution)/shard_map/hidden_grad_chunk/pallas_call | solution.py:105
  131.8 4.1 %hidden_grad_chunk.10 = bf16[4,256,512]{2,1,0:T(8,128)(2,1)} custom-call(s32[2]{0:T(128)S(1)} %pad_add_fusion.position, bf16[4,2,256,1024]{3,2,1,0:T(8,128)(2,1)S(1)} %bitcast.44, bf16[7168,1024]{1,0:T(8,128)(2,1)S(1)} %copy-done.1, bf16[512,1024]{1,0:T(8,128)(2,1)S(1)} %collective-permute-done.8.cross), custom_call_target="tpu_custom_call" | custom-call | flops 4294967296 | tf_op jit(solution)/shard_map/hidden_grad_chunk/pallas_call | solution.py:105
  136.9 10.1 %collective-permute-done.10.refs_7_ = bf16[256,1792]{1,0:T(8,128)(2,1)} collective-permute-done((bf16[256,1792]{1,0:T(8,128)(2,1)}, bf16[256,1792]{1,0:T(8,128)(2,1)}, u32[]{:S(2)}, u32[]{:S(2)}) %collective-permute-start.10) | collective-permute-done | bytes 917536 | tf_op jit(solution)/shard_map/ppermute | solution.py:330
  154.7 5.2 %copy-done.2 = bf16[7168,1024]{1,0:T(8,128)(2,1)S(1)} copy-done((bf16[7168,1024]{1,0:T(8,128)(2,1)S(1)}, bf16[7168,1024]{1,0:T(8,128)(2,1)}, u32[]{:S(2)}) %copy-start.2) | copy-done | bytes 14680088
  162.0 3.2 hidden_grad_chunk.11.refs_1_
  172.5 5.0 %rank_terms.1 = f32[512,1792]{1,0:T(8,128)S(1)} custom-call(s32[2]{0:T(128)S(1)} %pad_add_fusion.position, bf16[4,256,128]{2,1,0:T(8,128)(2,1)S(1)} %fusion.3.refs_0_, bf16[4,256,128]{2,1,0:T(8,128)(2,1)S(1)} %copy-done.31, bf16[4,256,128]{2,1,0:T(8,128)(2,1)S(1)} %copy-done.29, bf16[4,256,128]{2,1,0:T(8,128)(2,1)S(1)} %copy-done.27, ...), custom_call_target="tpu_custom_call" | custom-call | tf_op jit(solution)/shard_map/rank_terms/pallas_call | solution.py:268
  178.6 16.2 %collective-permute-done.14.cross = bf16[512,1024]{1,0:T(8,128)(2,1)S(1)} collective-permute-done((bf16[512,1024]{1,0:T(8,128)(2,1)}, bf16[512,1024]{1,0:T(8,128)(2,1)S(1)}, u32[]{:S(2)}, u32[]{:S(2)}) %collective-permute-start.14) | collective-permute-done | bytes 1048608 | tf_op jit(solution)/shard_map/ppermute | solution.py:330
  197.8 3.2 hidden_grad_chunk.12
  201.0 2.9 hidden_grad_sum.3
  205.7 3.3 %hidden_grad_chunk.14.refs_0_ = f32[4,256,512]{2,1,0:T(8,128)S(1)} custom-call(s32[2]{0:T(128)S(1)} %pad_add_fusion.position, bf16[4,2,256,1024]{3,2,1,0:T(8,128)(2,1)S(1)} %bitcast.39, bf16[7168,1024]{1,0:T(8,128)(2,1)S(1)} %bitcast.36, bf16[512,1024]{1,0:T(8,128)(2,1)S(1)} %collective-permute-done.14.cross), custom_call_target="tpu_custom_call" | custom-call | tf_op jit(solution)/shard_map/hidden_grad_chunk/pallas_call | solution.py:105
  209.0 10.5 %collective-permute-done.17.cross = bf16[256,1024]{1,0:T(8,128)(2,1)S(1)} collective-permute-done((bf16[256,1024]{1,0:T(8,128)(2,1)}, bf16[256,1024]{1,0:T(8,128)(2,1)S(1)}, u32[]{:S(2)}, u32[]{:S(2)}) %collective-permute-start.17) | collective-permute-done | bytes 524320 | tf_op jit(solution)/shard_map/ppermute | solution.py:330
  221.4 12.0 %collective-permute-done.16 = bf16[2,128,1792]{2,1,0:T(8,128)(2,1)S(1)} collective-permute-done((bf16[2,128,1792]{2,1,0:T(8,128)(2,1)}, bf16[2,128,1792]{2,1,0:T(8,128)(2,1)S(1)}, u32[]{:S(2)}, u32[]{:S(2)}) %collective-permute-start.16) | collective-permute-done | bytes 917536 | tf_op jit(solution)/shard_map/ppermute | solution.py:330
  234.0 21.8 %collective-permute-done.18.refs_1_ = bf16[4,256,512]{2,1,0:T(8,128)(2,1)S(1)} collective-permute-done((bf16[4,256,512]{2,1,0:T(8,128)(2,1)S(1)}, bf16[4,256,512]{2,1,0:T(8,128)(2,1)S(1)}, u32[]{:S(2)}, u32[]{:S(2)}) %collective-permute-start.18) | collective-permute-done | bytes 1048608 | tf_op jit(solution)/shard_map/ppermute | solution.py:330
  257.1 3.6 %collective-permute-start.20 = (bf16[128,1792]{1,0:T(8,128)(2,1)S(1)}, bf16[128,1792]{1,0:T(8,128)(2,1)S(1)}, u32[]{:S(2)}, u32[]{:S(2)}) collective-permute-start(bf16[128,1792]{1,0:T(8,128)(2,1)S(1)} %fusion.4), channel_id=1, source_target_pairs={{0,4},{1,5},{2,6},{3,7},{4,0},{5,1},{6,2},{7,3},{8,12},{9,13},{10,... | collective-permute-start | bytes 1376264 | tf_op jit(solution)/shard_map/ppermute | solution.py:330
  263.1 16.7 %collective-permute-done.20 = bf16[128,1792]{1,0:T(8,128)(2,1)S(1)} collective-permute-done((bf16[128,1792]{1,0:T(8,128)(2,1)S(1)}, bf16[128,1792]{1,0:T(8,128)(2,1)S(1)}, u32[]{:S(2)}, u32[]{:S(2)}) %collective-permute-start.20) | collective-permute-done | bytes 458784 | tf_op jit(solution)/shard_map/ppermute | solution.py:330
  284.8 8.8 %grads_chunk.3 = (bf16[256,7168]{1,0:T(8,128)(2,1)}, bf16[256,7168]{1,0:T(8,128)(2,1)}) custom-call(s32[2]{0:T(128)S(1)} %pad_add_fusion.position, bf16[1,256,1024]{2,1,0:T(8,128)(2,1)S(1)} %get-tuple-element.111.p0, bf16[2,256,1024]{2,1,0:T(8,128)(2,1)S(1)} %collective-permute-done.22.p1.p3, bf16[2,256,1024]{2,1,0:T(8,128)(2,1)S(1)} %collective-permute-done.19.p2, ...), custom_call_target="tpu_custom_call" | custom-call | bytes 10485760 | tf_op jit(solution)/shard_map/grads_chunk/pallas_call | solution.py:191
  293.7 5.0 %collective-permute-done.24.p2 = bf16[2,256,256]{2,1,0:T(8,128)(2,1)S(1)} collective-permute-done((bf16[2,256,256]{2,1,0:T(8,128)(2,1)S(1)}, bf16[2,256,256]{2,1,0:T(8,128)(2,1)S(1)}, u32[]{:S(2)}, u32[]{:S(2)}) %collective-permute-start.24) | collective-permute-done | bytes 262176 | tf_op jit(solution)/shard_map/ppermute | solution.py:330
  300.5 4.8 %grads_chunk.4 = (bf16[256,7168]{1,0:T(8,128)(2,1)}, bf16[256,7168]{1,0:T(8,128)(2,1)}) custom-call(s32[2]{0:T(128)S(1)} %pad_add_fusion.position, bf16[1,256,512]{2,1,0:T(8,128)(2,1)S(1)} %get-tuple-element.114.p0, bf16[2,256,512]{2,1,0:T(8,128)(2,1)S(1)} %collective-permute-done.26.p1.p3, ...), custom_call_target="tpu_custom_call", output_to_operand_aliasing={{0}: (7, {}), {1}: (8, {})} | custom-call | bytes 5242880 | tf_op jit(solution)/shard_map/grads_chunk/pallas_call | solution.py:191
  (145 shorter events, 64.0 us)
Async XLA Ops:
  7.2 69.9 %all-gather.7.cloned.1.call-start = ((), (), s32[]{:S(2)}) async-start(), calls=%async_computation.1 | async-start | bytes 4718592 | tf_op jit(solution)/shard_map/all_gather | solution.py:375
  9.3 14.6 %collective-permute-start = (bf16[256,1024]{1,0:T(8,128)(2,1)S(1)}, bf16[256,1024]{1,0:T(8,128)(2,1)S(1)}, u32[]{:S(2)}, u32[]{:S(2)}) collective-permute-start(bf16[256,1024]{1,0:T(8,128)(2,1)S(1)} %get-tuple-element.126), channel_id=1, source_target_pairs={{0,2},{1,3},{2,0},{3,1},{4,6},{5,7},{6,4},{7,5},{8,10},{9,11},{10,... | collective-permute-start | bytes 1572872 | tf_op jit(solution)/shard_map/ppermute | solution.py:330
  10.4 7.7 %collective-permute-start.2 = (bf16[1024,128]{1,0:T(8,128)(2,1)S(1)}, bf16[1024,128]{1,0:T(8,128)(2,1)S(1)}, u32[]{:S(2)}, u32[]{:S(2)}) collective-permute-start(bf16[1024,128]{1,0:T(8,128)(2,1)S(1)} %get-tuple-element.130), channel_id=1, source_target_pairs={{0,4},{1,5},{10,14},{11,15},{20,16},{21,17},{30,26},{31,27}} | collective-permute-start | bytes 786440 | tf_op jit(solution)/shard_map/ppermute | solution.py:330
  14.8 9.1 %collective-permute-start.3 = (bf16[1024,128]{1,0:T(8,128)(2,1)S(1)}, bf16[1024,128]{1,0:T(8,128)(2,1)S(1)}, u32[]{:S(2)}, u32[]{:S(2)}) collective-permute-start(bf16[1024,128]{1,0:T(8,128)(2,1)S(1)} %get-tuple-element.131), channel_id=1, source_target_pairs={{0,2},{1,3},{10,8},{11,9},{20,22},{21,23},{30,28},{31,29}} | collective-permute-start | bytes 786440 | tf_op jit(solution)/shard_map/ppermute | solution.py:330
  16.1 7.8 %collective-permute-start.1 = (bf16[1024,128]{1,0:T(8,128)(2,1)S(1)}, bf16[1024,128]{1,0:T(8,128)(2,1)S(1)}, u32[]{:S(2)}, u32[]{:S(2)}) collective-permute-start(bf16[1024,128]{1,0:T(8,128)(2,1)S(1)} %get-tuple-element.131), channel_id=1, source_target_pairs={{0,6},{1,7},{10,12},{11,13},{20,18},{21,19},{30,24},{31,25}} | collective-permute-start | bytes 786440 | tf_op jit(solution)/shard_map/ppermute | solution.py:330
  24.8 95.2 %all-gather.5.cloned.1.call-start = ((), (), s32[]{:S(2)}) async-start(), calls=%async_computation | async-start | bytes 4718592 | tf_op jit(solution)/shard_map/all_gather | solution.py:375
  29.2 47.9 %collective-permute-start.5 = (bf16[512,1024]{1,0:T(8,128)(2,1)}, bf16[512,1024]{1,0:T(8,128)(2,1)S(1)}, u32[]{:S(2)}, u32[]{:S(2)}) collective-permute-start(bf16[512,1024]{1,0:T(8,128)(2,1)} %get-tuple-element.68), channel_id=1, source_target_pairs={{0,4},{1,5},{2,6},{3,7},{4,0},{5,1},{6,2},{7,3},{8,12},{9,13},{10,... | collective-permute-start | bytes 3145736 | tf_op jit(solution)/shard_map/ppermute | solution.py:330
  43.0 18.5 %collective-permute-start.4 = (bf16[256,1792]{1,0:T(8,128)(2,1)S(1)}, bf16[256,1792]{1,0:T(8,128)(2,1)S(1)}, u32[]{:S(2)}, u32[]{:S(2)}) collective-permute-start(bf16[256,1792]{1,0:T(8,128)(2,1)S(1)} %get-tuple-element.66), channel_id=1, source_target_pairs={{0,8},{1,9},{2,10},{3,11},{4,12},{5,13},{6,14},{7,15},{8,0},{9,1},... | collective-permute-start | bytes 2752520 | tf_op jit(solution)/shard_map/ppermute | solution.py:330
  50.5 9.9 %collective-permute-start.6 = (bf16[1024,128]{1,0:T(8,128)(2,1)S(1)}, bf16[1024,128]{1,0:T(8,128)(2,1)}, u32[]{:S(2)}, u32[]{:S(2)}) collective-permute-start(bf16[1024,128]{1,0:T(8,128)(2,1)S(1)} %select_select_fusion), channel_id=1, source_target_pairs={{0,1},{1,0},{2,3},{3,2},{4,5},{5,4},{6,7},{7,6},{8,9},{9,8},{10,11... | collective-permute-start | bytes 786440 | tf_op jit(solution)/shard_map/ppermute | solution.py:330
  77.0 54.7 %collective-permute-start.8 = (bf16[512,1024]{1,0:T(8,128)(2,1)}, bf16[512,1024]{1,0:T(8,128)(2,1)S(1)}, u32[]{:S(2)}, u32[]{:S(2)}) collective-permute-start(bf16[512,1024]{1,0:T(8,128)(2,1)} %get-tuple-element.73), channel_id=1, source_target_pairs={{0,4},{1,5},{2,6},{3,7},{4,0},{5,1},{6,2},{7,3},{8,12},{9,13},{10,... | collective-permute-start | bytes 3145736 | tf_op jit(solution)/shard_map/ppermute | solution.py:330
  93.1 53.8 %collective-permute-start.7 = (bf16[4,256,640]{2,1,0:T(8,128)(2,1)}, bf16[4,256,640]{2,1,0:T(8,128)(2,1)}, u32[]{:S(2)}, u32[]{:S(2)}) collective-permute-start(bf16[4,256,640]{2,1,0:T(8,128)(2,1)} %hidden_grad_chunk.8), channel_id=1, source_target_pairs={{0,2},{1,3},{2,0},{3,1},{4,6},{5,7},{6,4},{7,5},{8,10},{9,11},{10,... | collective-permute-start | bytes 3932168 | tf_op jit(solution)/shard_map/ppermute | solution.py:330
  93.1 42.8 %collective-permute-start.9 = (bf16[256,1792]{1,0:T(8,128)(2,1)}, bf16[256,1792]{1,0:T(8,128)(2,1)S(1)}, u32[]{:S(2)}, u32[]{:S(2)}) collective-permute-start(bf16[256,1792]{1,0:T(8,128)(2,1)} %get-tuple-element.75), channel_id=1, source_target_pairs={{0,16},{1,17},{2,18},{3,19},{4,20},{5,21},{6,22},{7,23},{8,24},{9,... | collective-permute-start | bytes 2752520 | tf_op jit(solution)/shard_map/ppermute | solution.py:330
  96.2 50.7 %collective-permute-start.10 = (bf16[256,1792]{1,0:T(8,128)(2,1)}, bf16[256,1792]{1,0:T(8,128)(2,1)}, u32[]{:S(2)}, u32[]{:S(2)}) collective-permute-start(bf16[256,1792]{1,0:T(8,128)(2,1)} %get-tuple-element.77), channel_id=1, source_target_pairs={{0,24},{1,25},{2,26},{3,27},{4,28},{5,29},{6,30},{7,31},{8,16},{9,... | collective-permute-start | bytes 2752520 | tf_op jit(solution)/shard_map/ppermute | solution.py:330
  146.9 47.8 %collective-permute-start.14 = (bf16[512,1024]{1,0:T(8,128)(2,1)}, bf16[512,1024]{1,0:T(8,128)(2,1)S(1)}, u32[]{:S(2)}, u32[]{:S(2)}) collective-permute-start(bf16[512,1024]{1,0:T(8,128)(2,1)} %get-tuple-element.86), channel_id=1, source_target_pairs={{0,4},{1,5},{2,6},{3,7},{4,0},{5,1},{6,2},{7,3},{8,12},{9,13},{10,... | collective-permute-start | bytes 3145736 | tf_op jit(solution)/shard_map/ppermute | solution.py:330
  149.2 45.9 %collective-permute-start.15 = (bf16[4,256,512]{2,1,0:T(8,128)(2,1)}, bf16[4,256,512]{2,1,0:T(8,128)(2,1)}, u32[]{:S(2)}, u32[]{:S(2)}) collective-permute-start(bf16[4,256,512]{2,1,0:T(8,128)(2,1)} %hidden_grad_chunk.10), channel_id=1, source_target_pairs={{0,2},{1,3},{2,0},{3,1},{4,6},{5,7},{6,4},{7,5},{8,10},{9,11},{10,... | collective-permute-start | bytes 3145736 | tf_op jit(solution)/shard_map/ppermute | solution.py:330
  150.4 14.8 %collective-permute-start.13 = (bf16[4,256,128]{2,1,0:T(8,128)(2,1)S(1)}, bf16[4,256,128]{2,1,0:T(8,128)(2,1)S(1)}, u32[]{:S(2)}, u32[]{:S(2)}) collective-permute-start(bf16[4,256,128]{2,1,0:T(8,128)(2,1)S(1)} %fusion.3.refs_0_), channel_id=1, source_target_pairs={{0,24},{1,25},{2,26},{3,27},{4,28},{5,29},{6,30},{7,31},{8,16},{9,... | collective-permute-start | bytes 786440 | tf_op jit(solution)/shard_map/ppermute | solution.py:330
  151.6 14.3 %collective-permute-start.12 = (bf16[4,256,128]{2,1,0:T(8,128)(2,1)S(1)}, bf16[4,256,128]{2,1,0:T(8,128)(2,1)S(1)}, u32[]{:S(2)}, u32[]{:S(2)}) collective-permute-start(bf16[4,256,128]{2,1,0:T(8,128)(2,1)S(1)} %fusion.3.refs_0_), channel_id=1, source_target_pairs={{0,16},{1,17},{2,18},{3,19},{4,20},{5,21},{6,22},{7,23},{8,24},{9,... | collective-permute-start | bytes 786440 | tf_op jit(solution)/shard_map/ppermute | solution.py:330
  152.8 13.8 %collective-permute-start.11 = (bf16[4,256,128]{2,1,0:T(8,128)(2,1)S(1)}, bf16[4,256,128]{2,1,0:T(8,128)(2,1)S(1)}, u32[]{:S(2)}, u32[]{:S(2)}) collective-permute-start(bf16[4,256,128]{2,1,0:T(8,128)(2,1)S(1)} %fusion.3.refs_0_), channel_id=1, source_target_pairs={{0,8},{1,9},{2,10},{3,11},{4,12},{5,13},{6,14},{7,15},{8,0},{9,1},... | collective-permute-start | bytes 786440 | tf_op jit(solution)/shard_map/ppermute | solution.py:330
  162.0 35.8 %slice-start.2 = ((s8[14680064]{0:T(1024)(128)(4,1)}), s8[4194304]{0:T(1024)(128)(4,1)S(1)}, s32[]{:S(2)}) async-start(s8[14680064]{0:T(1024)(128)(4,1)} %bitcast.35), calls=%async_computation.4 | async-start | bytes 8388608
  195.1 24.4 %collective-permute-start.17 = (bf16[256,1024]{1,0:T(8,128)(2,1)}, bf16[256,1024]{1,0:T(8,128)(2,1)S(1)}, u32[]{:S(2)}, u32[]{:S(2)}) collective-permute-start(bf16[256,1024]{1,0:T(8,128)(2,1)} %constant_dynamic-slice_fusion), channel_id=1, source_target_pairs={{0,4},{1,5},{2,6},{3,7},{4,0},{5,1},{6,2},{7,3},{8,12},{9,13},{10,... | collective-permute-start | bytes 1572872 | tf_op jit(solution)/shard_map/ppermute | solution.py:330
  204.0 29.4 %collective-permute-start.16 = (bf16[2,128,1792]{2,1,0:T(8,128)(2,1)}, bf16[2,128,1792]{2,1,0:T(8,128)(2,1)S(1)}, u32[]{:S(2)}, u32[]{:S(2)}) collective-permute-start(bf16[2,128,1792]{2,1,0:T(8,128)(2,1)} %fusion), channel_id=1, source_target_pairs={{0,2},{1,3},{2,0},{3,1},{4,6},{5,7},{6,4},{7,5},{8,10},{9,11},{10,... | collective-permute-start | bytes 2752520 | tf_op jit(solution)/shard_map/ppermute | solution.py:330
  204.0 51.7 %collective-permute-start.18 = (bf16[4,256,512]{2,1,0:T(8,128)(2,1)S(1)}, bf16[4,256,512]{2,1,0:T(8,128)(2,1)S(1)}, u32[]{:S(2)}, u32[]{:S(2)}) collective-permute-start(bf16[4,256,512]{2,1,0:T(8,128)(2,1)S(1)} %hidden_grad_chunk.12), channel_id=1, source_target_pairs={{0,2},{1,3},{2,0},{3,1},{4,6},{5,7},{6,4},{7,5},{8,10},{9,11},{10,... | collective-permute-start | bytes 3145736 | tf_op jit(solution)/shard_map/ppermute | solution.py:330
  205.5 28.3 %collective-permute-start.19 = (bf16[2,256,1024]{2,1,0:T(8,128)(2,1)S(1)}, bf16[2,256,1024]{2,1,0:T(8,128)(2,1)S(1)}, u32[]{:S(2)}, u32[]{:S(2)}) collective-permute-start(bf16[2,256,1024]{2,1,0:T(8,128)(2,1)S(1)} %get-tuple-element.96), channel_id=1, source_target_pairs={{0,16},{1,17},{2,18},{3,19},{4,20},{5,21},{6,22},{7,23},{8,24},{9,... | collective-permute-start | bytes 3145736 | tf_op jit(solution)/shard_map/ppermute | solution.py:330
  255.8 26.1 %collective-permute-start.22 = (bf16[2,256,1024]{2,1,0:T(8,128)(2,1)S(1)}, bf16[2,256,1024]{2,1,0:T(8,128)(2,1)S(1)}, u32[]{:S(2)}, u32[]{:S(2)}) collective-permute-start(bf16[2,256,1024]{2,1,0:T(8,128)(2,1)S(1)} %pad_maximum_fusion), channel_id=1, source_target_pairs={{0,8},{1,9},{2,10},{3,11},{4,12},{5,13},{6,14},{7,15},{8,0},{9,1},... | collective-permute-start | bytes 3145736 | tf_op jit(solution)/shard_map/ppermute | solution.py:330
  257.1 22.7 %collective-permute-start.20 = (bf16[128,1792]{1,0:T(8,128)(2,1)S(1)}, bf16[128,1792]{1,0:T(8,128)(2,1)S(1)}, u32[]{:S(2)}, u32[]{:S(2)}) collective-permute-start(bf16[128,1792]{1,0:T(8,128)(2,1)S(1)} %fusion.4), channel_id=1, source_target_pairs={{0,4},{1,5},{2,6},{3,7},{4,0},{5,1},{6,2},{7,3},{8,12},{9,13},{10,... | collective-permute-start | bytes 1376264 | tf_op jit(solution)/shard_map/ppermute | solution.py:330
  260.6 21.2 %collective-permute-start.21 = (bf16[4,256,256]{2,1,0:T(8,128)(2,1)S(1)}, bf16[4,256,256]{2,1,0:T(8,128)(2,1)S(1)}, u32[]{:S(2)}, u32[]{:S(2)}) collective-permute-start(bf16[4,256,256]{2,1,0:T(8,128)(2,1)S(1)} %hidden_grad_chunk.13), channel_id=1, source_target_pairs={{0,2},{1,3},{2,0},{3,1},{4,6},{5,7},{6,4},{7,5},{8,10},{9,11},{10,... | collective-permute-start | bytes 1572872 | tf_op jit(solution)/shard_map/ppermute | solution.py:330
  260.9 20.9 %collective-permute-start.23 = (bf16[2,256,512]{2,1,0:T(8,128)(2,1)S(1)}, bf16[2,256,512]{2,1,0:T(8,128)(2,1)S(1)}, u32[]{:S(2)}, u32[]{:S(2)}) collective-permute-start(bf16[2,256,512]{2,1,0:T(8,128)(2,1)S(1)} %get-tuple-element.103), channel_id=1, source_target_pairs={{0,16},{1,17},{2,18},{3,19},{4,20},{5,21},{6,22},{7,23},{8,24},{9,... | collective-permute-start | bytes 1572872 | tf_op jit(solution)/shard_map/ppermute | solution.py:330
  281.9 11.8 %collective-permute-start.25 = (bf16[128,1792]{1,0:T(8,128)(2,1)S(1)}, bf16[128,1792]{1,0:T(8,128)(2,1)S(1)}, u32[]{:S(2)}, u32[]{:S(2)}) collective-permute-start(bf16[128,1792]{1,0:T(8,128)(2,1)S(1)} %fusion.2), channel_id=1, source_target_pairs={{0,16},{1,17},{2,18},{3,19},{4,20},{5,21},{6,22},{7,23},{8,24},{9,... | collective-permute-start | bytes 1376264 | tf_op jit(solution)/shard_map/ppermute | solution.py:330
  283.1 15.7 %collective-permute-start.26 = (bf16[2,256,512]{2,1,0:T(8,128)(2,1)S(1)}, bf16[2,256,512]{2,1,0:T(8,128)(2,1)S(1)}, u32[]{:S(2)}, u32[]{:S(2)}) collective-permute-start(bf16[2,256,512]{2,1,0:T(8,128)(2,1)S(1)} %pad_maximum_fusion.2), channel_id=1, source_target_pairs={{0,8},{1,9},{2,10},{3,11},{4,12},{5,13},{6,14},{7,15},{8,0},{9,1},... | collective-permute-start | bytes 1572872 | tf_op jit(solution)/shard_map/ppermute | solution.py:330
  284.2 14.5 %collective-permute-start.24 = (bf16[2,256,256]{2,1,0:T(8,128)(2,1)S(1)}, bf16[2,256,256]{2,1,0:T(8,128)(2,1)S(1)}, u32[]{:S(2)}, u32[]{:S(2)}) collective-permute-start(bf16[2,256,256]{2,1,0:T(8,128)(2,1)S(1)} %get-tuple-element.107), channel_id=1, source_target_pairs={{0,16},{1,17},{2,18},{3,19},{4,20},{5,21},{6,22},{7,23},{8,24},{9,... | collective-permute-start | bytes 786440 | tf_op jit(solution)/shard_map/ppermute | solution.py:330
  298.7 9.4 %collective-permute-start.28 = (bf16[2,128,1792]{2,1,0:T(8,128)(2,1)S(1)}, bf16[2,128,1792]{2,1,0:T(8,128)(2,1)S(1)}, u32[]{:S(2)}, u32[]{:S(2)}) collective-permute-start(bf16[2,128,1792]{2,1,0:T(8,128)(2,1)S(1)} %pad_maximum_fusion.1.refs_0_.refs_2_), channel_id=1, source_target_pairs={{0,8},{1,9},{2,10},{3,11},{4,12},{5,13},{6,14},{7,15},{8,0},{9,1},... | collective-permute-start | bytes 2752520 | tf_op jit(solution)/shard_map/ppermute | solution.py:330
  300.5 4.9 %collective-permute-start.27 = (bf16[2,256,256]{2,1,0:T(8,128)(2,1)S(1)}, bf16[2,256,256]{2,1,0:T(8,128)(2,1)S(1)}, u32[]{:S(2)}, u32[]{:S(2)}) collective-permute-start(bf16[2,256,256]{2,1,0:T(8,128)(2,1)S(1)} %pad_maximum_fusion.3), channel_id=1, source_target_pairs={{0,8},{1,9},{2,10},{3,11},{4,12},{5,13},{6,14},{7,15},{8,0},{9,1},... | collective-permute-start | bytes 786440 | tf_op jit(solution)/shard_map/ppermute | solution.py:330
  (37 other events, 366.7 us)
Sparse Core Ops, SparseCore 0:
  24.9 46.8 all-gather.6
  73.7 46.2 all-gather.4

commit v5 on v4

--- a/solution.py
+++ b/solution.py
@@ -436,12 +436,12 @@
     third = total_of(3, after(kept[3:], *tick), parts[3:])
     third_y = over_replicas(third)
     written = finish(0, first, first_y, first_home, ())
-    tick = (over_y, second_home, third_y, written[0])
+    written = finish(2, second, second_y, second_home, written)
+    tick = (over_y, third_y, written[0])
 
     two = jnp.stack([final, over_y])
     other = send(after(two, *tick), (1, 0, 0))
     third_home = over_cores(third, third_y, *tick)
-    written = finish(2, second, second_y, second_home, after(written, *tick))
     kept = finish(3, third, third_y, third_home, written)
     projected_grad = widen(position, ((two, 0), (other, 0), (two, 1), (other, 1)))
     return (kept[0], kept[1], projected_grad)

time: 322 us -> 320 us (level)
    unnamed x76 -> x80, local copies, waits for them, and re-layouts: 37.4 us -> 37.5 us
  transfers between devices with their start and end apart: 31 -> 31, of which waited for: 14 -> 15; matrix products, arithmetic and copies ran while one was open for 3% -> 3% of each run, Pallas kernels for 18% -> 18%
where the time goes in v5:
time: 320 us; the launch traced here: 316 us
  waiting for transfers between devices  146 us (46%)
  Pallas kernels  60.3 us (19%)
  starting transfers between devices  45.2 us (14%)
  local copies, waits for them, and re-layouts  45.1 us (14%)
  between operations  14.5 us (5%)
  other arithmetic  5.15 us (2%)
    ppermute x29, waiting for transfers between devices, send(): return lax.ppermute(x, AXES, pairs)  122 us
    ppermute x29, starting transfers between devices, send(): return lax.ppermute(x, AXES, pairs)  45.1 us
    unnamed x80, local copies, waits for them, and re-layouts  37.5 us
    pallas_call x8, Pallas kernels, mix(): pl.pallas_call(mix_kernel, out_shape=jax.ShapeDtypeStruct(shape, kind), g...  27.3 us
    all_gather x2, waiting for transfers between devices, everyone(): lax.all_gather(x, ('replica', 'tensor'))  23.2 us
    pallas_call x3, Pallas kernels, grads(): pl.pallas_call(grads_kernel, out_shape=[jax.ShapeDtypeStruct(gate.shape,...  16.4 us
  transfers between devices with their start and end apart: 31, of which 15 were waited for; matrix products, arithmetic and copies ran while one was open for 3% of the time, Pallas kernels for 18%

profile of v5, /device:TPU:9, one launch (start us, length us, event | category | flops | bytes accessed | tf_op | source)
XLA Modules:
  0.0 316.0 jit_solution(2525223643782442856)
XLA Ops:
  10.4 4.4 %collective-permute-start.2 = (bf16[1024,128]{1,0:T(8,128)(2,1)S(1)}, bf16[1024,128]{1,0:T(8,128)(2,1)S(1)}, u32[]{:S(2)}, u32[]{:S(2)}) collective-permute-start(bf16[1024,128]{1,0:T(8,128)(2,1)S(1)} %get-tuple-element.126), channel_id=1, source_target_pairs={{0,4},{1,5},{10,14},{11,15},{20,16},{21,17},{30,26},{31,27}} | collective-permute-start | bytes 786440 | tf_op jit(solution)/shard_map/ppermute | solution.py:330
  18.1 5.7 %collective-permute-done.3 = bf16[1024,128]{1,0:T(8,128)(2,1)S(1)} collective-permute-done((bf16[1024,128]{1,0:T(8,128)(2,1)S(1)}, bf16[1024,128]{1,0:T(8,128)(2,1)S(1)}, u32[]{:S(2)}, u32[]{:S(2)}) %collective-permute-start.3) | collective-permute-done | bytes 262176 | tf_op jit(solution)/shard_map/ppermute | solution.py:330
  25.6 3.6 %constant_dynamic-slice_fusion.1 = (bf16[512,1024]{1,0:T(8,128)(2,1)}, bf16[512,1024]{1,0:T(8,128)(2,1)}, bf16[512,1024]{1,0:T(8,128)(2,1)}) fusion(bf16[7168,1024]{1,0:T(8,128)(2,1)} %own.15, s32[]{:T(128)S(6)} %select_n.131, s32[]{:T(128)S(6)} %select_n.127, s32[]{:T(128)S(6)} %select_n.123), kind=kLoop, calls=%fused_computation.22 | loop fusion | bytes 6291468 | tf_op jit(solution)/shard_map/dynamic_slice | solution.py:356
  29.2 3.2 %collective-permute-start.5 = (bf16[512,1024]{1,0:T(8,128)(2,1)}, bf16[512,1024]{1,0:T(8,128)(2,1)S(1)}, u32[]{:S(2)}, u32[]{:S(2)}) collective-permute-start(bf16[512,1024]{1,0:T(8,128)(2,1)} %get-tuple-element.66), channel_id=1, source_target_pairs={{0,4},{1,5},{2,6},{3,7},{4,0},{5,1},{6,2},{7,3},{8,12},{9,13},{10,... | collective-permute-start | bytes 3145736 | tf_op jit(solution)/shard_map/ppermute | solution.py:330
  36.6 5.5 %hidden_quarters.1 = (bf16[256,1792]{1,0:T(8,128)(2,1)S(1)}, bf16[256,1792]{1,0:T(8,128)(2,1)S(1)}, bf16[256,1792]{1,0:T(8,128)(2,1)}, bf16[256,1792]{1,0:T(8,128)(2,1)}) custom-call(s32[2]{0:T(128)S(1)} %pad_add_fusion.position, bf16[256,7168]{1,0:T(8,128)(2,1)S(1)} %copy-done.6, bf16[256,7168]{1,0:T(8,128)(2,1)S(1)} %copy-done.8), custom_call_target="tpu_custom_call" | custom-call | tf_op jit(solution)/shard_map/hidden_quarters/pallas_call | solution.py:225
  43.0 7.6 %collective-permute-start.4 = (bf16[256,1792]{1,0:T(8,128)(2,1)S(1)}, bf16[256,1792]{1,0:T(8,128)(2,1)S(1)}, u32[]{:S(2)}, u32[]{:S(2)}) collective-permute-start(bf16[256,1792]{1,0:T(8,128)(2,1)S(1)} %get-tuple-element.64), channel_id=1, source_target_pairs={{0,8},{1,9},{2,10},{3,11},{4,12},{5,13},{6,14},{7,15},{8,0},{9,1},... | collective-permute-start | bytes 2752520 | tf_op jit(solution)/shard_map/ppermute | solution.py:330
  51.8 8.7 %collective-permute-done.6 = bf16[1024,128]{1,0:T(8,128)(2,1)} collective-permute-done((bf16[1024,128]{1,0:T(8,128)(2,1)S(1)}, bf16[1024,128]{1,0:T(8,128)(2,1)}, u32[]{:S(2)}, u32[]{:S(2)}) %collective-permute-start.6) | collective-permute-done | bytes 262176 | tf_op jit(solution)/shard_map/ppermute | solution.py:330
  62.5 14.6 %collective-permute-done.5.cross = bf16[512,1024]{1,0:T(8,128)(2,1)S(1)} collective-permute-done((bf16[512,1024]{1,0:T(8,128)(2,1)}, bf16[512,1024]{1,0:T(8,128)(2,1)S(1)}, u32[]{:S(2)}, u32[]{:S(2)}) %collective-permute-start.5) | collective-permute-done | bytes 1048608 | tf_op jit(solution)/shard_map/ppermute | solution.py:330
  77.0 3.0 collective-permute-start.8
  80.0 5.5 %copy-done = bf16[7168,1024]{1,0:T(8,128)(2,1)S(1)} copy-done((bf16[7168,1024]{1,0:T(8,128)(2,1)S(1)}, bf16[7168,1024]{1,0:T(8,128)(2,1)}, u32[]{:S(2)}) %copy-start) | copy-done | bytes 14680088
  87.7 5.4 %hidden_grad_chunk.8 = bf16[4,256,640]{2,1,0:T(8,128)(2,1)} custom-call(s32[2]{0:T(128)S(1)} %pad_add_fusion.position, bf16[4,2,256,1024]{3,2,1,0:T(8,128)(2,1)S(1)} %bitcast.43, bf16[7168,1024]{1,0:T(8,128)(2,1)S(1)} %copy-done, bf16[512,1024]{1,0:T(8,128)(2,1)S(1)} %collective-permute-done.5.cross, bf16[1024,128]{1,0:T(8,128)(2,1)S(1)} %get-tuple-element.125.refs_0_, ...), custom_call_target="tpu_custom_call" | custom-call | flops 2147483648 | tf_op jit(solution)/shard_map/hidden_grad_chunk/pallas_call | solution.py:105
  93.1 3.1 collective-permute-start.9
  96.8 23.2 %all-gather.5.cloned.1.call-done = bf16[2048,1024]{1,0:T(8,128)(2,1)} async-done(((bf16[256,1024]{1,0:T(8,128)(2,1)}), bf16[2048,1024]{1,0:T(8,128)(2,1)}) %all-gather.5.cloned.1.call-update) | async-done | bytes 4194320 | tf_op jit(solution)/shard_map/all_gather | solution.py:375
  120.1 5.2 %copy-done.1 = bf16[7168,1024]{1,0:T(8,128)(2,1)S(1)} copy-done((bf16[7168,1024]{1,0:T(8,128)(2,1)S(1)}, bf16[7168,1024]{1,0:T(8,128)(2,1)}, u32[]{:S(2)}) %copy-start.1) | copy-done | bytes 14680088
  127.4 4.4 %hidden_grad_chunk.9.refs_0_ = f32[4,256,640]{2,1,0:T(8,128)S(1)} custom-call(s32[2]{0:T(128)S(1)} %pad_add_fusion.position, bf16[4,2,256,1024]{3,2,1,0:T(8,128)(2,1)S(1)} %bitcast.37, bf16[7168,1024]{1,0:T(8,128)(2,1)S(1)} %copy-done.1, bf16[512,1024]{1,0:T(8,128)(2,1)S(1)} %collective-permute-done.5.cross, ...), custom_call_target="tpu_custom_call" | custom-call | tf_op jit(solution)/shard_map/hidden_grad_chunk/pallas_call | solution.py:105
  131.9 4.1 %hidden_grad_chunk.10 = bf16[4,256,512]{2,1,0:T(8,128)(2,1)} custom-call(s32[2]{0:T(128)S(1)} %pad_add_fusion.position, bf16[4,2,256,1024]{3,2,1,0:T(8,128)(2,1)S(1)} %bitcast.44, bf16[7168,1024]{1,0:T(8,128)(2,1)S(1)} %copy-done.1, bf16[512,1024]{1,0:T(8,128)(2,1)S(1)} %collective-permute-done.8.cross), custom_call_target="tpu_custom_call" | custom-call | flops 4294967296 | tf_op jit(solution)/shard_map/hidden_grad_chunk/pallas_call | solution.py:105
  136.9 10.1 %collective-permute-done.10.refs_7_ = bf16[256,1792]{1,0:T(8,128)(2,1)} collective-permute-done((bf16[256,1792]{1,0:T(8,128)(2,1)}, bf16[256,1792]{1,0:T(8,128)(2,1)}, u32[]{:S(2)}, u32[]{:S(2)}) %collective-permute-start.10) | collective-permute-done | bytes 917536 | tf_op jit(solution)/shard_map/ppermute | solution.py:330
  154.7 5.2 %copy-done.2 = bf16[7168,1024]{1,0:T(8,128)(2,1)S(1)} copy-done((bf16[7168,1024]{1,0:T(8,128)(2,1)S(1)}, bf16[7168,1024]{1,0:T(8,128)(2,1)}, u32[]{:S(2)}) %copy-start.2) | copy-done | bytes 14680088
  162.1 3.2 hidden_grad_chunk.11.refs_1_
  172.6 5.0 %rank_terms.1 = f32[512,1792]{1,0:T(8,128)S(1)} custom-call(s32[2]{0:T(128)S(1)} %pad_add_fusion.position, bf16[4,256,128]{2,1,0:T(8,128)(2,1)S(1)} %fusion.3.refs_0_, bf16[4,256,128]{2,1,0:T(8,128)(2,1)S(1)} %copy-done.33, bf16[4,256,128]{2,1,0:T(8,128)(2,1)S(1)} %copy-done.31, bf16[4,256,128]{2,1,0:T(8,128)(2,1)S(1)} %copy-done.29, ...), custom_call_target="tpu_custom_call" | custom-call | tf_op jit(solution)/shard_map/rank_terms/pallas_call | solution.py:268
  178.7 16.1 %collective-permute-done.14.cross = bf16[512,1024]{1,0:T(8,128)(2,1)S(1)} collective-permute-done((bf16[512,1024]{1,0:T(8,128)(2,1)}, bf16[512,1024]{1,0:T(8,128)(2,1)S(1)}, u32[]{:S(2)}, u32[]{:S(2)}) %collective-permute-start.14) | collective-permute-done | bytes 1048608 | tf_op jit(solution)/shard_map/ppermute | solution.py:330
  197.9 3.2 %hidden_grad_chunk.12 = bf16[4,256,512]{2,1,0:T(8,128)(2,1)S(1)} custom-call(s32[2]{0:T(128)S(1)} %pad_add_fusion.position, bf16[4,2,256,1024]{3,2,1,0:T(8,128)(2,1)S(1)} %bitcast.45, bf16[7168,1024]{1,0:T(8,128)(2,1)S(1)} %bitcast.36, bf16[512,1024]{1,0:T(8,128)(2,1)S(1)} %collective-permute-done.14.cross), custom_call_target="tpu_custom_call" | custom-call | flops 6442450944 | tf_op jit(solution)/shard_map/hidden_grad_chunk/pallas_call | solution.py:105
  201.1 2.9 hidden_grad_sum.3
  205.7 3.3 %hidden_grad_chunk.14.refs_0_ = f32[4,256,512]{2,1,0:T(8,128)S(1)} custom-call(s32[2]{0:T(128)S(1)} %pad_add_fusion.position, bf16[4,2,256,1024]{3,2,1,0:T(8,128)(2,1)S(1)} %bitcast.39, bf16[7168,1024]{1,0:T(8,128)(2,1)S(1)} %bitcast.36, bf16[512,1024]{1,0:T(8,128)(2,1)S(1)} %collective-permute-done.14.cross), custom_call_target="tpu_custom_call" | custom-call | tf_op jit(solution)/shard_map/hidden_grad_chunk/pallas_call | solution.py:105
  209.1 10.5 %collective-permute-done.17.cross = bf16[256,1024]{1,0:T(8,128)(2,1)S(1)} collective-permute-done((bf16[256,1024]{1,0:T(8,128)(2,1)}, bf16[256,1024]{1,0:T(8,128)(2,1)S(1)}, u32[]{:S(2)}, u32[]{:S(2)}) %collective-permute-start.17) | collective-permute-done | bytes 524320 | tf_op jit(solution)/shard_map/ppermute | solution.py:330
  221.4 12.0 %collective-permute-done.16 = bf16[2,128,1792]{2,1,0:T(8,128)(2,1)S(1)} collective-permute-done((bf16[2,128,1792]{2,1,0:T(8,128)(2,1)}, bf16[2,128,1792]{2,1,0:T(8,128)(2,1)S(1)}, u32[]{:S(2)}, u32[]{:S(2)}) %collective-permute-start.16) | collective-permute-done | bytes 917536 | tf_op jit(solution)/shard_map/ppermute | solution.py:330
  234.0 21.8 %collective-permute-done.18.refs_1_ = bf16[4,256,512]{2,1,0:T(8,128)(2,1)S(1)} collective-permute-done((bf16[4,256,512]{2,1,0:T(8,128)(2,1)S(1)}, bf16[4,256,512]{2,1,0:T(8,128)(2,1)S(1)}, u32[]{:S(2)}, u32[]{:S(2)}) %collective-permute-start.18) | collective-permute-done | bytes 1048608 | tf_op jit(solution)/shard_map/ppermute | solution.py:330
  257.1 3.6 %collective-permute-start.20 = (bf16[128,1792]{1,0:T(8,128)(2,1)S(1)}, bf16[128,1792]{1,0:T(8,128)(2,1)S(1)}, u32[]{:S(2)}, u32[]{:S(2)}) collective-permute-start(bf16[128,1792]{1,0:T(8,128)(2,1)S(1)} %fusion.4), channel_id=1, source_target_pairs={{0,4},{1,5},{2,6},{3,7},{4,0},{5,1},{6,2},{7,3},{8,12},{9,13},{10,... | collective-permute-start | bytes 1376264 | tf_op jit(solution)/shard_map/ppermute | solution.py:330
  263.2 16.7 %collective-permute-done.20 = bf16[128,1792]{1,0:T(8,128)(2,1)S(1)} collective-permute-done((bf16[128,1792]{1,0:T(8,128)(2,1)S(1)}, bf16[128,1792]{1,0:T(8,128)(2,1)S(1)}, u32[]{:S(2)}, u32[]{:S(2)}) %collective-permute-start.20) | collective-permute-done | bytes 458784 | tf_op jit(solution)/shard_map/ppermute | solution.py:330
  284.9 8.8 %grads_chunk.3 = (bf16[256,7168]{1,0:T(8,128)(2,1)}, bf16[256,7168]{1,0:T(8,128)(2,1)}) custom-call(s32[2]{0:T(128)S(1)} %pad_add_fusion.position, bf16[1,256,1024]{2,1,0:T(8,128)(2,1)S(1)} %copy-done.25, bf16[2,256,1024]{2,1,0:T(8,128)(2,1)S(1)} %collective-permute-done.22.p1.p3, bf16[2,256,1024]{2,1,0:T(8,128)(2,1)S(1)} %collective-permute-done.19.p2, ...), custom_call_target="tpu_custom_call" | custom-call | bytes 10485760 | tf_op jit(solution)/shard_map/grads_chunk/pallas_call | solution.py:191
  293.8 4.8 %grads_chunk.4 = (bf16[256,7168]{1,0:T(8,128)(2,1)}, bf16[256,7168]{1,0:T(8,128)(2,1)}) custom-call(s32[2]{0:T(128)S(1)} %pad_add_fusion.position, bf16[1,256,512]{2,1,0:T(8,128)(2,1)S(1)} %get-tuple-element.107.p0, bf16[2,256,512]{2,1,0:T(8,128)(2,1)S(1)} %collective-permute-done.26.p1.p3, ...), custom_call_target="tpu_custom_call", output_to_operand_aliasing={{0}: (7, {}), {1}: (8, {})} | custom-call | bytes 5242880 | tf_op jit(solution)/shard_map/grads_chunk/pallas_call | solution.py:191
  306.3 2.9 projected_grad.1
  (149 shorter events, 64.3 us)
Async XLA Ops:
  7.2 69.9 %all-gather.7.cloned.1.call-start = ((), (), s32[]{:S(2)}) async-start(), calls=%async_computation.1 | async-start | bytes 4718592 | tf_op jit(solution)/shard_map/all_gather | solution.py:375
  9.3 14.6 %collective-permute-start = (bf16[256,1024]{1,0:T(8,128)(2,1)S(1)}, bf16[256,1024]{1,0:T(8,128)(2,1)S(1)}, u32[]{:S(2)}, u32[]{:S(2)}) collective-permute-start(bf16[256,1024]{1,0:T(8,128)(2,1)S(1)} %get-tuple-element.122), channel_id=1, source_target_pairs={{0,2},{1,3},{2,0},{3,1},{4,6},{5,7},{6,4},{7,5},{8,10},{9,11},{10,... | collective-permute-start | bytes 1572872 | tf_op jit(solution)/shard_map/ppermute | solution.py:330
  10.4 7.7 %collective-permute-start.2 = (bf16[1024,128]{1,0:T(8,128)(2,1)S(1)}, bf16[1024,128]{1,0:T(8,128)(2,1)S(1)}, u32[]{:S(2)}, u32[]{:S(2)}) collective-permute-start(bf16[1024,128]{1,0:T(8,128)(2,1)S(1)} %get-tuple-element.126), channel_id=1, source_target_pairs={{0,4},{1,5},{10,14},{11,15},{20,16},{21,17},{30,26},{31,27}} | collective-permute-start | bytes 786440 | tf_op jit(solution)/shard_map/ppermute | solution.py:330
  14.8 9.1 %collective-permute-start.3 = (bf16[1024,128]{1,0:T(8,128)(2,1)S(1)}, bf16[1024,128]{1,0:T(8,128)(2,1)S(1)}, u32[]{:S(2)}, u32[]{:S(2)}) collective-permute-start(bf16[1024,128]{1,0:T(8,128)(2,1)S(1)} %get-tuple-element.127), channel_id=1, source_target_pairs={{0,2},{1,3},{10,8},{11,9},{20,22},{21,23},{30,28},{31,29}} | collective-permute-start | bytes 786440 | tf_op jit(solution)/shard_map/ppermute | solution.py:330
  16.1 7.8 %collective-permute-start.1 = (bf16[1024,128]{1,0:T(8,128)(2,1)S(1)}, bf16[1024,128]{1,0:T(8,128)(2,1)S(1)}, u32[]{:S(2)}, u32[]{:S(2)}) collective-permute-start(bf16[1024,128]{1,0:T(8,128)(2,1)S(1)} %get-tuple-element.127), channel_id=1, source_target_pairs={{0,6},{1,7},{10,12},{11,13},{20,18},{21,19},{30,24},{31,25}} | collective-permute-start | bytes 786440 | tf_op jit(solution)/shard_map/ppermute | solution.py:330
  24.8 95.2 %all-gather.5.cloned.1.call-start = ((), (), s32[]{:S(2)}) async-start(), calls=%async_computation | async-start | bytes 4718592 | tf_op jit(solution)/shard_map/all_gather | solution.py:375
  29.2 47.9 %collective-permute-start.5 = (bf16[512,1024]{1,0:T(8,128)(2,1)}, bf16[512,1024]{1,0:T(8,128)(2,1)S(1)}, u32[]{:S(2)}, u32[]{:S(2)}) collective-permute-start(bf16[512,1024]{1,0:T(8,128)(2,1)} %get-tuple-element.66), channel_id=1, source_target_pairs={{0,4},{1,5},{2,6},{3,7},{4,0},{5,1},{6,2},{7,3},{8,12},{9,13},{10,... | collective-permute-start | bytes 3145736 | tf_op jit(solution)/shard_map/ppermute | solution.py:330
  43.0 18.5 %collective-permute-start.4 = (bf16[256,1792]{1,0:T(8,128)(2,1)S(1)}, bf16[256,1792]{1,0:T(8,128)(2,1)S(1)}, u32[]{:S(2)}, u32[]{:S(2)}) collective-permute-start(bf16[256,1792]{1,0:T(8,128)(2,1)S(1)} %get-tuple-element.64), channel_id=1, source_target_pairs={{0,8},{1,9},{2,10},{3,11},{4,12},{5,13},{6,14},{7,15},{8,0},{9,1},... | collective-permute-start | bytes 2752520 | tf_op jit(solution)/shard_map/ppermute | solution.py:330
  50.6 9.9 %collective-permute-start.6 = (bf16[1024,128]{1,0:T(8,128)(2,1)S(1)}, bf16[1024,128]{1,0:T(8,128)(2,1)}, u32[]{:S(2)}, u32[]{:S(2)}) collective-permute-start(bf16[1024,128]{1,0:T(8,128)(2,1)S(1)} %select_select_fusion), channel_id=1, source_target_pairs={{0,1},{1,0},{2,3},{3,2},{4,5},{5,4},{6,7},{7,6},{8,9},{9,8},{10,11... | collective-permute-start | bytes 786440 | tf_op jit(solution)/shard_map/ppermute | solution.py:330
  77.0 54.8 %collective-permute-start.8 = (bf16[512,1024]{1,0:T(8,128)(2,1)}, bf16[512,1024]{1,0:T(8,128)(2,1)S(1)}, u32[]{:S(2)}, u32[]{:S(2)}) collective-permute-start(bf16[512,1024]{1,0:T(8,128)(2,1)} %get-tuple-element.71), channel_id=1, source_target_pairs={{0,4},{1,5},{2,6},{3,7},{4,0},{5,1},{6,2},{7,3},{8,12},{9,13},{10,... | collective-permute-start | bytes 3145736 | tf_op jit(solution)/shard_map/ppermute | solution.py:330
  93.1 53.9 %collective-permute-start.7 = (bf16[4,256,640]{2,1,0:T(8,128)(2,1)}, bf16[4,256,640]{2,1,0:T(8,128)(2,1)}, u32[]{:S(2)}, u32[]{:S(2)}) collective-permute-start(bf16[4,256,640]{2,1,0:T(8,128)(2,1)} %hidden_grad_chunk.8), channel_id=1, source_target_pairs={{0,2},{1,3},{2,0},{3,1},{4,6},{5,7},{6,4},{7,5},{8,10},{9,11},{10,... | collective-permute-start | bytes 3932168 | tf_op jit(solution)/shard_map/ppermute | solution.py:330
  93.1 42.8 %collective-permute-start.9 = (bf16[256,1792]{1,0:T(8,128)(2,1)}, bf16[256,1792]{1,0:T(8,128)(2,1)S(1)}, u32[]{:S(2)}, u32[]{:S(2)}) collective-permute-start(bf16[256,1792]{1,0:T(8,128)(2,1)} %get-tuple-element.73), channel_id=1, source_target_pairs={{0,16},{1,17},{2,18},{3,19},{4,20},{5,21},{6,22},{7,23},{8,24},{9,... | collective-permute-start | bytes 2752520 | tf_op jit(solution)/shard_map/ppermute | solution.py:330
  96.2 50.8 %collective-permute-start.10 = (bf16[256,1792]{1,0:T(8,128)(2,1)}, bf16[256,1792]{1,0:T(8,128)(2,1)}, u32[]{:S(2)}, u32[]{:S(2)}) collective-permute-start(bf16[256,1792]{1,0:T(8,128)(2,1)} %get-tuple-element.75), channel_id=1, source_target_pairs={{0,24},{1,25},{2,26},{3,27},{4,28},{5,29},{6,30},{7,31},{8,16},{9,... | collective-permute-start | bytes 2752520 | tf_op jit(solution)/shard_map/ppermute | solution.py:330
  147.0 47.8 %collective-permute-start.14 = (bf16[512,1024]{1,0:T(8,128)(2,1)}, bf16[512,1024]{1,0:T(8,128)(2,1)S(1)}, u32[]{:S(2)}, u32[]{:S(2)}) collective-permute-start(bf16[512,1024]{1,0:T(8,128)(2,1)} %get-tuple-element.84), channel_id=1, source_target_pairs={{0,4},{1,5},{2,6},{3,7},{4,0},{5,1},{6,2},{7,3},{8,12},{9,13},{10,... | collective-permute-start | bytes 3145736 | tf_op jit(solution)/shard_map/ppermute | solution.py:330
  149.3 45.9 %collective-permute-start.15 = (bf16[4,256,512]{2,1,0:T(8,128)(2,1)}, bf16[4,256,512]{2,1,0:T(8,128)(2,1)}, u32[]{:S(2)}, u32[]{:S(2)}) collective-permute-start(bf16[4,256,512]{2,1,0:T(8,128)(2,1)} %hidden_grad_chunk.10), channel_id=1, source_target_pairs={{0,2},{1,3},{2,0},{3,1},{4,6},{5,7},{6,4},{7,5},{8,10},{9,11},{10,... | collective-permute-start | bytes 3145736 | tf_op jit(solution)/shard_map/ppermute | solution.py:330
  150.5 14.8 %collective-permute-start.13 = (bf16[4,256,128]{2,1,0:T(8,128)(2,1)S(1)}, bf16[4,256,128]{2,1,0:T(8,128)(2,1)S(1)}, u32[]{:S(2)}, u32[]{:S(2)}) collective-permute-start(bf16[4,256,128]{2,1,0:T(8,128)(2,1)S(1)} %fusion.3.refs_0_), channel_id=1, source_target_pairs={{0,24},{1,25},{2,26},{3,27},{4,28},{5,29},{6,30},{7,31},{8,16},{9,... | collective-permute-start | bytes 786440 | tf_op jit(solution)/shard_map/ppermute | solution.py:330
  151.7 14.3 %collective-permute-start.12 = (bf16[4,256,128]{2,1,0:T(8,128)(2,1)S(1)}, bf16[4,256,128]{2,1,0:T(8,128)(2,1)S(1)}, u32[]{:S(2)}, u32[]{:S(2)}) collective-permute-start(bf16[4,256,128]{2,1,0:T(8,128)(2,1)S(1)} %fusion.3.refs_0_), channel_id=1, source_target_pairs={{0,16},{1,17},{2,18},{3,19},{4,20},{5,21},{6,22},{7,23},{8,24},{9,... | collective-permute-start | bytes 786440 | tf_op jit(solution)/shard_map/ppermute | solution.py:330
  152.8 13.9 %collective-permute-start.11 = (bf16[4,256,128]{2,1,0:T(8,128)(2,1)S(1)}, bf16[4,256,128]{2,1,0:T(8,128)(2,1)S(1)}, u32[]{:S(2)}, u32[]{:S(2)}) collective-permute-start(bf16[4,256,128]{2,1,0:T(8,128)(2,1)S(1)} %fusion.3.refs_0_), channel_id=1, source_target_pairs={{0,8},{1,9},{2,10},{3,11},{4,12},{5,13},{6,14},{7,15},{8,0},{9,1},... | collective-permute-start | bytes 786440 | tf_op jit(solution)/shard_map/ppermute | solution.py:330
  162.1 35.8 %slice-start.2 = ((s8[14680064]{0:T(1024)(128)(4,1)}), s8[4194304]{0:T(1024)(128)(4,1)S(1)}, s32[]{:S(2)}) async-start(s8[14680064]{0:T(1024)(128)(4,1)} %bitcast.35), calls=%async_computation.4 | async-start | bytes 8388608
  195.2 24.4 %collective-permute-start.17 = (bf16[256,1024]{1,0:T(8,128)(2,1)}, bf16[256,1024]{1,0:T(8,128)(2,1)S(1)}, u32[]{:S(2)}, u32[]{:S(2)}) collective-permute-start(bf16[256,1024]{1,0:T(8,128)(2,1)} %constant_dynamic-slice_fusion), channel_id=1, source_target_pairs={{0,4},{1,5},{2,6},{3,7},{4,0},{5,1},{6,2},{7,3},{8,12},{9,13},{10,... | collective-permute-start | bytes 1572872 | tf_op jit(solution)/shard_map/ppermute | solution.py:330
  204.0 29.4 %collective-permute-start.16 = (bf16[2,128,1792]{2,1,0:T(8,128)(2,1)}, bf16[2,128,1792]{2,1,0:T(8,128)(2,1)S(1)}, u32[]{:S(2)}, u32[]{:S(2)}) collective-permute-start(bf16[2,128,1792]{2,1,0:T(8,128)(2,1)} %fusion), channel_id=1, source_target_pairs={{0,2},{1,3},{2,0},{3,1},{4,6},{5,7},{6,4},{7,5},{8,10},{9,11},{10,... | collective-permute-start | bytes 2752520 | tf_op jit(solution)/shard_map/ppermute | solution.py:330
  204.1 51.7 %collective-permute-start.18 = (bf16[4,256,512]{2,1,0:T(8,128)(2,1)S(1)}, bf16[4,256,512]{2,1,0:T(8,128)(2,1)S(1)}, u32[]{:S(2)}, u32[]{:S(2)}) collective-permute-start(bf16[4,256,512]{2,1,0:T(8,128)(2,1)S(1)} %hidden_grad_chunk.12), channel_id=1, source_target_pairs={{0,2},{1,3},{2,0},{3,1},{4,6},{5,7},{6,4},{7,5},{8,10},{9,11},{10,... | collective-permute-start | bytes 3145736 | tf_op jit(solution)/shard_map/ppermute | solution.py:330
  205.5 28.3 %collective-permute-start.19 = (bf16[2,256,1024]{2,1,0:T(8,128)(2,1)S(1)}, bf16[2,256,1024]{2,1,0:T(8,128)(2,1)S(1)}, u32[]{:S(2)}, u32[]{:S(2)}) collective-permute-start(bf16[2,256,1024]{2,1,0:T(8,128)(2,1)S(1)} %get-tuple-element.94), channel_id=1, source_target_pairs={{0,16},{1,17},{2,18},{3,19},{4,20},{5,21},{6,22},{7,23},{8,24},{9,... | collective-permute-start | bytes 3145736 | tf_op jit(solution)/shard_map/ppermute | solution.py:330
  255.8 26.1 %collective-permute-start.22 = (bf16[2,256,1024]{2,1,0:T(8,128)(2,1)S(1)}, bf16[2,256,1024]{2,1,0:T(8,128)(2,1)S(1)}, u32[]{:S(2)}, u32[]{:S(2)}) collective-permute-start(bf16[2,256,1024]{2,1,0:T(8,128)(2,1)S(1)} %pad_maximum_fusion), channel_id=1, source_target_pairs={{0,8},{1,9},{2,10},{3,11},{4,12},{5,13},{6,14},{7,15},{8,0},{9,1},... | collective-permute-start | bytes 3145736 | tf_op jit(solution)/shard_map/ppermute | solution.py:330
  257.1 22.7 %collective-permute-start.20 = (bf16[128,1792]{1,0:T(8,128)(2,1)S(1)}, bf16[128,1792]{1,0:T(8,128)(2,1)S(1)}, u32[]{:S(2)}, u32[]{:S(2)}) collective-permute-start(bf16[128,1792]{1,0:T(8,128)(2,1)S(1)} %fusion.4), channel_id=1, source_target_pairs={{0,4},{1,5},{2,6},{3,7},{4,0},{5,1},{6,2},{7,3},{8,12},{9,13},{10,... | collective-permute-start | bytes 1376264 | tf_op jit(solution)/shard_map/ppermute | solution.py:330
  260.7 21.2 %collective-permute-start.21 = (bf16[4,256,256]{2,1,0:T(8,128)(2,1)S(1)}, bf16[4,256,256]{2,1,0:T(8,128)(2,1)S(1)}, u32[]{:S(2)}, u32[]{:S(2)}) collective-permute-start(bf16[4,256,256]{2,1,0:T(8,128)(2,1)S(1)} %hidden_grad_chunk.13), channel_id=1, source_target_pairs={{0,2},{1,3},{2,0},{3,1},{4,6},{5,7},{6,4},{7,5},{8,10},{9,11},{10,... | collective-permute-start | bytes 1572872 | tf_op jit(solution)/shard_map/ppermute | solution.py:330
  261.0 20.9 %collective-permute-start.23 = (bf16[2,256,512]{2,1,0:T(8,128)(2,1)S(1)}, bf16[2,256,512]{2,1,0:T(8,128)(2,1)S(1)}, u32[]{:S(2)}, u32[]{:S(2)}) collective-permute-start(bf16[2,256,512]{2,1,0:T(8,128)(2,1)S(1)} %get-tuple-element.101), channel_id=1, source_target_pairs={{0,16},{1,17},{2,18},{3,19},{4,20},{5,21},{6,22},{7,23},{8,24},{9,... | collective-permute-start | bytes 1572872 | tf_op jit(solution)/shard_map/ppermute | solution.py:330
  281.9 11.8 %collective-permute-start.25 = (bf16[128,1792]{1,0:T(8,128)(2,1)S(1)}, bf16[128,1792]{1,0:T(8,128)(2,1)S(1)}, u32[]{:S(2)}, u32[]{:S(2)}) collective-permute-start(bf16[128,1792]{1,0:T(8,128)(2,1)S(1)} %fusion.2), channel_id=1, source_target_pairs={{0,16},{1,17},{2,18},{3,19},{4,20},{5,21},{6,22},{7,23},{8,24},{9,... | collective-permute-start | bytes 1376264 | tf_op jit(solution)/shard_map/ppermute | solution.py:330
  283.1 10.6 %collective-permute-start.26 = (bf16[2,256,512]{2,1,0:T(8,128)(2,1)S(1)}, bf16[2,256,512]{2,1,0:T(8,128)(2,1)S(1)}, u32[]{:S(2)}, u32[]{:S(2)}) collective-permute-start(bf16[2,256,512]{2,1,0:T(8,128)(2,1)S(1)} %pad_maximum_fusion.2), channel_id=1, source_target_pairs={{0,8},{1,9},{2,10},{3,11},{4,12},{5,13},{6,14},{7,15},{8,0},{9,1},... | collective-permute-start | bytes 1572872 | tf_op jit(solution)/shard_map/ppermute | solution.py:330
  284.3 14.5 %collective-permute-start.24 = (bf16[2,256,256]{2,1,0:T(8,128)(2,1)S(1)}, bf16[2,256,256]{2,1,0:T(8,128)(2,1)S(1)}, u32[]{:S(2)}, u32[]{:S(2)}) collective-permute-start(bf16[2,256,256]{2,1,0:T(8,128)(2,1)S(1)} %get-tuple-element.105), channel_id=1, source_target_pairs={{0,16},{1,17},{2,18},{3,19},{4,20},{5,21},{6,22},{7,23},{8,24},{9,... | collective-permute-start | bytes 786440 | tf_op jit(solution)/shard_map/ppermute | solution.py:330
  298.8 7.5 %collective-permute-start.28 = (bf16[2,128,1792]{2,1,0:T(8,128)(2,1)S(1)}, bf16[2,128,1792]{2,1,0:T(8,128)(2,1)S(1)}, u32[]{:S(2)}, u32[]{:S(2)}) collective-permute-start(bf16[2,128,1792]{2,1,0:T(8,128)(2,1)S(1)} %pad_maximum_fusion.1.refs_0_.refs_2_), channel_id=1, source_target_pairs={{0,8},{1,9},{2,10},{3,11},{4,12},{5,13},{6,14},{7,15},{8,0},{9,1},... | collective-permute-start | bytes 2752520 | tf_op jit(solution)/shard_map/ppermute | solution.py:330
  301.1 2.4 collective-permute-start.27
  (39 other events, 393.5 us)
Sparse Core Ops, SparseCore 0:
  25.0 46.8 all-gather.6
  73.7 46.3 all-gather.4
